TPU v7x, 32 devices: a whole 2x2x4 slice. The times are simulated.
32 devices in a mesh: row: 2 (over y), col: 16 (over z, x, core).
Axes of the slice: x: 2, y: 2, z: 4, core: 2. Of those that a mesh axis runs over, the one named last changes fastest.
Arguments:
- transfer: bfloat16 [2, 512, 16384], P(None, 'row', 'col'), may hold values from -0.046875 to 0.046875
- phase: float32 [16384, 128], P('col', 'row'), may hold values from -3.140625 to 3.140625
- trap_index: int32 [128, 64], replicated, may hold values from 0 to 511
- levels: int32 [128, 64], replicated, may hold values from 1 to 4
- weights_old: float32 [128, 64], replicated, may hold values from 0.5 to 1.5
Outputs:
- far_field: bfloat16 [512, 2, 128], P(('row', 'col'))
- weights_new: float32 [128, 64], replicated
- slm_field: float32 [16384, 2, 128], P('col', None, 'row')
All inputs are finite; a program needn't handle non-finite values.
Results may differ from a plain program's by a relative error of at most 0.013.
Values may be sent and summed in bfloat16 or wider, within the bound.
No kernel may reach another device: no remote copies, remote signals or barrier semaphores. Data moves between devices by JAX's collectives and lax.ppermute only.
A program may use at most 64 MiB of HBM per device.

v0:
```python
import jax
import jax.numpy as jnp
from jax import lax
from jax.sharding import PartitionSpec as P

MODES = 16384
TRAPS = 64


def update_weights(shared, target, weights_old):
    amp = jnp.sqrt(shared[..., 0] ** 2 + shared[..., 1] ** 2 + 0.25)
    ratio = amp / target
    weights_new = weights_old * jnp.mean(ratio, axis=1, keepdims=True) / ratio
    coef = weights_new * target / amp
    return (weights_new, coef)


def body(transfer, phase, trap_index, levels, weights_old):
    n_col = lax.axis_size("col")
    tile_rows = transfer.shape[1]
    modes_local = transfer.shape[2]
    field = jnp.stack([jnp.cos(phase), jnp.sin(phase)], axis=0).astype(jnp.bfloat16)
    whole = lax.all_gather(field, "row", axis=2, tiled=True)
    count = whole.shape[2]
    target = levels.astype(jnp.float32)
    row_start = lax.axis_index("row") * tile_rows
    per_col = count // n_col
    number = per_col * lax.axis_size("col")
    real_cols = whole[0]
    imag_cols = whole[1]
    sliced = jnp.concatenate([real_cols, imag_cols], axis=1)
    dims = (((0,), (1,)), ((), ()))
    first = lax.dot_general(sliced, transfer[0], dims, preferred_element_type=jnp.float32)
    second = lax.dot_general(sliced, transfer[1], dims, preferred_element_type=jnp.float32)
    mine_p = lax.psum_scatter(
        jnp.stack([first[:number] - second[number:], first[number:] + second[:number]], axis=1),
        "col",
        scatter_dimension=0,
        tiled=True,
    )
    far_cols = lax.all_to_all(
        mine_p.astype(jnp.bfloat16), "col", split_axis=2, concat_axis=0, tiled=True
    )
    far_field = jnp.transpose(far_cols, (2, 1, 0))
    pattern_start = lax.axis_index("col") * per_col
    my_index = lax.dynamic_slice_in_dim(trap_index, pattern_start, per_col, 0)
    my_target = lax.dynamic_slice_in_dim(target, pattern_start, per_col, 0)
    my_old = lax.dynamic_slice_in_dim(weights_old, pattern_start, per_col, 0)
    local = my_index - row_start
    within = (local >= 0) & (local < tile_rows)
    placed = jnp.clip(local, 0, tile_rows - 1)
    local_ids = jnp.arange(per_col, dtype=jnp.int32)[:, None]
    values = mine_p[local_ids, :, placed]
    shared = lax.psum(jnp.where(within[..., None], values, 0.0), "row")
    my_weights, coef = update_weights(shared, my_target, my_old)
    weights_new = lax.all_gather(my_weights, "col", axis=0, tiled=True)
    adds = jnp.where(within[..., None], coef[..., None] * shared, 0.0)
    projected_p = (
        jnp.zeros((per_col, 2, tile_rows), jnp.float32)
        .at[local_ids, :, placed]
        .add(adds)
        .astype(jnp.bfloat16)
    )
    gathered = lax.all_gather(projected_p, "col", axis=0, tiled=True)
    flat = gathered.reshape(count * 2, tile_rows)
    dims = (((0,), (1,)), ((), ()))
    first_b = lax.dot_general(transfer[0], flat, dims, preferred_element_type=jnp.float32).reshape(
        modes_local, count, 2
    )
    second_b = lax.dot_general(transfer[1], flat, dims, preferred_element_type=jnp.float32).reshape(
        modes_local, count, 2
    )
    back = jnp.stack(
        [first_b[:, :, 0] + second_b[:, :, 1], first_b[:, :, 1] - second_b[:, :, 0]], axis=1
    )
    back = lax.psum_scatter(
        back.astype(jnp.bfloat16), "row", scatter_dimension=2, tiled=True
    ).astype(jnp.float32)
    scaled = jnp.sqrt(jnp.float32(MODES) / jnp.float32(TRAPS)) * back
    slm_field = scaled / jnp.sqrt(scaled[:, 0:1] ** 2 + scaled[:, 1:2] ** 2 + 1.0)
    return (far_field, weights_new, slm_field)


def solution(mesh):
    placed = (P(None, "row", "col"), P("col", "row"), P(), P(), P())
    return jax.shard_map(
        body,
        mesh=mesh,
        in_specs=placed,
        out_specs=(P(("row", "col"), None, None), P(), P("col", None, "row")),
        check_vma=False,
    )
```

profile of v0, /device:TPU:0, one launch (start us, length us, event | category | flops | bytes accessed | tf_op | source)
XLA Modules:
  0.0 181.5 jit_solution(7628695527762102631)
XLA Ops:
  7.2 0.0 reduce-scatter.3.cloned.1.call-start
  7.2 1.9 %fusion.18 = (bf16[1,1024,64]{1,2,0:T(8,128)(2,1)S(1)}, bf16[1,1024,64]{1,2,0:T(8,128)(2,1)S(1)}) fusion(f32[1024,64]{0,1:T(8,128)} %param.6), kind=kLoop, calls=%fused_computation.36 | loop fusion | flops 131072 | bytes 524288 | tf_op jit(solution)/shard_map/stack | solution.py:22
  9.1 10.1 %all_gather.9 = bf16[2,1024,128]{1,2,0:T(8,128)(2,1)S(1)} all-gather(bf16[2,1024,64]{1,2,0:T(8,128)(2,1)S(1)} %pad_maximum_fusion.4), channel_id=1, replica_groups=mesh['row'=2,'col'=16] {'row'}, dimensions={2}, use_global_device_ids=true | all-gather | bytes 786432 | tf_op jit(solution)/shard_map/all_gather | solution.py:23
  19.3 0.3 fusion.3
  19.6 0.3 fusion.6
  20.0 0.7 pad_maximum_fusion.5
  20.7 0.0 reduce-scatter.5.cloned.1.call-start
  20.8 0.1 constant_dynamic-slice_fusion
  20.9 0.1 copy.83
  21.0 0.1 reshape.76
  21.0 0.1 reshape.70
  21.1 0.1 copy.64
  21.2 56.5 %reduce-scatter.3.cloned.1.call-done = f32[8,2,256]{2,0,1:T(8,128)} async-done(((f32[128,2,256]{2,0,1:T(8,128)}), f32[8,2,256]{2,0,1:T(8,128)}) %reduce-scatter.3.cloned.1.call-update) | async-done | bytes 16400 | tf_op jit(solution)/shard_map/reduce_scatter | solution.py:35
  77.7 1.1 copy.65
  78.8 3.7 %gather_fusion = f32[512,2]{1,0:T(8,128)S(1)} fusion(f32[8,2,256]{1,2,0:T(8,128)S(1)} %copy.65, s32[512]{0:T(512)S(1)} %reshape.70), kind=kCustom, calls=%fused_computation | custom fusion | bytes 12288 | tf_op jit(solution)/shard_map/gather | solution.py:53
  82.5 0.5 copy.67
  83.0 8.8 %psum.7 = f32[8,64,2]{0,1,2:T(8,128)S(1)} all-reduce(f32[8,64,2]{0,1,2:T(8,128)S(1)} %broadcast_select_fusion), channel_id=1, replica_groups=mesh['row'=2,'col'=16] {'row'}, use_global_device_ids=true, to_apply=%region_1.2 | all-reduce | flops 1024 | bytes 8192 | tf_op jit(solution)/shard_map/psum | solution.py:54
  91.8 0.1 divide_reduce_fusion
  91.9 0.6 copy-done.5
  92.6 0.1 multiply_divide_fusion
  92.7 0.5 copy.81
  93.1 0.1 broadcast_in_dim.40
  93.2 24.8 %scatter_fusion = f32[8,2,256]{1,2,0:T(8,128)S(1)} fusion(f32[8,2,256]{1,2,0:T(8,128)S(1)} %broadcast_in_dim.40, s32[512]{0:T(512)S(1)} %reshape.76, f32[512,2]{1,0:T(8,128)S(1)} %bitcast.69), kind=kCustom, calls=%fused_computation.1 | custom fusion | flops 1024 | bytes 16384 | tf_op jit(solution)/shard_map/scatter-add | solution.py:61
  118.0 0.3 copy.71
  118.4 19.9 %all_gather.11 = bf16[128,2,256]{2,1,0:T(2,128)(2,1)S(1)} all-gather(bf16[8,2,256]{2,1,0:T(2,128)(2,1)S(1)} %copy.72), channel_id=1, replica_groups=mesh['row'=2,'col'=16] {'col'}, dimensions={0}, use_global_device_ids=true | all-gather | bytes 139264 | tf_op jit(solution)/shard_map/all_gather | solution.py:64
  138.2 0.1 reshape.67
  138.3 0.3 convolution_bitcast_fusion
  138.6 0.3 convolution_bitcast_fusion.1
  138.9 0.6 reshape.69
  139.5 0.8 fusion.34
  140.3 0.6 reshape.68
  141.0 0.8 fusion.33
  141.8 0.5 fusion.12
  142.3 0.8 pad_maximum_fusion.1
  143.1 0.7 copy-done.4
  143.8 0.2 copy.61
  144.0 0.8 reshape.82
  144.8 3.5 %all-to-all-start = ((bf16[16,2,128]{2,1,0:T(2,128)(2,1)}), bf16[16,2,128]{2,1,0:T(2,128)(2,1)S(1)}, u32[]{:S(2)}, u32[]{:S(2)}) async-start(bf16[16,2,128]{2,1,0:T(2,128)(2,1)} %reshape.82), calls=%async_computation.1 | async-start | bytes 16384 | tf_op jit(solution)/shard_map/all_to_all | solution.py:41
  148.2 0.1 copy.68
  148.3 21.8 %all_gather.10 = f32[128,64]{1,0:T(8,128)S(1)} all-gather(f32[8,64]{1,0:T(8,128)S(1)} %copy.68), channel_id=1, replica_groups=mesh['row'=2,'col'=16] {'col'}, dimensions={0}, use_global_device_ids=true | all-gather | bytes 34816 | tf_op jit(solution)/shard_map/all_gather | solution.py:56
  170.1 0.7 copy.78
  170.8 0.2 reshape.83
  171.0 0.1 copy.62
  171.2 0.7 copy.77
  171.8 1.0 convert_multiply_fusion
  172.9 0.1 fusion.17
  173.0 0.8 copy-done.2
  173.8 0.9 broadcast_divide_fusion
  (23 shorter events, 0.2 us)
Async XLA Ops:
  7.2 13.6 %copy-start = (s32[128,64]{0,1:T(8,128)S(1)}, s32[128,64]{0,1:T(8,128)}, u32[]{:S(2)}) copy-start(s32[128,64]{0,1:T(8,128)} %param.7) | copy-start | bytes 98308
  7.2 70.5 %reduce-scatter.3.cloned.1.call-start = ((), (), s32[]{:S(2)}) async-start(), calls=%async_computation.3 | async-start | bytes 278528 | tf_op jit(solution)/shard_map/reduce_scatter | solution.py:35
  9.1 10.1 %copy-start.1 = (bf16[2,256,1024]{2,1,0:T(8,128)(2,1)S(1)}, bf16[2,256,1024]{2,1,0:T(8,128)(2,1)}, u32[]{:S(2)}) copy-start(bf16[2,256,1024]{2,1,0:T(8,128)(2,1)} %param.5) | copy-start | bytes 3145732
  20.7 151.1 %reduce-scatter.5.cloned.1.call-start = ((), (), s32[]{:S(2)}) async-start(), calls=%async_computation.4 | async-start | bytes 786432 | tf_op jit(solution)/shard_map/reduce_scatter | solution.py:76
  83.0 8.8 %copy-start.3 = (s32[128,64]{0,1:T(8,128)S(1)}, s32[128,64]{0,1:T(8,128)}, u32[]{:S(2)}) copy-start(s32[128,64]{0,1:T(8,128)} %param.8) | copy-start | bytes 98308
  91.8 0.8 copy-start.5
  143.1 0.7 copy-start.4
  144.8 26.1 %all-to-all-start = ((bf16[16,2,128]{2,1,0:T(2,128)(2,1)}), bf16[16,2,128]{2,1,0:T(2,128)(2,1)S(1)}, u32[]{:S(2)}, u32[]{:S(2)}) async-start(bf16[16,2,128]{2,1,0:T(2,128)(2,1)} %reshape.82), calls=%async_computation.1 | async-start | bytes 16384 | tf_op jit(solution)/shard_map/all_to_all | solution.py:41
  172.8 1.0 copy-start.2
Sparse Core Ops, SparseCore 0:
  20.9 56.8 reduce-scatter.2
  143.3 10.9 reduce-scatter.4
where the time goes:
time: 182 us
  blocking collectives  60.6 us (33%)
  waiting for transfers between devices  56.5 us (31%)
  other arithmetic  31 us (17%)
  local copies, waits for them, and re-layouts  14.3 us (8%)
  between operations  14.3 us (8%)
  starting transfers between devices  3.55 us (2%)
    reduce_scatter x1, waiting for transfers between devices, body(): lax.psum_scatter(jnp.stack([first[:number] - second[number:], first[numbe...  56.5 us
    scatter-add x1, other arithmetic, body(): projected_p = jnp.zeros((per_col, 2, tile_rows), jnp.float32).at[local_id...  24.8 us
    all_gather x1, blocking collectives, body(): weights_new = lax.all_gather(my_weights, 'col', axis=0, tiled=True)  21.8 us
    all_gather x1, blocking collectives, body(): gathered = lax.all_gather(projected_p, 'col', axis=0, tiled=True)  19.9 us
    all_gather x1, blocking collectives, body(): whole = lax.all_gather(field, 'row', axis=2, tiled=True)  10.1 us
    psum x1, blocking collectives, body(): shared = lax.psum(jnp.where(within[..., None], values, 0.0), 'row')  8.78 us
    unnamed x17, local copies, waits for them, and re-layouts  4.58 us
    gather x2, local copies, waits for them, and re-layouts, body(): values = mine_p[local_ids, :, placed]  4.17 us
  transfers between devices with their start and end apart: 3, of which 1 were waited for; matrix products, arithmetic and copies ran while one was open for 2% of the time, Pallas kernels for 0%

commit v1 on v0

v1 whole, which is shorter than its diff:
```python
import functools

import jax
import jax.numpy as jnp
from jax import lax
from jax.experimental import pallas as pl
from jax.experimental.pallas import tpu as pltpu
from jax.sharding import PartitionSpec as P

MODES = 16384
TRAPS = 64
BF = jnp.bfloat16
F32 = jnp.float32
AXES = ("row", "col")
LANES = 128
SIN = (0.9999996052826214, -0.16666553769418907, 0.008332409691364227, -0.00019808794770261517, 2.6998844729663915e-06,
       -2.0368733379709898e-08)
COS = (0.999999989217114, -0.49999989221470714, 0.041666490704389186, -0.0013887810304225767, 2.4770020037729276e-05,
       -2.708030902998698e-07, 1.7249574387300172e-09)
STEEP = 25.0
CROSS = ()
NT = (((1,), (1,)), ((), ()))
NN = (((1,), (0,)), ((), ()))
SMEM = pl.BlockSpec(memory_space=pltpu.SMEM)
VMEM = pl.BlockSpec(memory_space=pltpu.VMEM)


def call(kernel, name, outs, ins, out_specs=None, scratch=(), flops=0, size=0):
    return pl.pallas_call(
        kernel,
        out_shape=[jax.ShapeDtypeStruct(s, d) for s, d in outs],
        in_specs=ins,
        out_specs=out_specs or [VMEM] * len(outs),
        scratch_shapes=list(scratch),
        compiler_params=pltpu.CompilerParams(vmem_limit_bytes=40 * 1024 * 1024),
        cost_estimate=pl.CostEstimate(flops=flops, bytes_accessed=size, transcendentals=0),
        name=name,
    )


def bits_of(n):
    return n.bit_length() - 1


def padded(n):
    return -(-2 * n // LANES) * LANES


def horner(coefs, y):
    acc = jnp.full_like(y, coefs[-1])
    for c in coefs[-2::-1]:
        acc = acc * y + c
    return acc


def swap_pairs(x, mask):
    n = lax.axis_size("row") * lax.axis_size("col")
    return lax.ppermute(x, AXES, [(i, i ^ mask) for i in range(n)])


def lane_of(x):
    return lax.broadcasted_iota(jnp.int32, x.shape, x.ndim - 1)


def turn(x, by):
    lanes = x.shape[-1]
    by = by % lanes
    return x if by == 0 else pltpu.roll(x, lanes - by, x.ndim - 1)


def flip_blocks(x, width, bit):
    w = width << bit
    return jnp.where((lane_of(x) // w) % 2 == 1, turn(x, -w), turn(x, w))


def spread(x, base, n):
    parts = []
    for c in range(padded(n) // LANES):
        at = LANES * c
        first, second = turn(x, at + base), turn(x, at + base - n)
        parts.append(jnp.where(lane_of(x) + at < n, first, second))
    return parts[0] if len(parts) == 1 else jnp.concatenate(parts, axis=1)


def partner(x, n):
    return jnp.where(lane_of(x) < n, turn(x, n), turn(x, -n))


def tree_sum(parts):
    while len(parts) > 1:
        parts = [parts[i] + parts[i + 1] for i in range(0, len(parts), 2)]
    return parts[0]


def relative(x, row, per_row):
    for b in range(bits_of(x.shape[1] // per_row)):
        x = jnp.where(((row >> b) & 1) == 1, flip_blocks(x, per_row, b), x)
    return x


def project(phase, t_ref, index, out_ref, ready=None):
    n = phase.shape[0]
    rows = t_ref.shape[1]
    traps, lanes = index.shape
    y = phase * phase
    co = horner(COS, y).astype(BF)
    si = (phase * horner(SIN, y)).astype(BF)
    fill = [jnp.zeros((lanes - 2 * n, phase.shape[1]), BF)] if lanes > 2 * n else []
    if ready is not None:
        ready.wait()
    out_ref[...] = lax.dot_general(
        t_ref[0], jnp.concatenate([co, si] + fill, axis=0), NT, preferred_element_type=F32
    ) + lax.dot_general(t_ref[1], jnp.concatenate([-si, co] + fill, axis=0), NT, preferred_element_type=F32)
    found = []
    for g in range(traps // 8):
        high = index[g * 8:(g + 1) * 8] >> 3
        low = index[g * 8:(g + 1) * 8] & 7
        got = jnp.zeros((8, lanes), F32)
        for h in range(rows // 8):
            got = jnp.where(high == h, jnp.take_along_axis(out_ref[h * 8:(h + 1) * 8, :], low, axis=0), got)
        found.append(got)
    return found


def own_kernel(place_ref, ph_ref, index_ref, transfer_ref, out_ref, trap_ref, t_ref, sem):
    bring = pltpu.make_async_copy(transfer_ref, t_ref, sem)
    bring.start()
    per_row = ph_ref.shape[0]
    row = place_ref[0]
    index = spread(relative(index_ref[...], row, per_row) - row * t_ref.shape[1], 0, per_row)
    for g, got in enumerate(project(ph_ref[...], t_ref, index, out_ref, bring)):
        trap_ref[g * 8:(g + 1) * 8, :] = got


def other_kernel(order, per_row, place_ref, code_ref, index_ref, t_ref, own_ref, own_trap_ref, keep_ref, send_ref, out_ref):
    row, col = place_ref[0], place_ref[1]
    traps, count = index_ref.shape
    rows = t_ref.shape[1]
    index = spread(relative(index_ref[...], row, per_row) - row * rows, per_row, count - per_row)
    code = code_ref[...].astype(F32)
    size = jnp.log(jnp.abs(code)) * (1.0 / STEEP)
    found = project(jnp.where(code < 0, -size, size), t_ref, index, out_ref)
    n_own = own_ref.shape[1] // LANES
    sets = [(own_ref, c) for c in range(n_own)] + [(out_ref, c) for c in range(out_ref.shape[1] // LANES)]
    parts = len(sets)
    n_send = send_ref.shape[0] - 2 * parts * traps
    for g in range(traps // 8):
        for p, (ref, c) in enumerate(sets):
            lanes = slice(c * LANES, (c + 1) * LANES)
            value = own_trap_ref[g * 8:(g + 1) * 8, lanes] if p < n_own else found[g][:, lanes]
            large = value.astype(BF)
            at = n_send + p * traps + g * 8
            send_ref[at:at + 8, :] = large
            at += parts * traps
            send_ref[at:at + 8, :] = (value - large.astype(F32)).astype(BF)
    px = rows // len(order)
    half = len(order) // 2
    for s, j in enumerate(order):
        start = pl.multiple_of((col ^ j) * px, px)
        for p, (ref, c) in enumerate(sets):
            piece = ref[pl.ds(start, px), c * LANES:(c + 1) * LANES]
            at = ((s % half) * parts + p) * px
            if s < half:
                keep_ref[at:at + px, :] = piece
            else:
                send_ref[at:at + px, :] = piece.astype(BF)


def plan_kernel(per_row, rows, cross, place_ref, index_ref, levels_ref, old_ref, *refs):
    row = place_ref[0]
    traps, count = index_ref.shape
    index = relative(index_ref[...], row, per_row)
    target = relative(levels_ref[...], row, per_row).astype(F32)
    old = relative(old_ref[...], row, per_row)
    refs[0][...] = old
    inverse = 1.0 / target
    numer = old * (target * target)
    now_ref = refs[-1]
    group = 4

    def slots(pixels, outs):
        now_ref[...] = pixels

        def find(g, carry):
            base = pl.multiple_of(g * (8 * group), 8 * group)
            pixel = lax.broadcasted_iota(jnp.int32, (8, count), 0) + base
            acc = [jnp.full((8, count), -1, jnp.int32) for _ in range(group)]
            for k in range(traps):
                ind = jnp.broadcast_to(now_ref[k:k + 1, :], (8, count))
                for i in range(group):
                    acc[i] = jnp.where(ind == pixel + 8 * i, k, acc[i])
            for i in range(group):
                for ref, base_lane, n in outs:
                    ref[pl.ds(base + 8 * i, 8), :] = spread(acc[i], base_lane, n)
            return carry

        lax.fori_loop(0, rows // (8 * group), find, 0)

    mine = index - row * rows
    sets = ((0, per_row), (per_row, count - per_row))
    for s, (base, n) in enumerate(sets):
        idx_ref, inv_ref, num_ref, _ = refs[1 + 4 * s:5 + 4 * s]
        idx_ref[...] = spread(mine, base, n)
        inv_ref[...] = spread(inverse, base, n)
        num_ref[...] = spread(numer, base, n)
    slots(mine, [(refs[4], *sets[0]), (refs[8], *sets[1])])
    if cross:
        theirs = index - (1 - row) * rows
        refs[9][...] = spread(theirs, *sets[0])
        slots(theirs, [(refs[10], *sets[0])])


def scatter(idx_ref, value_ref, slot_ref, px_ref, n):
    traps, lanes = idx_ref.shape
    index = idx_ref[...]
    acc = [jnp.zeros((8, lanes), F32) for _ in range(traps // 8)]
    for k in range(traps):
        ind = jnp.broadcast_to(idx_ref[k:k + 1, :], (8, lanes))
        val = jnp.broadcast_to(value_ref[k:k + 1, :], (8, lanes))
        for g in range(traps // 8):
            acc[g] += jnp.where(index[g * 8:(g + 1) * 8, :] == ind, val, 0.0)
    for h in range(slot_ref.shape[0] // 8):
        slot = slot_ref[h * 8:(h + 1) * 8, :]
        high = slot >> 3
        low = slot & 7
        got = jnp.zeros((8, lanes), F32)
        for g in range(traps // 8):
            got = jnp.where(high == g, jnp.take_along_axis(acc[g], low, axis=0), got)
        px_ref[h * 8:(h + 1) * 8, :] = got
    proj = px_ref[...].T.astype(BF)
    turned = [proj[n:2 * n], -proj[:n]] + ([proj[2 * n:]] if lanes > 2 * n else [])
    return proj, jnp.concatenate(turned, axis=0)


def back_through(pair, t_ref, modes):
    return lax.dot_general(pair[0], t_ref[0, :, modes], NN, preferred_element_type=F32) + lax.dot_general(
        pair[1], t_ref[1, :, modes], NN, preferred_element_type=F32
    )


def values_kernel(per_row, crossing, own_ref, got_ref, t_ref, *refs):
    sets = (refs[0:3], refs[3:6])
    slot_ref, value_own_ref, away_ref, value_oth_ref, px_ref = refs[6:]
    rows, modes = t_ref.shape[1:]
    traps = sets[0][0].shape[0]
    ratios = []
    part = 0
    for (idx_ref, inv_ref, num_ref), value_ref, n in zip(sets, (value_own_ref, value_oth_ref), (per_row, LANES - per_row)):
        chunks = []
        for c in range(idx_ref.shape[1] // LANES):
            at = slice(part * traps, (part + 1) * traps)
            chunks.append(own_ref[at, :].astype(F32) + got_ref[at, :].astype(F32))
            part += 1
        v = chunks[0] if len(chunks) == 1 else jnp.concatenate(chunks, axis=1)
        within = (idx_ref[...] >= 0) & (idx_ref[...] < rows)
        square = v * v
        amp2 = square + partner(square, n) + 0.25
        ratios.append(jnp.where(within, jnp.sqrt(amp2) * inv_ref[...], 0.0))
        value_ref[...] = jnp.where(within, num_ref[...] / amp2 * v, 0.0)
    own_lanes = lane_of(ratios[0][:, :LANES]) < per_row
    q = jnp.where(own_lanes, ratios[0][:, :LANES], turn(ratios[1][:, :LANES], -per_row)).astype(BF)
    n = LANES - per_row
    back = back_through(scatter(sets[1][0], value_oth_ref, slot_ref, px_ref, n), t_ref, slice(crossing, modes))
    for j in range(n // per_row):
        away_ref[j, :traps, :] = q
        at = traps
        if crossing:
            away_ref[j, at:at + traps, :] = value_oth_ref[...].astype(BF)
            at += traps
        for w in range((modes - crossing) // LANES):
            lanes = slice(w * LANES, (w + 1) * LANES)
            away_ref[j, at:at + per_row, :] = back[j * per_row:(j + 1) * per_row, lanes].astype(BF)
            at += per_row
            away_ref[j, at:at + per_row, :] = back[n + j * per_row:n + (j + 1) * per_row, lanes].astype(BF)
            at += per_row


def mine_kernel(per_row, place_ref, value_ref, idx_ref, slot_ref, t_ref, far_ref, mine_ref, field_ref, px_ref):
    px = field_ref.shape[1]
    own = far_ref[:px, :]
    others = [far_ref[at:at + px, :] for at in range(px, far_ref.shape[0], px)]
    others = others[0] if len(others) == 1 else jnp.concatenate(others, axis=1)
    n = LANES - per_row
    first = lane_of(own) < per_row
    for part in range(2):
        theirs = turn(turn(others, part * n)[:, :LANES], -per_row)
        both = jnp.where(first, turn(own, part * per_row), theirs)
        field_ref[part] = relative(both, place_ref[0], per_row).astype(BF)
    pair = scatter(idx_ref, value_ref, slot_ref, px_ref, per_row)
    mine_ref[...] = back_through(pair, t_ref, slice(None))[:2 * per_row]


def final_kernel(per_row, crossing, place_ref, old_ref, mine_ref, sent_ref, got_ref, *refs):
    n_extra = len(refs) - (7 if crossing else 5)
    slm_ref, weights_ref = refs[n_extra:n_extra + 2]
    out_ref, scaled_ref, sems = refs[-3:]
    traps, count = old_ref.shape
    n_rows = count // per_row
    modes = mine_ref.shape[1]
    q = [sent_ref[0, :traps, :].astype(F32)]
    for m in range(1, n_rows):
        x = got_ref[m - 1, :traps, :].astype(F32)
        for b in range(bits_of(n_rows)):
            if (m >> b) & 1:
                x = flip_blocks(x, per_row, b)
        q.append(x)
    q = tree_sum(q)
    mean = jnp.sum(q, axis=0, keepdims=True) / TRAPS
    scaled_ref[...] = relative(old_ref[...] * mean / q, place_ref[0], per_row)
    copies = [pltpu.make_async_copy(scaled_ref, weights_ref, sems.at[0])]
    copies[0].start()
    scale = jnp.broadcast_to(mean, (count, count)).T[:per_row, 0:1]
    scale = scale * jnp.sqrt(jnp.float32(MODES) / jnp.float32(TRAPS))
    at = traps
    if crossing:
        idx_ref, slot_ref = refs[0:2]
        t_refs = refs[2:n_extra]
        px_ref, value_ref = refs[n_extra + 2:n_extra + 4]
        value_ref[...] = got_ref[0, at:at + traps, :].astype(F32)
        at += traps
        pair = scatter(idx_ref, value_ref, slot_ref, px_ref, per_row)
        across = [back_through(pair, t_ref, slice(None)) for t_ref in t_refs]
    step = 16
    for i in range(per_row // step):
        halves = []
        for part in range(2):
            first = part * per_row + i * step
            total = mine_ref[first:first + step, :]
            theirs = []
            if crossing:
                theirs += [x[first:first + step] for x in across]
            for w in range((modes - crossing) // LANES):
                piece = 0.0
                for m in range(n_rows - 1):
                    piece = piece + got_ref[m, at + 2 * w * per_row + first:at + 2 * w * per_row + first + step, :].astype(F32)
                theirs.append(piece)
            total = total + jnp.concatenate(theirs, axis=1)
            halves.append(total * scale[i * step:(i + 1) * step])
        inv = lax.rsqrt(halves[0] * halves[0] + halves[1] * halves[1] + 1.0)
        for part in range(2):
            out_ref[part, i * step:(i + 1) * step, :] = halves[part] * inv
        piece = pl.ds(i * step, step)
        copies.append(pltpu.make_async_copy(out_ref.at[:, piece, :], slm_ref.at[:, piece, :], sems.at[i + 1]))
        copies[-1].start()
    for copy in copies:
        copy.wait()


def body(transfer, phase, trap_index, levels, weights_old):
    n_rows = lax.axis_size("row")
    n_cols = lax.axis_size("col")
    row = lax.axis_index("row")
    col = lax.axis_index("col")
    rows, modes = transfer.shape[1:]
    count, traps = trap_index.shape
    per_row = count // n_rows
    px = rows // n_cols
    steps = bits_of(n_cols)
    place = jnp.stack([row, col]).astype(jnp.int32)
    masks = [1] + [(1 << b) | 1 for b in range(1, steps)]
    order = []
    for s in range(n_cols):
        j = 0
        for k in range(steps):
            if (s >> (steps - 1 - k)) & 1:
                j ^= masks[k]
        order.append(j)
    wide_own, wide_oth = padded(per_row), padded(count - per_row)
    parts = (wide_own + wide_oth) // LANES
    cuts = [0]
    for piece in CROSS if n_rows == 2 else ():
        cuts.append(cuts[-1] + modes * piece // 8 // LANES * LANES)
    crossing = cuts[-1]

    phase_t = phase.T
    code = jnp.where(phase_t < 0, -1.0, 1.0) * jnp.exp(STEEP * jnp.abs(phase_t))
    code = code.astype(BF)
    others = [swap_pairs(code, m * n_cols) for m in range(1, n_rows)]
    other = others[0] if n_rows == 2 else jnp.concatenate(others, axis=0)
    t_across = []
    for a, b in zip(cuts, cuts[1:]):
        piece = transfer[:, :, a:b]
        if t_across:
            t_across[-1], piece = lax.optimization_barrier((t_across[-1], piece))
        t_across.append(swap_pairs(piece, n_cols))

    cost = dict(flops=1, size=1)
    index, target, old = trap_index.T, levels.T, weights_old.T
    any_space = pl.BlockSpec(memory_space=pl.ANY)
    hbm = pl.BlockSpec(memory_space=pltpu.HBM)
    own_out, own_trap, near = call(
        own_kernel,
        "own",
        [((rows, wide_own), F32), ((traps, wide_own), F32), (transfer.shape, BF)],
        [SMEM, VMEM, VMEM, hbm],
        scratch=[pltpu.SemaphoreType.DMA],
        **cost,
    )(place, phase_t, index, transfer)
    n_half = rows * parts // 2
    n_trap = parts * traps
    keep, send = call(
        functools.partial(other_kernel, order, per_row),
        "other",
        [((n_half, LANES), F32), ((n_half + 2 * n_trap, LANES), BF)],
        [SMEM] + [VMEM] * 5,
        scratch=[pltpu.VMEM((rows, wide_oth), F32)],
        **cost,
    )(place, other, index, near, own_out, own_trap)

    trap = send[n_half:n_half + n_trap].astype(F32) + send[n_half + n_trap:].astype(F32)
    for k in range(steps):
        got = swap_pairs(send, masks[k])
        n = n_half >> k
        total = keep + got[:n].astype(F32)
        if k == steps - 1:
            break
        got_trap = got[n:n + n_trap].astype(F32)
        if k == 0:
            got_trap = got_trap + got[n + n_trap:].astype(F32)
        trap = (trap.astype(F32) + got_trap).astype(BF)
        keep = total[:n // 2]
        send = jnp.concatenate([total[n // 2:].astype(BF), trap], axis=0)
        if k == 0:
            send, index, target, old = lax.optimization_barrier((send, index, target, old))

    tables = [((traps, count), F32)]
    for wide in (wide_own, wide_oth):
        tables += [((traps, wide), jnp.int32), ((traps, wide), F32), ((traps, wide), F32), ((rows, wide), jnp.int32)]
    if crossing:
        tables += [((traps, wide_own), jnp.int32), ((rows, wide_own), jnp.int32)]
    tables = call(
        functools.partial(plan_kernel, per_row, rows, crossing > 0),
        "plan",
        tables,
        [SMEM] + [VMEM] * 3,
        scratch=[pltpu.VMEM((traps, count), jnp.int32)],
        **cost,
    )(place, index, target, old)
    old = tables[0]
    n_away = traps * (2 if crossing else 1) + 2 * per_row * (modes - crossing) // LANES
    value_own, away = call(
        functools.partial(values_kernel, per_row, crossing),
        "values",
        [((traps, wide_own), F32), ((n_rows - 1, n_away, LANES), BF)],
        [VMEM] * 10,
        scratch=[pltpu.VMEM((traps, wide_oth), F32), pltpu.VMEM((rows, wide_oth), F32)],
        **cost,
    )(trap, got[n:], near, *tables[1:4], *tables[5:8], tables[8])
    back = [swap_pairs(away[m - 1], m * n_cols)[None] for m in range(1, n_rows)]
    back = back[0] if n_rows == 2 else jnp.concatenate(back, axis=0)
    mine, field = call(
        functools.partial(mine_kernel, per_row),
        "mine",
        [((2 * per_row, modes), F32), ((2, px, count), BF)],
        [SMEM] + [VMEM] * 5,
        scratch=[pltpu.VMEM((rows, wide_own), F32)],
        **cost,
    )(place, value_own, tables[1], tables[4], near, total)
    extra = [tables[9], tables[10], *t_across] if crossing else []
    room = [pltpu.VMEM((rows, wide_own), F32), pltpu.VMEM((traps, wide_own), F32)] if crossing else []
    slm, weights = call(
        functools.partial(final_kernel, per_row, crossing),
        "final",
        [((2, per_row, modes), F32), ((traps, count), F32)],
        [SMEM] + [VMEM] * (4 + len(extra)),
        out_specs=[any_space, any_space],
        scratch=room
        + [
            pltpu.VMEM((2, per_row, modes), F32),
            pltpu.VMEM((traps, count), F32),
            pltpu.SemaphoreType.DMA((1 + per_row // 16,)),
        ],
        **cost,
    )(place, old, mine, away, back, *extra)

    return jnp.transpose(field, (1, 0, 2)), weights.T, jnp.transpose(slm, (2, 0, 1))


def solution(mesh):
    placed = (P(None, "row", "col"), P("col", "row"), P(), P(), P())
    return jax.shard_map(
        body,
        mesh=mesh,
        in_specs=placed,
        out_specs=(P(("row", "col"), None, None), P(), P("col", None, "row")),
        check_vma=False,
    )
```

time: 182 us -> 35.2 us (0.19)
  blocking collectives: 60.6 us -> 0 us
  waiting for transfers between devices: 56.5 us -> 12.4 us
  other arithmetic: 31 us -> 1.24 us
  between operations: 14.3 us -> 0.78 us
  local copies, waits for them, and re-layouts: 14.3 us -> 1.87 us
  Pallas kernels: 0 us -> 8.21 us
  starting transfers between devices: 3.55 us -> 10.5 us
    reduce_scatter x2 -> x0, waiting for transfers between devices: 56.5 us -> none  [the longest x1 56.5 us: body(): lax.psum_scatter(jnp.stack([first[:number] - second[number:], first[numbe...]
    all_gather x3 -> x0, blocking collectives: 51.8 us -> none  [the longest x1 21.8 us: body(): weights_new = lax.all_gather(my_weights, 'col', axis=0, tiled=True)]
    scatter-add x1 -> x0, other arithmetic: 24.8 us -> none  [body(): projected_p = jnp.zeros((per_col, 2, tile_rows), jnp.float32).at[local_id...]
    ppermute x0 -> x6, waiting for transfers between devices: none -> 12.4 us  [swap_pairs(): return lax.ppermute(x, AXES, [(i, i ^ mask) for i in range(n)])]
    ppermute x0 -> x6, starting transfers between devices: none -> 10.5 us  [swap_pairs(): return lax.ppermute(x, AXES, [(i, i ^ mask) for i in range(n)])]
    psum x1 -> x0, blocking collectives: 8.78 us -> none  [body(): shared = lax.psum(jnp.where(within[..., None], values, 0.0), 'row')]
    pallas_call x0 -> x6, Pallas kernels: none -> 8.21 us  [the longest x1 1.91 us: body(): call(functools.partial(plan_kernel, per_row, rows, crossing > 0), 'plan',...]
    gather x2 -> x0, local copies, waits for them, and re-layouts: 4.17 us -> none  [body(): values = mine_p[local_ids, :, placed]]
  transfers between devices with their start and end apart: 3 -> 6, of which waited for: 1 -> 6; matrix products, arithmetic and copies ran while one was open for 2% -> 2% of each run, Pallas kernels for 0% -> 13%
where the time goes in v1:
time: 35.2 us; the launch traced here: 35 us
  waiting for transfers between devices  12.4 us (35%)
  starting transfers between devices  10.5 us (30%)
  Pallas kernels  8.21 us (23%)
  local copies, waits for them, and re-layouts  1.87 us (5%)
  other arithmetic  1.24 us (4%)
  between operations  0.78 us (2%)
    ppermute x6, waiting for transfers between devices, swap_pairs(): return lax.ppermute(x, AXES, [(i, i ^ mask) for i in range(n)])  12.4 us
    ppermute x6, starting transfers between devices, swap_pairs(): return lax.ppermute(x, AXES, [(i, i ^ mask) for i in range(n)])  10.5 us
    pallas_call x1, Pallas kernels, body(): call(functools.partial(plan_kernel, per_row, rows, crossing > 0), 'plan',...  1.91 us
    unnamed x11, local copies, waits for them, and re-layouts  1.85 us
    pallas_call x1, Pallas kernels, body(): call(functools.partial(final_kernel, per_row, crossing), 'final', [((2, p...  1.68 us
    pallas_call x1, Pallas kernels, body(): call(own_kernel, 'own', [((rows, wide_own), F32), ((traps, wide_own), F32...  1.47 us
    pallas_call x1, Pallas kernels, body(): call(functools.partial(mine_kernel, per_row), 'mine', [((2 * per_row, mod...  1.2 us
    pallas_call x1, Pallas kernels, body(): call(functools.partial(other_kernel, order, per_row), 'other', [((n_half,...  1.16 us
  transfers between devices with their start and end apart: 6, of which 6 were waited for; matrix products, arithmetic and copies ran while one was open for 2% of the time, Pallas kernels for 13%

profile of v1, /device:TPU:0, one launch (start us, length us, event | category | flops | bytes accessed | tf_op | source)
XLA Modules:
  0.0 35.0 jit_solution(2138560771882751492)
XLA Ops:
  0.6 0.0 copy-start
  0.6 0.0 copy-start.2
  0.7 1.1 %multiply_convert_fusion = bf16[64,1024]{1,0:T(8,128)(2,1)S(1)} fusion(f32[1024,64]{0,1:T(8,128)} %param.6), kind=kLoop, calls=%fused_computation | loop fusion | flops 393216 | bytes 393216 | tf_op jit(solution)/shard_map/convert_element_type | solution.py:377
  1.7 3.0 %collective-permute-start = (bf16[64,1024]{1,0:T(8,128)(2,1)S(1)}, bf16[64,1024]{1,0:T(8,128)(2,1)S(1)}, u32[]{:S(2)}, u32[]{:S(2)}) collective-permute-start(bf16[64,1024]{1,0:T(8,128)(2,1)S(1)} %multiply_convert_fusion), channel_id=1, source_target_pairs={{0,16},{1,17},{2,18},{3,19},{4,20},{5,21},{6,22},{7,23},{8,24},{9,... | collective-permute-start | bytes 393224 | tf_op jit(solution)/shard_map/ppermute | solution.py:58
  4.8 0.1 pad_add_fusion.place_ref
  4.8 0.0 copy-done
  4.8 0.0 copy-done.2
  4.8 0.0 copy-start.1
  4.8 1.2 %copy-done.1 = bf16[2,256,1024]{2,1,0:T(8,128)(2,1)S(1)} copy-done((bf16[2,256,1024]{2,1,0:T(8,128)(2,1)S(1)}, bf16[2,256,1024]{2,1,0:T(8,128)(2,1)}, u32[]{:S(2)}) %copy-start.1) | copy-done | bytes 1048600
  6.1 1.5 %own.1 = (f32[256,128]{1,0:T(8,128)S(1)}, f32[64,128]{1,0:T(8,128)S(1)}, bf16[2,256,1024]{2,1,0:T(8,128)(2,1)S(1)}) custom-call(s32[2]{0:T(128)S(1)} %pad_add_fusion.place_ref, f32[64,1024]{1,0:T(8,128)S(1)} %bitcast.12, s32[64,128]{1,0:T(8,128)S(1)} %bitcast.13, bf16[2,256,1024]{2,1,0:T(8,128)(2,1)S(1)} %copy-done.1), custom_call_target="tpu_custom_call" | custom-call | flops 1 | bytes 1 | tf_op jit(solution)/shard_map/own/pallas_call | solution.py:391
  7.5 0.7 %collective-permute-done.code_ref = bf16[64,1024]{1,0:T(8,128)(2,1)S(1)} collective-permute-done((bf16[64,1024]{1,0:T(8,128)(2,1)S(1)}, bf16[64,1024]{1,0:T(8,128)(2,1)S(1)}, u32[]{:S(2)}, u32[]{:S(2)}) %collective-permute-start) | collective-permute-done | bytes 131104 | tf_op jit(solution)/shard_map/ppermute | solution.py:58
  8.3 1.2 %other.1 = (f32[256,128]{1,0:T(8,128)S(1)}, bf16[512,128]{1,0:T(8,128)(2,1)S(1)}) custom-call(s32[2]{0:T(128)S(1)} %pad_add_fusion.place_ref, bf16[64,1024]{1,0:T(8,128)(2,1)S(1)} %collective-permute-done.code_ref, s32[64,128]{1,0:T(8,128)S(1)} %bitcast.14, bf16[2,256,1024]{2,1,0:T(8,128)(2,1)S(1)} %get-tuple-element.27.t_ref, ...), custom_call_target="tpu_custom_call" | custom-call | flops 1 | bytes 1 | tf_op jit(solution)/shard_map/other/pallas_call | solution.py:401
  9.4 0.1 collective-permute-start.1
  9.5 1.3 %collective-permute-done.1 = bf16[512,128]{1,0:T(8,128)(2,1)S(1)} collective-permute-done((bf16[512,128]{1,0:T(8,128)(2,1)S(1)}, bf16[512,128]{1,0:T(8,128)(2,1)S(1)}, u32[]{:S(2)}, u32[]{:S(2)}) %collective-permute-start.1) | collective-permute-done | bytes 131104 | tf_op jit(solution)/shard_map/ppermute | solution.py:58
  10.9 1.5 %collective-permute-start.2 = (bf16[256,128]{1,0:T(8,128)(2,1)S(1)}, bf16[256,128]{1,0:T(8,128)(2,1)S(1)}, u32[]{:S(2)}, u32[]{:S(2)}) collective-permute-start(bf16[256,128]{1,0:T(8,128)(2,1)S(1)} %pad_maximum_fusion), channel_id=1, source_target_pairs={{0,3},{1,2},{2,1},{3,0},{4,7},{5,6},{6,5},{7,4},{8,11},{9,10},{10,... | collective-permute-start | bytes 196616 | tf_op jit(solution)/shard_map/ppermute | solution.py:58
  12.4 2.6 %collective-permute-done.2 = bf16[256,128]{1,0:T(8,128)(2,1)S(1)} collective-permute-done((bf16[256,128]{1,0:T(8,128)(2,1)S(1)}, bf16[256,128]{1,0:T(8,128)(2,1)S(1)}, u32[]{:S(2)}, u32[]{:S(2)}) %collective-permute-start.2) | collective-permute-done | bytes 65568 | tf_op jit(solution)/shard_map/ppermute | solution.py:58
  15.1 1.6 %collective-permute-start.3 = (bf16[192,128]{1,0:T(8,128)(2,1)S(1)}, bf16[192,128]{1,0:T(8,128)(2,1)S(1)}, u32[]{:S(2)}, u32[]{:S(2)}) collective-permute-start(bf16[192,128]{1,0:T(8,128)(2,1)S(1)} %pad_maximum_fusion.1), channel_id=1, source_target_pairs={{0,5},{1,4},{2,7},{3,6},{4,1},{5,0},{6,3},{7,2},{8,13},{9,12},{10,... | collective-permute-start | bytes 147464 | tf_op jit(solution)/shard_map/ppermute | solution.py:58
  16.7 2.2 %collective-permute-done.3 = bf16[192,128]{1,0:T(8,128)(2,1)S(1)} collective-permute-done((bf16[192,128]{1,0:T(8,128)(2,1)S(1)}, bf16[192,128]{1,0:T(8,128)(2,1)S(1)}, u32[]{:S(2)}, u32[]{:S(2)}) %collective-permute-start.3) | collective-permute-done | bytes 49184 | tf_op jit(solution)/shard_map/ppermute | solution.py:58
  19.0 0.0 copy-start.3
  19.0 0.0 copy-start.4
  19.0 2.6 %collective-permute-start.4 = (bf16[160,128]{1,0:T(8,128)(2,1)S(1)}, bf16[160,128]{1,0:T(8,128)(2,1)S(1)}, u32[]{:S(2)}, u32[]{:S(2)}) collective-permute-start(bf16[160,128]{1,0:T(8,128)(2,1)S(1)} %pad_maximum_fusion.2), channel_id=1, source_target_pairs={{0,9},{1,8},{2,11},{3,10},{4,13},{5,12},{6,15},{7,14},{8,1},{9,0},... | collective-permute-start | bytes 122888 | tf_op jit(solution)/shard_map/ppermute | solution.py:58
  21.6 0.0 copy-done.3
  21.6 0.0 copy-done.4
  21.6 1.9 %plan.1 = (f32[64,128]{1,0:T(8,128)S(1)}, s32[64,128]{1,0:T(8,128)S(1)}, f32[64,128]{1,0:T(8,128)S(1)}, f32[64,128]{1,0:T(8,128)S(1)}, s32[256,128]{1,0:T(8,128)...) custom-call(s32[2]{0:T(128)S(1)} %pad_add_fusion.place_ref, ...), custom_call_target="tpu_custom_call" | custom-call | flops 1 | bytes 1 | tf_op jit(solution)/shard_map/plan/pallas_call | solution.py:431
  23.5 0.1 collective-permute-done.4
  23.5 0.8 %values.1 = (f32[64,128]{1,0:T(8,128)S(1)}, bf16[1,1088,128]{2,1,0:T(8,128)(2,1)S(1)}) custom-call(bf16[128,128]{1,0:T(8,128)(2,1)S(1)} %add_convert_fusion.own_ref, bf16[128,128]{1,0:T(8,128)(2,1)S(1)} %slice.83.got_ref, bf16[2,256,1024]{2,1,0:T(8,128)(2,1)S(1)} %get-tuple-element.27.t_ref, s32[64,128]{1,0:T(8,128)S(1)} %get-tuple-element.36.refs_0_.idx_ref, ...), custom_call_target="tpu_custom_call" | custom-call | flops 1 | bytes 1 | tf_op jit(solution)/shard_map/values/pallas_call | solution.py:441
  24.3 1.7 %collective-permute-start.5 = (bf16[1088,128]{1,0:T(8,128)(2,1)S(1)}, bf16[1088,128]{1,0:T(8,128)(2,1)S(1)}, u32[]{:S(2)}, u32[]{:S(2)}) collective-permute-start(bf16[1088,128]{1,0:T(8,128)(2,1)S(1)} %bitcast.16), channel_id=1, source_target_pairs={{0,16},{1,17},{2,18},{3,19},{4,20},{5,21},{6,22},{7,23},{8,24},{9,... | collective-permute-start | bytes 835592 | tf_op jit(solution)/shard_map/ppermute | solution.py:58
  26.0 1.2 %mine.1 = (f32[128,1024]{1,0:T(8,128)S(1)}, bf16[2,16,128]{2,1,0:T(8,128)(2,1)S(1)}) custom-call(s32[2]{0:T(128)S(1)} %pad_add_fusion.place_ref, f32[64,128]{1,0:T(8,128)S(1)} %get-tuple-element.43.value_ref, s32[64,128]{1,0:T(8,128)S(1)} %get-tuple-element.36.refs_0_.idx_ref, s32[256,128]{1,0:T(8,128)S(1)} %get-tuple-element.44.slot_ref, ...), custom_call_target="tpu_custom_call" | custom-call | flops 1 | bytes 1 | tf_op jit(solution)/shard_map/mine/pallas_call | solution.py:451
  27.2 0.6 %copy.8 = bf16[16,2,128]{2,1,0:T(2,128)(2,1)} copy(bf16[16,2,128]{2,0,1:T(8,128)(2,1)S(1)} %bitcast.20) | data formatting | bytes 16384
  27.9 5.4 %collective-permute-done.5 = bf16[1088,128]{1,0:T(8,128)(2,1)S(1)} collective-permute-done((bf16[1088,128]{1,0:T(8,128)(2,1)S(1)}, bf16[1088,128]{1,0:T(8,128)(2,1)S(1)}, u32[]{:S(2)}, u32[]{:S(2)}) %collective-permute-start.5) | collective-permute-done | bytes 278560 | tf_op jit(solution)/shard_map/ppermute | solution.py:58
  33.3 1.7 %final.1 = (f32[2,64,1024]{2,1,0:T(8,128)}, f32[64,128]{1,0:T(8,128)}) custom-call(s32[2]{0:T(128)S(1)} %pad_add_fusion.place_ref, f32[64,128]{1,0:T(8,128)S(1)} %get-tuple-element.46.old_ref, f32[128,1024]{1,0:T(8,128)S(1)} %get-tuple-element.47.mine_ref, bf16[1,1088,128]{2,1,0:T(8,128)(2,1)S(1)} %get-tuple-element.48.sent_ref, ...), custom_call_target="tpu_custom_call" | custom-call | flops 1 | bytes 1 | tf_op jit(solution)/shard_map/final/pallas_call | solution.py:461
  (13 shorter events, 0.1 us)
Async XLA Ops:
  0.6 4.2 %copy-start = (f32[1024,64]{0,1:T(8,128)S(1)}, f32[1024,64]{0,1:T(8,128)}, u32[]{:S(2)}) copy-start(f32[1024,64]{0,1:T(8,128)} %param.6) | copy-start | bytes 786436
  0.6 4.2 %copy-start.2 = (s32[128,64]{0,1:T(8,128)S(1)}, s32[128,64]{0,1:T(8,128)}, u32[]{:S(2)}) copy-start(s32[128,64]{0,1:T(8,128)} %param.7) | copy-start | bytes 98308
  1.7 6.5 %collective-permute-start = (bf16[64,1024]{1,0:T(8,128)(2,1)S(1)}, bf16[64,1024]{1,0:T(8,128)(2,1)S(1)}, u32[]{:S(2)}, u32[]{:S(2)}) collective-permute-start(bf16[64,1024]{1,0:T(8,128)(2,1)S(1)} %multiply_convert_fusion), channel_id=1, source_target_pairs={{0,16},{1,17},{2,18},{3,19},{4,20},{5,21},{6,22},{7,23},{8,24},{9,... | collective-permute-start | bytes 393224 | tf_op jit(solution)/shard_map/ppermute | solution.py:58
  4.8 1.2 %copy-start.1 = (bf16[2,256,1024]{2,1,0:T(8,128)(2,1)S(1)}, bf16[2,256,1024]{2,1,0:T(8,128)(2,1)}, u32[]{:S(2)}) copy-start(bf16[2,256,1024]{2,1,0:T(8,128)(2,1)} %transfer_ref.1) | copy-start | bytes 3145732
  9.4 1.4 %collective-permute-start.1 = (bf16[512,128]{1,0:T(8,128)(2,1)S(1)}, bf16[512,128]{1,0:T(8,128)(2,1)S(1)}, u32[]{:S(2)}, u32[]{:S(2)}) collective-permute-start(bf16[512,128]{1,0:T(8,128)(2,1)S(1)} %get-tuple-element.30), channel_id=1, source_target_pairs={{0,1},{1,0},{2,3},{3,2},{4,5},{5,4},{6,7},{7,6},{8,9},{9,8},{10,11... | collective-permute-start | bytes 393224 | tf_op jit(solution)/shard_map/ppermute | solution.py:58
  10.9 4.1 %collective-permute-start.2 = (bf16[256,128]{1,0:T(8,128)(2,1)S(1)}, bf16[256,128]{1,0:T(8,128)(2,1)S(1)}, u32[]{:S(2)}, u32[]{:S(2)}) collective-permute-start(bf16[256,128]{1,0:T(8,128)(2,1)S(1)} %pad_maximum_fusion), channel_id=1, source_target_pairs={{0,3},{1,2},{2,1},{3,0},{4,7},{5,6},{6,5},{7,4},{8,11},{9,10},{10,... | collective-permute-start | bytes 196616 | tf_op jit(solution)/shard_map/ppermute | solution.py:58
  15.1 3.8 %collective-permute-start.3 = (bf16[192,128]{1,0:T(8,128)(2,1)S(1)}, bf16[192,128]{1,0:T(8,128)(2,1)S(1)}, u32[]{:S(2)}, u32[]{:S(2)}) collective-permute-start(bf16[192,128]{1,0:T(8,128)(2,1)S(1)} %pad_maximum_fusion.1), channel_id=1, source_target_pairs={{0,5},{1,4},{2,7},{3,6},{4,1},{5,0},{6,3},{7,2},{8,13},{9,12},{10,... | collective-permute-start | bytes 147464 | tf_op jit(solution)/shard_map/ppermute | solution.py:58
  19.0 2.6 %copy-start.3 = (s32[128,64]{0,1:T(8,128)S(1)}, s32[128,64]{0,1:T(8,128)}, u32[]{:S(2)}) copy-start(s32[128,64]{0,1:T(8,128)} %param.8) | copy-start | bytes 98308
  19.0 2.6 %copy-start.4 = (f32[128,64]{0,1:T(8,128)S(1)}, f32[128,64]{0,1:T(8,128)}, u32[]{:S(2)}) copy-start(f32[128,64]{0,1:T(8,128)} %param.9) | copy-start | bytes 98308
  19.0 4.5 %collective-permute-start.4 = (bf16[160,128]{1,0:T(8,128)(2,1)S(1)}, bf16[160,128]{1,0:T(8,128)(2,1)S(1)}, u32[]{:S(2)}, u32[]{:S(2)}) collective-permute-start(bf16[160,128]{1,0:T(8,128)(2,1)S(1)} %pad_maximum_fusion.2), channel_id=1, source_target_pairs={{0,9},{1,8},{2,11},{3,10},{4,13},{5,12},{6,15},{7,14},{8,1},{9,0},... | collective-permute-start | bytes 122888 | tf_op jit(solution)/shard_map/ppermute | solution.py:58
  24.3 8.9 %collective-permute-start.5 = (bf16[1088,128]{1,0:T(8,128)(2,1)S(1)}, bf16[1088,128]{1,0:T(8,128)(2,1)S(1)}, u32[]{:S(2)}, u32[]{:S(2)}) collective-permute-start(bf16[1088,128]{1,0:T(8,128)(2,1)S(1)} %bitcast.16), channel_id=1, source_target_pairs={{0,16},{1,17},{2,18},{3,19},{4,20},{5,21},{6,22},{7,23},{8,24},{9,... | collective-permute-start | bytes 835592 | tf_op jit(solution)/shard_map/ppermute | solution.py:58

commit v2 on v1

v2 whole, which is shorter than its diff:
```python
import functools

import jax
import jax.numpy as jnp
from jax import lax
from jax.experimental import pallas as pl
from jax.experimental.pallas import tpu as pltpu
from jax.sharding import PartitionSpec as P

MODES = 16384
TRAPS = 64
BF = jnp.bfloat16
F32 = jnp.float32
AXES = ("row", "col")
LANES = 128
SIN = (0.9999996052826214, -0.16666553769418907, 0.008332409691364227, -0.00019808794770261517, 2.6998844729663915e-06,
       -2.0368733379709898e-08)
COS = (0.999999989217114, -0.49999989221470714, 0.041666490704389186, -0.0013887810304225767, 2.4770020037729276e-05,
       -2.708030902998698e-07, 1.7249574387300172e-09)
STEEP = 25.0
NT = (((1,), (1,)), ((), ()))
NN = (((1,), (0,)), ((), ()))
VMEM = pl.BlockSpec(memory_space=pltpu.VMEM)


def call(kernel, name, outs, ins, out_specs=None, scratch=(), flops=0, size=0):
    return pl.pallas_call(
        kernel,
        out_shape=[jax.ShapeDtypeStruct(s, d) for s, d in outs],
        in_specs=ins,
        out_specs=out_specs or [VMEM] * len(outs),
        scratch_shapes=list(scratch),
        compiler_params=pltpu.CompilerParams(vmem_limit_bytes=40 * 1024 * 1024),
        cost_estimate=pl.CostEstimate(flops=flops, bytes_accessed=size, transcendentals=0),
        name=name,
    )


def bits_of(n):
    return n.bit_length() - 1


def padded(n):
    return -(-2 * n // LANES) * LANES


def horner(coefs, y):
    acc = jnp.full_like(y, coefs[-1])
    for c in coefs[-2::-1]:
        acc = acc * y + c
    return acc


def swap_pairs(x, mask):
    n = lax.axis_size("row") * lax.axis_size("col")
    return lax.ppermute(x, AXES, [(i, i ^ mask) for i in range(n)])


def lane_of(x):
    return lax.broadcasted_iota(jnp.int32, x.shape, x.ndim - 1)


def turn(x, by):
    lanes = x.shape[-1]
    by = by % lanes
    return x if by == 0 else pltpu.roll(x, lanes - by, x.ndim - 1)


def flip_blocks(x, width, bit):
    w = width << bit
    return jnp.where((lane_of(x) // w) % 2 == 1, turn(x, -w), turn(x, w))


def spread(x, base, n):
    parts = []
    for c in range(padded(n) // LANES):
        at = LANES * c
        first, second = turn(x, at + base), turn(x, at + base - n)
        parts.append(jnp.where(lane_of(x) + at < n, first, second))
    return parts[0] if len(parts) == 1 else jnp.concatenate(parts, axis=1)


def partner(x, n):
    return jnp.where(lane_of(x) < n, turn(x, n), turn(x, -n))


def tree_sum(parts):
    while len(parts) > 1:
        parts = [parts[i] + parts[i + 1] for i in range(0, len(parts), 2)]
    return parts[0]


def relative(x, row, per_row):
    for b in range(bits_of(x.shape[1] // per_row)):
        x = jnp.where(((row >> b) & 1) == 1, flip_blocks(x, per_row, b), x)
    return x


def project(phase, t_ref, index, out_ref):
    n = phase.shape[0]
    rows = t_ref.shape[1]
    traps, lanes = index.shape
    y = phase * phase
    co = horner(COS, y).astype(BF)
    si = (phase * horner(SIN, y)).astype(BF)
    fill = [jnp.zeros((lanes - 2 * n, phase.shape[1]), BF)] if lanes > 2 * n else []
    out_ref[...] = lax.dot_general(
        t_ref[0], jnp.concatenate([co, si] + fill, axis=0), NT, preferred_element_type=F32
    ) + lax.dot_general(t_ref[1], jnp.concatenate([-si, co] + fill, axis=0), NT, preferred_element_type=F32)
    found = []
    for g in range(traps // 8):
        high = index[g * 8:(g + 1) * 8] >> 3
        low = index[g * 8:(g + 1) * 8] & 7
        got = jnp.zeros((8, lanes), F32)
        for h in range(rows // 8):
            got = jnp.where(high == h, jnp.take_along_axis(out_ref[h * 8:(h + 1) * 8, :], low, axis=0), got)
        found.append(got)
    return found


def own_kernel(ph_ref, index_ref, t_ref, out_ref, trap_ref):
    per_row = ph_ref.shape[0]
    row = lax.axis_index("row")
    index = spread(relative(index_ref[...], row, per_row) - row * t_ref.shape[1], 0, per_row)
    for g, got in enumerate(project(ph_ref[...], t_ref, index, out_ref)):
        trap_ref[g * 8:(g + 1) * 8, :] = got


def other_kernel(order, per_row, code_ref, index_ref, t_ref, own_ref, own_trap_ref, trap_ref, keep_ref, send_ref, out_ref):
    row, col = lax.axis_index("row"), lax.axis_index("col")
    traps, count = index_ref.shape
    rows = t_ref.shape[1]
    index = spread(relative(index_ref[...], row, per_row) - row * rows, per_row, count - per_row)
    code = code_ref[...].astype(F32)
    size = jnp.log(jnp.abs(code)) * (1.0 / STEEP)
    found = project(jnp.where(code < 0, -size, size), t_ref, index, out_ref)
    n_own = own_ref.shape[1] // LANES
    sets = [(own_ref, c) for c in range(n_own)] + [(out_ref, c) for c in range(out_ref.shape[1] // LANES)]
    parts = len(sets)
    for g in range(traps // 8):
        for p, (ref, c) in enumerate(sets):
            lanes = slice(c * LANES, (c + 1) * LANES)
            at = p * traps + g * 8
            trap_ref[at:at + 8, :] = own_trap_ref[g * 8:(g + 1) * 8, lanes] if p < n_own else found[g][:, lanes]
    px = rows // len(order)
    half = len(order) // 2
    for s, j in enumerate(order):
        start = pl.multiple_of((col ^ j) * px, px)
        for p, (ref, c) in enumerate(sets):
            piece = ref[pl.ds(start, px), c * LANES:(c + 1) * LANES]
            at = ((s % half) * parts + p) * px
            if s < half:
                keep_ref[at:at + px, :] = piece
            else:
                send_ref[at:at + px, :] = piece.astype(BF)


def plan_kernel(per_row, rows, index_ref, levels_ref, old_ref, now_ref, *refs):
    row = lax.axis_index("row")
    count = index_ref.shape[1]
    target = relative(levels_ref[...], row, per_row).astype(F32)
    old = relative(old_ref[...], row, per_row)
    mine = relative(index_ref[...], row, per_row) - row * rows
    now_ref[...] = mine
    refs[0][...] = old
    inverse = 1.0 / target
    numer = old * (target * target)
    for s, (base, n) in enumerate(((0, per_row), (per_row, count - per_row))):
        idx_ref, inv_ref, num_ref = refs[1 + 3 * s:4 + 3 * s]
        idx_ref[...] = spread(mine, base, n)
        inv_ref[...] = spread(inverse, base, n)
        num_ref[...] = spread(numer, base, n)


def slot_kernel(per_row, now_ref, *slot_refs):
    traps, count = now_ref.shape
    group = 8

    def find(g, carry):
        start = pl.multiple_of(g * (8 * group), 8 * group)
        pixels = [lax.broadcasted_iota(jnp.int32, (8, count), 0) + (start + 8 * i) for i in range(group)]
        acc = [jnp.full((8, count), -1, jnp.int32) for _ in range(group)]
        for k in range(traps):
            ind = jnp.broadcast_to(now_ref[k:k + 1, :], (8, count))
            for i in range(group):
                acc[i] = jnp.where(ind == pixels[i], k, acc[i])
        for i in range(group):
            for ref, (base, n) in zip(slot_refs, ((0, per_row), (per_row, count - per_row))):
                ref[pl.ds(start + 8 * i, 8), :] = spread(acc[i], base, n)
        return carry

    lax.fori_loop(0, slot_refs[0].shape[0] // (8 * group), find, 0)


def scatter(idx_ref, value_ref, slot_ref, px_ref, n):
    traps, lanes = idx_ref.shape
    index = idx_ref[...]
    acc = [jnp.zeros((8, lanes), F32) for _ in range(traps // 8)]
    for k in range(traps):
        ind = jnp.broadcast_to(idx_ref[k:k + 1, :], (8, lanes))
        val = jnp.broadcast_to(value_ref[k:k + 1, :], (8, lanes))
        for g in range(traps // 8):
            acc[g] += jnp.where(index[g * 8:(g + 1) * 8, :] == ind, val, 0.0)
    for h in range(slot_ref.shape[0] // 8):
        slot = slot_ref[h * 8:(h + 1) * 8, :]
        high = slot >> 3
        low = slot & 7
        got = jnp.zeros((8, lanes), F32)
        for g in range(traps // 8):
            got = jnp.where(high == g, jnp.take_along_axis(acc[g], low, axis=0), got)
        px_ref[h * 8:(h + 1) * 8, :] = got
    proj = px_ref[...].T.astype(BF)
    turned = [proj[n:2 * n], -proj[:n]] + ([proj[2 * n:]] if lanes > 2 * n else [])
    return proj, jnp.concatenate(turned, axis=0)


def back_through(pair, t_ref):
    return lax.dot_general(pair[0], t_ref[0], NN, preferred_element_type=F32) + lax.dot_general(
        pair[1], t_ref[1], NN, preferred_element_type=F32
    )


def values_kernel(per_row, own_ref, got_ref, t_ref, *refs):
    sets = (refs[0:3], refs[3:6])
    slot_ref, value_own_ref, away_ref, value_oth_ref, px_ref = refs[6:]
    rows, modes = t_ref.shape[1:]
    traps = sets[0][0].shape[0]
    ratios = []
    part = 0
    for (idx_ref, inv_ref, num_ref), value_ref, n in zip(sets, (value_own_ref, value_oth_ref), (per_row, LANES - per_row)):
        chunks = []
        for c in range(idx_ref.shape[1] // LANES):
            at = slice(part * traps, (part + 1) * traps)
            chunks.append(own_ref[at, :].astype(F32) + got_ref[at, :].astype(F32))
            part += 1
        v = chunks[0] if len(chunks) == 1 else jnp.concatenate(chunks, axis=1)
        within = (idx_ref[...] >= 0) & (idx_ref[...] < rows)
        square = v * v
        amp2 = square + partner(square, n) + 0.25
        ratios.append(jnp.where(within, jnp.sqrt(amp2) * inv_ref[...], 0.0))
        value_ref[...] = jnp.where(within, num_ref[...] / amp2 * v, 0.0)
    own_lanes = lane_of(ratios[0][:, :LANES]) < per_row
    q = jnp.where(own_lanes, ratios[0][:, :LANES], turn(ratios[1][:, :LANES], -per_row)).astype(BF)
    n = LANES - per_row
    back = back_through(scatter(sets[1][0], value_oth_ref, slot_ref, px_ref, n), t_ref)
    for j in range(n // per_row):
        away_ref[j, :traps, :] = q
        at = traps
        for w in range(modes // LANES):
            lanes = slice(w * LANES, (w + 1) * LANES)
            away_ref[j, at:at + per_row, :] = back[j * per_row:(j + 1) * per_row, lanes].astype(BF)
            at += per_row
            away_ref[j, at:at + per_row, :] = back[n + j * per_row:n + (j + 1) * per_row, lanes].astype(BF)
            at += per_row


def mine_kernel(per_row, value_ref, idx_ref, slot_ref, t_ref, far_ref, mine_ref, field_ref, px_ref):
    px = field_ref.shape[1]
    own = far_ref[:px, :]
    others = [far_ref[at:at + px, :] for at in range(px, far_ref.shape[0], px)]
    others = others[0] if len(others) == 1 else jnp.concatenate(others, axis=1)
    n = LANES - per_row
    first = lane_of(own) < per_row
    for part in range(2):
        theirs = turn(turn(others, part * n)[:, :LANES], -per_row)
        both = jnp.where(first, turn(own, part * per_row), theirs)
        field_ref[part] = relative(both, lax.axis_index("row"), per_row).astype(BF)
    pair = scatter(idx_ref, value_ref, slot_ref, px_ref, per_row)
    mine_ref[...] = back_through(pair, t_ref)[:2 * per_row]


def final_kernel(per_row, old_ref, mine_ref, sent_ref, got_ref, slm_ref, weights_ref, out_ref, scaled_ref, sems):
    traps, count = old_ref.shape
    n_rows = count // per_row
    modes = mine_ref.shape[1]
    q = [sent_ref[0, :traps, :].astype(F32)]
    for m in range(1, n_rows):
        x = got_ref[m - 1, :traps, :].astype(F32)
        for b in range(bits_of(n_rows)):
            if (m >> b) & 1:
                x = flip_blocks(x, per_row, b)
        q.append(x)
    q = tree_sum(q)
    mean = jnp.sum(q, axis=0, keepdims=True) / TRAPS
    scaled_ref[...] = relative(old_ref[...] * mean / q, lax.axis_index("row"), per_row)
    copies = [pltpu.make_async_copy(scaled_ref, weights_ref, sems.at[0])]
    copies[0].start()
    scale = jnp.broadcast_to(mean, (count, count)).T[:per_row, 0:1]
    scale = scale * jnp.sqrt(jnp.float32(MODES) / jnp.float32(TRAPS))
    at = traps
    step = 16
    for i in range(per_row // step):
        halves = []
        for part in range(2):
            first = part * per_row + i * step
            total = mine_ref[first:first + step, :]
            theirs = []
            for w in range(modes // LANES):
                piece = 0.0
                for m in range(n_rows - 1):
                    piece = piece + got_ref[m, at + 2 * w * per_row + first:at + 2 * w * per_row + first + step, :].astype(F32)
                theirs.append(piece)
            total = total + jnp.concatenate(theirs, axis=1)
            halves.append(total * scale[i * step:(i + 1) * step])
        inv = lax.rsqrt(halves[0] * halves[0] + halves[1] * halves[1] + 1.0)
        for part in range(2):
            out_ref[part, i * step:(i + 1) * step, :] = halves[part] * inv
        piece = pl.ds(i * step, step)
        copies.append(pltpu.make_async_copy(out_ref.at[:, piece, :], slm_ref.at[:, piece, :], sems.at[i + 1]))
        copies[-1].start()
    for copy in copies:
        copy.wait()


def body(transfer, phase, trap_index, levels, weights_old):
    n_rows = lax.axis_size("row")
    n_cols = lax.axis_size("col")
    rows, modes = transfer.shape[1:]
    count, traps = trap_index.shape
    per_row = count // n_rows
    px = rows // n_cols
    steps = bits_of(n_cols)
    masks = [1] + [(1 << b) | 1 for b in range(1, steps)]
    order = []
    for s in range(n_cols):
        j = 0
        for k in range(steps):
            if (s >> (steps - 1 - k)) & 1:
                j ^= masks[k]
        order.append(j)
    wide_own, wide_oth = padded(per_row), padded(count - per_row)
    parts = (wide_own + wide_oth) // LANES
    phase_t = phase.T
    code = jnp.where(phase_t < 0, -1.0, 1.0) * jnp.exp(STEEP * jnp.abs(phase_t))
    code = code.astype(BF)
    others = [swap_pairs(code, m * n_cols) for m in range(1, n_rows)]
    other = others[0] if n_rows == 2 else jnp.concatenate(others, axis=0)

    cost = dict(flops=1, size=1)
    index, target, old = trap_index.T, levels.T, weights_old.T
    any_space = pl.BlockSpec(memory_space=pl.ANY)
    sets = (wide_own, wide_oth)
    now, old, *tables = call(
        functools.partial(plan_kernel, per_row, rows),
        "plan",
        [((traps, count), jnp.int32), ((traps, count), F32)]
        + [((traps, wide), d) for wide in sets for d in (jnp.int32, F32, F32)],
        [VMEM] * 3,
        **cost,
    )(index, target, old)

    other, now = lax.optimization_barrier((other, now))
    own_out, own_trap = call(
        own_kernel,
        "own",
        [((rows, wide_own), F32), ((traps, wide_own), F32)],
        [VMEM, VMEM, VMEM],
        **cost,
    )(phase_t, index, transfer)
    n_half = rows * parts // 2
    n_trap = parts * traps
    trap, keep, send = call(
        functools.partial(other_kernel, order, per_row),
        "other",
        [((n_trap, LANES), F32), ((n_half, LANES), F32), ((n_half, LANES), BF)],
        [VMEM] * 5,
        scratch=[pltpu.VMEM((rows, wide_oth), F32)],
        **cost,
    )(other, index, transfer, own_out, own_trap)

    total = trap
    for k in range(steps):
        trap = total if k == 0 else total.astype(BF)
        got = swap_pairs(trap, masks[k])
        total = trap.astype(F32) + got.astype(F32)
        if k == 0:
            total, now = lax.optimization_barrier((total, now))
            slots = call(
                functools.partial(slot_kernel, per_row), "slots", [((rows, wide), jnp.int32) for wide in sets], [VMEM], **cost
            )(now)
        if k == 1:
            total, *slots = lax.optimization_barrier((total, *slots))
    for k in range(steps):
        block = keep + swap_pairs(send, masks[k]).astype(F32)
        half = block.shape[0] // 2
        keep, send = block[:half], block[half:].astype(BF)

    n_away = traps + 2 * per_row * modes // LANES
    value_own, away = call(
        functools.partial(values_kernel, per_row),
        "values",
        [((traps, wide_own), F32), ((n_rows - 1, n_away, LANES), BF)],
        [VMEM] * 10,
        scratch=[pltpu.VMEM((traps, wide_oth), F32), pltpu.VMEM((rows, wide_oth), F32)],
        **cost,
    )(trap, got, transfer, *tables, slots[1])
    back = [swap_pairs(away[m - 1], m * n_cols)[None] for m in range(1, n_rows)]
    back = back[0] if n_rows == 2 else jnp.concatenate(back, axis=0)
    mine, field = call(
        functools.partial(mine_kernel, per_row),
        "mine",
        [((2 * per_row, modes), F32), ((2, px, count), BF)],
        [VMEM] * 5,
        scratch=[pltpu.VMEM((rows, wide_own), F32)],
        **cost,
    )(value_own, tables[0], slots[0], transfer, block)
    slm, weights = call(
        functools.partial(final_kernel, per_row),
        "final",
        [((2, per_row, modes), F32), ((traps, count), F32)],
        [VMEM] * 4,
        out_specs=[any_space, any_space],
        scratch=[
            pltpu.VMEM((2, per_row, modes), F32),
            pltpu.VMEM((traps, count), F32),
            pltpu.SemaphoreType.DMA((1 + per_row // 16,)),
        ],
        **cost,
    )(old, mine, away, back)

    return jnp.transpose(field, (1, 0, 2)), weights.T, jnp.transpose(slm, (2, 0, 1))


def solution(mesh):
    placed = (P(None, "row", "col"), P("col", "row"), P(), P(), P())
    return jax.shard_map(
        body,
        mesh=mesh,
        in_specs=placed,
        out_specs=(P(("row", "col"), None, None), P(), P("col", None, "row")),
        check_vma=False,
    )
```

time: 35.2 us -> 32.5 us (0.923)
  starting transfers between devices: 10.5 us -> 16.4 us
  waiting for transfers between devices: 12.4 us -> 7.41 us
  Pallas kernels: 8.21 us -> 4.8 us
    ppermute x6 -> x10, starting transfers between devices: 10.5 us -> 16.4 us  [swap_pairs(): return lax.ppermute(x, AXES, [(i, i ^ mask) for i in range(n)])]
    ppermute x6 -> x10, waiting for transfers between devices: 12.4 us -> 7.41 us  [swap_pairs(): return lax.ppermute(x, AXES, [(i, i ^ mask) for i in range(n)])]
    pallas_call x4 -> x5, Pallas kernels: 5.54 us -> 3.6 us  [the longest x1 1.14 us: body(): call(functools.partial(final_kernel, per_row), 'final', [((2, per_row, mo...]
    pallas_call x1, Pallas kernels: 1.47 us -> 0.53 us  [body(): call(own_kernel, 'own', [((rows, wide_own), F32), ((traps, wide_own), F32...]
    pallas_call x1, Pallas kernels: 1.2 us -> 0.67 us  [body(): call(functools.partial(mine_kernel, per_row), 'mine', [((2 * per_row, mod...]
    unnamed x11 -> x13, local copies, waits for them, and re-layouts: 1.85 us -> 1.85 us
  transfers between devices with their start and end apart: 6 -> 10, of which waited for: 6 -> 6; matrix products, arithmetic and copies ran while one was open for 2% -> 2% of each run, Pallas kernels for 13% -> 9%
where the time goes in v2:
time: 32.5 us; the launch traced here: 32.4 us
  starting transfers between devices  16.4 us (50%)
  waiting for transfers between devices  7.41 us (23%)
  Pallas kernels  4.8 us (15%)
  local copies, waits for them, and re-layouts  1.86 us (6%)
  other arithmetic  1.13 us (3%)
  between operations  0.78 us (2%)
    ppermute x10, starting transfers between devices, swap_pairs(): return lax.ppermute(x, AXES, [(i, i ^ mask) for i in range(n)])  16.4 us
    ppermute x10, waiting for transfers between devices, swap_pairs(): return lax.ppermute(x, AXES, [(i, i ^ mask) for i in range(n)])  7.41 us
    unnamed x13, local copies, waits for them, and re-layouts  1.85 us
    pallas_call x1, Pallas kernels, body(): call(functools.partial(final_kernel, per_row), 'final', [((2, per_row, mo...  1.14 us
    convert_element_type x1, other arithmetic, body(): code = code.astype(BF)  1.06 us
    pallas_call x1, Pallas kernels, body(): call(functools.partial(slot_kernel, per_row), 'slots', [((rows, wide), jn...  0.88 us
    pallas_call x1, Pallas kernels, body(): call(functools.partial(values_kernel, per_row), 'values', [((traps, wide_...  0.78 us
    pallas_call x1, Pallas kernels, body(): call(functools.partial(mine_kernel, per_row), 'mine', [((2 * per_row, mod...  0.67 us
  transfers between devices with their start and end apart: 10, of which 6 were waited for; matrix products, arithmetic and copies ran while one was open for 2% of the time, Pallas kernels for 9%

profile of v2, /device:TPU:0, one launch (start us, length us, event | category | flops | bytes accessed | tf_op | source)
XLA Modules:
  0.0 32.4 jit_solution(16172517183778760811)
XLA Ops:
  0.6 0.0 copy-start.2
  0.6 0.0 copy-start.3
  0.7 0.0 copy-start.4
  0.7 0.0 copy-start.5
  0.7 1.1 %multiply_convert_fusion = bf16[64,1024]{1,0:T(8,128)(2,1)S(1)} fusion(f32[1024,64]{0,1:T(8,128)} %param.6), kind=kLoop, calls=%fused_computation | loop fusion | flops 393216 | bytes 393216 | tf_op jit(solution)/shard_map/convert_element_type | solution.py:335
  1.7 3.0 %collective-permute-start = (bf16[64,1024]{1,0:T(8,128)(2,1)S(1)}, bf16[64,1024]{1,0:T(8,128)(2,1)S(1)}, u32[]{:S(2)}, u32[]{:S(2)}) collective-permute-start(bf16[64,1024]{1,0:T(8,128)(2,1)S(1)} %multiply_convert_fusion), channel_id=1, source_target_pairs={{0,16},{1,17},{2,18},{3,19},{4,20},{5,21},{6,22},{7,23},{8,24},{9,... | collective-permute-start | bytes 393224 | tf_op jit(solution)/shard_map/ppermute | solution.py:56
  4.8 0.0 copy-done.3
  4.8 0.0 copy-done.4
  4.8 0.0 copy-done.5
  4.8 0.2 plan.1
  5.0 0.0 copy-done.2
  5.0 0.0 copy-start
  5.0 1.2 %copy-done = bf16[2,256,1024]{2,1,0:T(8,128)(2,1)S(1)} copy-done((bf16[2,256,1024]{2,1,0:T(8,128)(2,1)S(1)}, bf16[2,256,1024]{2,1,0:T(8,128)(2,1)}, u32[]{:S(2)}) %copy-start) | copy-done | bytes 1048600
  6.2 0.0 copy-start.1
  6.2 0.5 %own.1 = (f32[256,128]{1,0:T(8,128)S(1)}, f32[64,128]{1,0:T(8,128)S(1)}) custom-call(f32[64,1024]{1,0:T(8,128)S(1)} %bitcast.10, s32[64,128]{1,0:T(8,128)S(1)} %bitcast.12, bf16[2,256,1024]{2,1,0:T(8,128)(2,1)S(1)} %copy-done), custom_call_target="tpu_custom_call" | custom-call | flops 1 | bytes 1 | tf_op jit(solution)/shard_map/own/pallas_call | solution.py:353
  6.7 1.5 %collective-permute-done.code_ref = bf16[64,1024]{1,0:T(8,128)(2,1)S(1)} collective-permute-done((bf16[64,1024]{1,0:T(8,128)(2,1)S(1)}, bf16[64,1024]{1,0:T(8,128)(2,1)S(1)}, u32[]{:S(2)}, u32[]{:S(2)}) %collective-permute-start) | collective-permute-done | bytes 131104 | tf_op jit(solution)/shard_map/ppermute | solution.py:56
  8.3 0.0 copy-done.1
  8.3 0.6 %other.1 = (f32[128,128]{1,0:T(8,128)S(1)}, f32[256,128]{1,0:T(8,128)S(1)}, bf16[256,128]{1,0:T(8,128)(2,1)S(1)}) custom-call(bf16[64,1024]{1,0:T(8,128)(2,1)S(1)} %collective-permute-done.code_ref, s32[64,128]{1,0:T(8,128)S(1)} %bitcast.13, bf16[2,256,1024]{2,1,0:T(8,128)(2,1)S(1)} %copy-done.1, f32[256,128]{1,0:T(8,128)S(1)} %get-tuple-element.33.own_ref, ...), custom_call_target="tpu_custom_call" | custom-call | flops 1 | bytes 1 | tf_op jit(solution)/shard_map/other/pallas_call | solution.py:362
  8.9 0.1 collective-permute-start.1
  9.0 1.2 %collective-permute-done.1 = f32[128,128]{1,0:T(8,128)S(1)} collective-permute-done((f32[128,128]{1,0:T(8,128)S(1)}, f32[128,128]{1,0:T(8,128)S(1)}, u32[]{:S(2)}, u32[]{:S(2)}) %collective-permute-start.1) | collective-permute-done | bytes 65568 | tf_op jit(solution)/shard_map/ppermute | solution.py:56
  10.2 1.5 %collective-permute-start.2 = (bf16[128,128]{1,0:T(8,128)(2,1)S(1)}, bf16[128,128]{1,0:T(8,128)(2,1)S(1)}, u32[]{:S(2)}, u32[]{:S(2)}) collective-permute-start(bf16[128,128]{1,0:T(8,128)(2,1)S(1)} %add.21), channel_id=1, source_target_pairs={{0,3},{1,2},{2,1},{3,0},{4,7},{5,6},{6,5},{7,4},{8,11},{9,10},{10,... | collective-permute-start | bytes 98312 | tf_op jit(solution)/shard_map/ppermute | solution.py:56
  11.8 0.4 %collective-permute-start.5 = (bf16[256,128]{1,0:T(8,128)(2,1)S(1)}, bf16[256,128]{1,0:T(8,128)(2,1)S(1)}, u32[]{:S(2)}, u32[]{:S(2)}) collective-permute-start(bf16[256,128]{1,0:T(8,128)(2,1)S(1)} %get-tuple-element.52), channel_id=1, source_target_pairs={{0,1},{1,0},{2,3},{3,2},{4,5},{5,4},{6,7},{7,6},{8,9},{9,8},{10,11... | collective-permute-start | bytes 196616 | tf_op jit(solution)/shard_map/ppermute | solution.py:56
  12.1 0.9 %slots.1 = (s32[256,128]{1,0:T(8,128)S(1)}, s32[256,128]{1,0:T(8,128)S(1)}) custom-call(s32[64,128]{1,0:T(8,128)S(1)} %get-tuple-element.38.now_ref), custom_call_target="tpu_custom_call" | custom-call | flops 1 | bytes 1 | tf_op jit(solution)/shard_map/slots/pallas_call | solution.py:378
  13.0 0.6 %collective-permute-done.2 = bf16[128,128]{1,0:T(8,128)(2,1)S(1)} collective-permute-done((bf16[128,128]{1,0:T(8,128)(2,1)S(1)}, bf16[128,128]{1,0:T(8,128)(2,1)S(1)}, u32[]{:S(2)}, u32[]{:S(2)}) %collective-permute-start.2) | collective-permute-done | bytes 32800 | tf_op jit(solution)/shard_map/ppermute | solution.py:56
  13.7 1.6 %collective-permute-start.3 = (bf16[128,128]{1,0:T(8,128)(2,1)S(1)}, bf16[128,128]{1,0:T(8,128)(2,1)S(1)}, u32[]{:S(2)}, u32[]{:S(2)}) collective-permute-start(bf16[128,128]{1,0:T(8,128)(2,1)S(1)} %convert_add_fusion.1), channel_id=1, source_target_pairs={{0,5},{1,4},{2,7},{3,6},{4,1},{5,0},{6,3},{7,2},{8,13},{9,12},{10,... | collective-permute-start | bytes 98312 | tf_op jit(solution)/shard_map/ppermute | solution.py:56
  15.3 0.0 collective-permute-done.5
  15.3 1.5 %collective-permute-start.6 = (bf16[128,128]{1,0:T(8,128)(2,1)S(1)}, bf16[128,128]{1,0:T(8,128)(2,1)S(1)}, u32[]{:S(2)}, u32[]{:S(2)}) collective-permute-start(bf16[128,128]{1,0:T(8,128)(2,1)S(1)} %slice.39), channel_id=1, source_target_pairs={{0,3},{1,2},{2,1},{3,0},{4,7},{5,6},{6,5},{7,4},{8,11},{9,10},{10,... | collective-permute-start | bytes 98312 | tf_op jit(solution)/shard_map/ppermute | solution.py:56
  16.8 0.2 collective-permute-done.3
  17.1 2.6 %collective-permute-start.4 = (bf16[128,128]{1,0:T(8,128)(2,1)S(1)}, bf16[128,128]{1,0:T(8,128)(2,1)S(1)}, u32[]{:S(2)}, u32[]{:S(2)}) collective-permute-start(bf16[128,128]{1,0:T(8,128)(2,1)S(1)} %add_convert_fusion.own_ref), channel_id=1, source_target_pairs={{0,9},{1,8},{2,11},{3,10},{4,13},{5,12},{6,15},{7,14},{8,1},{9,0},... | collective-permute-start | bytes 98312 | tf_op jit(solution)/shard_map/ppermute | solution.py:56
  19.7 0.0 collective-permute-done.6
  19.8 1.6 %collective-permute-start.7 = (bf16[64,128]{1,0:T(8,128)(2,1)S(1)}, bf16[64,128]{1,0:T(8,128)(2,1)S(1)}, u32[]{:S(2)}, u32[]{:S(2)}) collective-permute-start(bf16[64,128]{1,0:T(8,128)(2,1)S(1)} %slice.40), channel_id=1, source_target_pairs={{0,5},{1,4},{2,7},{3,6},{4,1},{5,0},{6,3},{7,2},{8,13},{9,12},{10,... | collective-permute-start | bytes 49160 | tf_op jit(solution)/shard_map/ppermute | solution.py:56
  21.3 0.0 collective-permute-done.4.got_ref
  21.4 0.8 %values.1 = (f32[64,128]{1,0:T(8,128)S(1)}, bf16[1,1088,128]{2,1,0:T(8,128)(2,1)S(1)}) custom-call(bf16[128,128]{1,0:T(8,128)(2,1)S(1)} %add_convert_fusion.own_ref, bf16[128,128]{1,0:T(8,128)(2,1)S(1)} %collective-permute-done.4.got_ref, bf16[2,256,1024]{2,1,0:T(8,128)(2,1)S(1)} %copy-done.1, s32[64,128]{1,0:T(8,128)S(1)} %get-tuple-element.42.refs_0_.idx_ref, ...), custom_call_target="tpu_custom_call" | custom-call | flops 1 | bytes 1 | tf_op jit(solution)/shard_map/values/pallas_call | solution.py:389
  22.2 1.8 %collective-permute-start.9 = (bf16[1088,128]{1,0:T(8,128)(2,1)S(1)}, bf16[1088,128]{1,0:T(8,128)(2,1)S(1)}, u32[]{:S(2)}, u32[]{:S(2)}) collective-permute-start(bf16[1088,128]{1,0:T(8,128)(2,1)S(1)} %bitcast.14), channel_id=1, source_target_pairs={{0,16},{1,17},{2,18},{3,19},{4,20},{5,21},{6,22},{7,23},{8,24},{9,... | collective-permute-start | bytes 835592 | tf_op jit(solution)/shard_map/ppermute | solution.py:56
  24.0 0.0 collective-permute-done.7
  24.0 2.2 %collective-permute-start.8 = (bf16[32,128]{1,0:T(8,128)(2,1)S(1)}, bf16[32,128]{1,0:T(8,128)(2,1)S(1)}, u32[]{:S(2)}, u32[]{:S(2)}) collective-permute-start(bf16[32,128]{1,0:T(8,128)(2,1)S(1)} %slice.41), channel_id=1, source_target_pairs={{0,9},{1,8},{2,11},{3,10},{4,13},{5,12},{6,15},{7,14},{8,1},{9,0},... | collective-permute-start | bytes 24584 | tf_op jit(solution)/shard_map/ppermute | solution.py:56
  26.2 1.8 %collective-permute-done.8 = bf16[32,128]{1,0:T(8,128)(2,1)S(1)} collective-permute-done((bf16[32,128]{1,0:T(8,128)(2,1)S(1)}, bf16[32,128]{1,0:T(8,128)(2,1)S(1)}, u32[]{:S(2)}, u32[]{:S(2)}) %collective-permute-start.8) | collective-permute-done | bytes 8224 | tf_op jit(solution)/shard_map/ppermute | solution.py:56
  28.1 0.7 %mine.1 = (f32[128,1024]{1,0:T(8,128)S(1)}, bf16[2,16,128]{2,1,0:T(8,128)(2,1)S(1)}) custom-call(f32[64,128]{1,0:T(8,128)S(1)} %get-tuple-element.49.value_ref, s32[64,128]{1,0:T(8,128)S(1)} %get-tuple-element.42.refs_0_.idx_ref, s32[256,128]{1,0:T(8,128)S(1)} %get-tuple-element.50.slot_ref, bf16[2,256,1024]{2,1,0:T(8,128)(2,1)S(1)} %copy-done.1, ...), custom_call_target="tpu_custom_call" | custom-call | flops 1 | bytes 1 | tf_op jit(solution)/shard_map/mine/pallas_call | solution.py:399
  28.7 0.6 %copy.8 = bf16[16,2,128]{2,1,0:T(2,128)(2,1)} copy(bf16[16,2,128]{2,0,1:T(8,128)(2,1)S(1)} %bitcast.18) | data formatting | bytes 16384
  29.3 1.9 %collective-permute-done.9 = bf16[1088,128]{1,0:T(8,128)(2,1)S(1)} collective-permute-done((bf16[1088,128]{1,0:T(8,128)(2,1)S(1)}, bf16[1088,128]{1,0:T(8,128)(2,1)S(1)}, u32[]{:S(2)}, u32[]{:S(2)}) %collective-permute-start.9) | collective-permute-done | bytes 278560 | tf_op jit(solution)/shard_map/ppermute | solution.py:56
  31.2 1.1 %final.1 = (f32[2,64,1024]{2,1,0:T(8,128)}, f32[64,128]{1,0:T(8,128)}) custom-call(f32[64,128]{1,0:T(8,128)S(1)} %get-tuple-element.54.old_ref, f32[128,1024]{1,0:T(8,128)S(1)} %get-tuple-element.55.mine_ref, bf16[1,1088,128]{2,1,0:T(8,128)(2,1)S(1)} %get-tuple-element.56.sent_ref, bf16[1,1088,128]{2,1,0:T(8,128)(2,1)S(1)} %bitcast.15), custom_call_target="tpu_custom_call" | custom-call | flops 1 | bytes 1 | tf_op jit(solution)/shard_map/final/pallas_call | solution.py:407
  (10 shorter events, 0.1 us)
Async XLA Ops:
  0.6 4.3 %copy-start.2 = (f32[1024,64]{0,1:T(8,128)S(1)}, f32[1024,64]{0,1:T(8,128)}, u32[]{:S(2)}) copy-start(f32[1024,64]{0,1:T(8,128)} %param.6) | copy-start | bytes 786436
  0.6 4.1 %copy-start.3 = (s32[128,64]{0,1:T(8,128)S(1)}, s32[128,64]{0,1:T(8,128)}, u32[]{:S(2)}) copy-start(s32[128,64]{0,1:T(8,128)} %param.7) | copy-start | bytes 98308
  0.7 4.1 %copy-start.4 = (s32[128,64]{0,1:T(8,128)S(1)}, s32[128,64]{0,1:T(8,128)}, u32[]{:S(2)}) copy-start(s32[128,64]{0,1:T(8,128)} %param.8) | copy-start | bytes 98308
  0.7 4.1 %copy-start.5 = (f32[128,64]{0,1:T(8,128)S(1)}, f32[128,64]{0,1:T(8,128)}, u32[]{:S(2)}) copy-start(f32[128,64]{0,1:T(8,128)} %param.9) | copy-start | bytes 98308
  1.7 6.5 %collective-permute-start = (bf16[64,1024]{1,0:T(8,128)(2,1)S(1)}, bf16[64,1024]{1,0:T(8,128)(2,1)S(1)}, u32[]{:S(2)}, u32[]{:S(2)}) collective-permute-start(bf16[64,1024]{1,0:T(8,128)(2,1)S(1)} %multiply_convert_fusion), channel_id=1, source_target_pairs={{0,16},{1,17},{2,18},{3,19},{4,20},{5,21},{6,22},{7,23},{8,24},{9,... | collective-permute-start | bytes 393224 | tf_op jit(solution)/shard_map/ppermute | solution.py:56
  5.0 1.2 %copy-start = (bf16[2,256,1024]{2,1,0:T(8,128)(2,1)S(1)}, bf16[2,256,1024]{2,1,0:T(8,128)(2,1)}, u32[]{:S(2)}) copy-start(bf16[2,256,1024]{2,1,0:T(8,128)(2,1)} %t_ref.7) | copy-start | bytes 3145732
  6.2 2.1 %copy-start.1 = (bf16[2,256,1024]{2,1,0:T(8,128)(2,1)S(1)}, bf16[2,256,1024]{2,1,0:T(8,128)(2,1)}, u32[]{:S(2)}) copy-start(bf16[2,256,1024]{2,1,0:T(8,128)(2,1)} %t_ref.7) | copy-start | bytes 3145732
  8.9 1.3 %collective-permute-start.1 = (f32[128,128]{1,0:T(8,128)S(1)}, f32[128,128]{1,0:T(8,128)S(1)}, u32[]{:S(2)}, u32[]{:S(2)}) collective-permute-start(f32[128,128]{1,0:T(8,128)S(1)} %get-tuple-element.35), channel_id=1, source_target_pairs={{0,1},{1,0},{2,3},{3,2},{4,5},{5,4},{6,7},{7,6},{8,9},{9,8},{10,11... | collective-permute-start | bytes 196616 | tf_op jit(solution)/shard_map/ppermute | solution.py:56
  10.2 3.4 %collective-permute-start.2 = (bf16[128,128]{1,0:T(8,128)(2,1)S(1)}, bf16[128,128]{1,0:T(8,128)(2,1)S(1)}, u32[]{:S(2)}, u32[]{:S(2)}) collective-permute-start(bf16[128,128]{1,0:T(8,128)(2,1)S(1)} %add.21), channel_id=1, source_target_pairs={{0,3},{1,2},{2,1},{3,0},{4,7},{5,6},{6,5},{7,4},{8,11},{9,10},{10,... | collective-permute-start | bytes 98312 | tf_op jit(solution)/shard_map/ppermute | solution.py:56
  11.8 3.5 %collective-permute-start.5 = (bf16[256,128]{1,0:T(8,128)(2,1)S(1)}, bf16[256,128]{1,0:T(8,128)(2,1)S(1)}, u32[]{:S(2)}, u32[]{:S(2)}) collective-permute-start(bf16[256,128]{1,0:T(8,128)(2,1)S(1)} %get-tuple-element.52), channel_id=1, source_target_pairs={{0,1},{1,0},{2,3},{3,2},{4,5},{5,4},{6,7},{7,6},{8,9},{9,8},{10,11... | collective-permute-start | bytes 196616 | tf_op jit(solution)/shard_map/ppermute | solution.py:56
  13.7 3.4 %collective-permute-start.3 = (bf16[128,128]{1,0:T(8,128)(2,1)S(1)}, bf16[128,128]{1,0:T(8,128)(2,1)S(1)}, u32[]{:S(2)}, u32[]{:S(2)}) collective-permute-start(bf16[128,128]{1,0:T(8,128)(2,1)S(1)} %convert_add_fusion.1), channel_id=1, source_target_pairs={{0,5},{1,4},{2,7},{3,6},{4,1},{5,0},{6,3},{7,2},{8,13},{9,12},{10,... | collective-permute-start | bytes 98312 | tf_op jit(solution)/shard_map/ppermute | solution.py:56
  15.3 4.4 %collective-permute-start.6 = (bf16[128,128]{1,0:T(8,128)(2,1)S(1)}, bf16[128,128]{1,0:T(8,128)(2,1)S(1)}, u32[]{:S(2)}, u32[]{:S(2)}) collective-permute-start(bf16[128,128]{1,0:T(8,128)(2,1)S(1)} %slice.39), channel_id=1, source_target_pairs={{0,3},{1,2},{2,1},{3,0},{4,7},{5,6},{6,5},{7,4},{8,11},{9,10},{10,... | collective-permute-start | bytes 98312 | tf_op jit(solution)/shard_map/ppermute | solution.py:56
  17.1 4.3 %collective-permute-start.4 = (bf16[128,128]{1,0:T(8,128)(2,1)S(1)}, bf16[128,128]{1,0:T(8,128)(2,1)S(1)}, u32[]{:S(2)}, u32[]{:S(2)}) collective-permute-start(bf16[128,128]{1,0:T(8,128)(2,1)S(1)} %add_convert_fusion.own_ref), channel_id=1, source_target_pairs={{0,9},{1,8},{2,11},{3,10},{4,13},{5,12},{6,15},{7,14},{8,1},{9,0},... | collective-permute-start | bytes 98312 | tf_op jit(solution)/shard_map/ppermute | solution.py:56
  19.8 4.2 %collective-permute-start.7 = (bf16[64,128]{1,0:T(8,128)(2,1)S(1)}, bf16[64,128]{1,0:T(8,128)(2,1)S(1)}, u32[]{:S(2)}, u32[]{:S(2)}) collective-permute-start(bf16[64,128]{1,0:T(8,128)(2,1)S(1)} %slice.40), channel_id=1, source_target_pairs={{0,5},{1,4},{2,7},{3,6},{4,1},{5,0},{6,3},{7,2},{8,13},{9,12},{10,... | collective-permute-start | bytes 49160 | tf_op jit(solution)/shard_map/ppermute | solution.py:56
  22.2 9.1 %collective-permute-start.9 = (bf16[1088,128]{1,0:T(8,128)(2,1)S(1)}, bf16[1088,128]{1,0:T(8,128)(2,1)S(1)}, u32[]{:S(2)}, u32[]{:S(2)}) collective-permute-start(bf16[1088,128]{1,0:T(8,128)(2,1)S(1)} %bitcast.14), channel_id=1, source_target_pairs={{0,16},{1,17},{2,18},{3,19},{4,20},{5,21},{6,22},{7,23},{8,24},{9,... | collective-permute-start | bytes 835592 | tf_op jit(solution)/shard_map/ppermute | solution.py:56
  24.0 4.0 %collective-permute-start.8 = (bf16[32,128]{1,0:T(8,128)(2,1)S(1)}, bf16[32,128]{1,0:T(8,128)(2,1)S(1)}, u32[]{:S(2)}, u32[]{:S(2)}) collective-permute-start(bf16[32,128]{1,0:T(8,128)(2,1)S(1)} %slice.41), channel_id=1, source_target_pairs={{0,9},{1,8},{2,11},{3,10},{4,13},{5,12},{6,15},{7,14},{8,1},{9,0},... | collective-permute-start | bytes 24584 | tf_op jit(solution)/shard_map/ppermute | solution.py:56

commit v3 on v2

--- a/solution.py
+++ b/solution.py
@@ -220,7 +220,7 @@
     )
 
 
-def values_kernel(per_row, own_ref, got_ref, t_ref, *refs):
+def values_kernel(per_row, trap_ref, t_ref, *refs):
     sets = (refs[0:3], refs[3:6])
     slot_ref, value_own_ref, away_ref, value_oth_ref, px_ref = refs[6:]
     rows, modes = t_ref.shape[1:]
@@ -231,7 +231,7 @@
         chunks = []
         for c in range(idx_ref.shape[1] // LANES):
             at = slice(part * traps, (part + 1) * traps)
-            chunks.append(own_ref[at, :].astype(F32) + got_ref[at, :].astype(F32))
+            chunks.append(trap_ref[at, :])
             part += 1
         v = chunks[0] if len(chunks) == 1 else jnp.concatenate(chunks, axis=1)
         within = (idx_ref[...] >= 0) & (idx_ref[...] < rows)
@@ -368,18 +368,20 @@
         **cost,
     )(other, index, transfer, own_out, own_trap)
 
-    total = trap
-    for k in range(steps):
-        trap = total if k == 0 else total.astype(BF)
-        got = swap_pairs(trap, masks[k])
-        total = trap.astype(F32) + got.astype(F32)
-        if k == 0:
-            total, now = lax.optimization_barrier((total, now))
-            slots = call(
-                functools.partial(slot_kernel, per_row), "slots", [((rows, wide), jnp.int32) for wide in sets], [VMEM], **cost
-            )(now)
-        if k == 1:
-            total, *slots = lax.optimization_barrier((total, *slots))
+    trap = trap + swap_pairs(trap, 1)
+    trap, now = lax.optimization_barrier((trap, now))
+    slots = call(
+        functools.partial(slot_kernel, per_row), "slots", [((rows, wide), jnp.int32) for wide in sets], [VMEM], **cost
+    )(now)
+    for group in (range(1, min(3, steps)), *[[b] for b in range(3, steps)]):
+        short = trap.astype(BF)
+        chips = [0]
+        for b in group:
+            chips += [m | 1 << b for m in chips]
+        got = [swap_pairs(short, m | 1) if m else short for m in chips]
+        trap = tree_sum([x.astype(F32) for x in got])
+        if group[0] == 1:
+            trap, *slots = lax.optimization_barrier((trap, *slots))
     for k in range(steps):
         block = keep + swap_pairs(send, masks[k]).astype(F32)
         half = block.shape[0] // 2
@@ -390,10 +392,10 @@
         functools.partial(values_kernel, per_row),
         "values",
         [((traps, wide_own), F32), ((n_rows - 1, n_away, LANES), BF)],
-        [VMEM] * 10,
+        [VMEM] * 9,
         scratch=[pltpu.VMEM((traps, wide_oth), F32), pltpu.VMEM((rows, wide_oth), F32)],
         **cost,
-    )(trap, got, transfer, *tables, slots[1])
+    )(trap, transfer, *tables, slots[1])
     back = [swap_pairs(away[m - 1], m * n_cols)[None] for m in range(1, n_rows)]
     back = back[0] if n_rows == 2 else jnp.concatenate(back, axis=0)
     mine, field = call(

time: 32.5 us -> 31.8 us (0.978)
  waiting for transfers between devices: 7.41 us -> 6.89 us
    ppermute x10 -> x11, waiting for transfers between devices: 7.41 us -> 6.89 us  [swap_pairs(): return lax.ppermute(x, AXES, [(i, i ^ mask) for i in range(n)])]
    ppermute x10 -> x11, starting transfers between devices: 16.4 us -> 16.2 us  [swap_pairs(): return lax.ppermute(x, AXES, [(i, i ^ mask) for i in range(n)])]
  transfers between devices with their start and end apart: 10 -> 11, of which waited for: 6 -> 7; matrix products, arithmetic and copies ran while one was open for 2% -> 2% of each run, Pallas kernels for 9% -> 10%
where the time goes in v3:
time: 31.8 us; the launch traced here: 31.6 us
  starting transfers between devices  16.2 us (51%)
  waiting for transfers between devices  6.89 us (22%)
  Pallas kernels  4.8 us (15%)
  local copies, waits for them, and re-layouts  1.86 us (6%)
  other arithmetic  1.13 us (4%)
  between operations  0.78 us (2%)
    ppermute x11, starting transfers between devices, swap_pairs(): return lax.ppermute(x, AXES, [(i, i ^ mask) for i in range(n)])  16.2 us
    ppermute x11, waiting for transfers between devices, swap_pairs(): return lax.ppermute(x, AXES, [(i, i ^ mask) for i in range(n)])  6.89 us
    unnamed x13, local copies, waits for them, and re-layouts  1.85 us
    pallas_call x1, Pallas kernels, body(): call(functools.partial(final_kernel, per_row), 'final', [((2, per_row, mo...  1.14 us
    convert_element_type x1, other arithmetic, body(): code = code.astype(BF)  1.06 us
    pallas_call x1, Pallas kernels, body(): call(functools.partial(slot_kernel, per_row), 'slots', [((rows, wide), jn...  0.88 us
    pallas_call x1, Pallas kernels, body(): call(functools.partial(values_kernel, per_row), 'values', [((traps, wide_...  0.79 us
    pallas_call x1, Pallas kernels, body(): call(functools.partial(mine_kernel, per_row), 'mine', [((2 * per_row, mod...  0.66 us
  transfers between devices with their start and end apart: 11, of which 7 were waited for; matrix products, arithmetic and copies ran while one was open for 2% of the time, Pallas kernels for 10%

profile of v3, /device:TPU:0, one launch (start us, length us, event | category | flops | bytes accessed | tf_op | source)
XLA Modules:
  0.0 31.6 jit_solution(9790151909762474953)
XLA Ops:
  0.6 0.0 copy-start.2
  0.6 0.0 copy-start.3
  0.7 0.0 copy-start.4
  0.7 0.0 copy-start.5
  0.7 1.1 %multiply_convert_fusion = bf16[64,1024]{1,0:T(8,128)(2,1)S(1)} fusion(f32[1024,64]{0,1:T(8,128)} %param.6), kind=kLoop, calls=%fused_computation | loop fusion | flops 393216 | bytes 393216 | tf_op jit(solution)/shard_map/convert_element_type | solution.py:335
  1.7 3.0 %collective-permute-start = (bf16[64,1024]{1,0:T(8,128)(2,1)S(1)}, bf16[64,1024]{1,0:T(8,128)(2,1)S(1)}, u32[]{:S(2)}, u32[]{:S(2)}) collective-permute-start(bf16[64,1024]{1,0:T(8,128)(2,1)S(1)} %multiply_convert_fusion), channel_id=1, source_target_pairs={{0,16},{1,17},{2,18},{3,19},{4,20},{5,21},{6,22},{7,23},{8,24},{9,... | collective-permute-start | bytes 393224 | tf_op jit(solution)/shard_map/ppermute | solution.py:56
  4.8 0.0 copy-done.3
  4.8 0.0 copy-done.4
  4.8 0.0 copy-done.5
  4.8 0.2 plan.1
  5.0 0.0 copy-done.2
  5.0 0.0 copy-start
  5.0 1.2 %copy-done = bf16[2,256,1024]{2,1,0:T(8,128)(2,1)S(1)} copy-done((bf16[2,256,1024]{2,1,0:T(8,128)(2,1)S(1)}, bf16[2,256,1024]{2,1,0:T(8,128)(2,1)}, u32[]{:S(2)}) %copy-start) | copy-done | bytes 1048600
  6.2 0.0 copy-start.1
  6.2 0.5 %own.1 = (f32[256,128]{1,0:T(8,128)S(1)}, f32[64,128]{1,0:T(8,128)S(1)}) custom-call(f32[64,1024]{1,0:T(8,128)S(1)} %bitcast.10, s32[64,128]{1,0:T(8,128)S(1)} %bitcast.12, bf16[2,256,1024]{2,1,0:T(8,128)(2,1)S(1)} %copy-done), custom_call_target="tpu_custom_call" | custom-call | flops 1 | bytes 1 | tf_op jit(solution)/shard_map/own/pallas_call | solution.py:353
  6.7 1.5 %collective-permute-done.code_ref = bf16[64,1024]{1,0:T(8,128)(2,1)S(1)} collective-permute-done((bf16[64,1024]{1,0:T(8,128)(2,1)S(1)}, bf16[64,1024]{1,0:T(8,128)(2,1)S(1)}, u32[]{:S(2)}, u32[]{:S(2)}) %collective-permute-start) | collective-permute-done | bytes 131104 | tf_op jit(solution)/shard_map/ppermute | solution.py:56
  8.3 0.0 copy-done.1
  8.3 0.6 %other.1 = (f32[128,128]{1,0:T(8,128)S(1)}, f32[256,128]{1,0:T(8,128)S(1)}, bf16[256,128]{1,0:T(8,128)(2,1)S(1)}) custom-call(bf16[64,1024]{1,0:T(8,128)(2,1)S(1)} %collective-permute-done.code_ref, s32[64,128]{1,0:T(8,128)S(1)} %bitcast.13, bf16[2,256,1024]{2,1,0:T(8,128)(2,1)S(1)} %copy-done.1, f32[256,128]{1,0:T(8,128)S(1)} %get-tuple-element.33.own_ref, ...), custom_call_target="tpu_custom_call" | custom-call | flops 1 | bytes 1 | tf_op jit(solution)/shard_map/other/pallas_call | solution.py:362
  8.9 0.1 collective-permute-start.1
  9.0 0.5 %collective-permute-start.6 = (bf16[256,128]{1,0:T(8,128)(2,1)S(1)}, bf16[256,128]{1,0:T(8,128)(2,1)S(1)}, u32[]{:S(2)}, u32[]{:S(2)}) collective-permute-start(bf16[256,128]{1,0:T(8,128)(2,1)S(1)} %get-tuple-element.52), channel_id=1, source_target_pairs={{0,1},{1,0},{2,3},{3,2},{4,5},{5,4},{6,7},{7,6},{8,9},{9,8},{10,11... | collective-permute-start | bytes 196616 | tf_op jit(solution)/shard_map/ppermute | solution.py:56
  9.5 0.7 %collective-permute-done.1 = f32[128,128]{1,0:T(8,128)S(1)} collective-permute-done((f32[128,128]{1,0:T(8,128)S(1)}, f32[128,128]{1,0:T(8,128)S(1)}, u32[]{:S(2)}, u32[]{:S(2)}) %collective-permute-start.1) | collective-permute-done | bytes 65568 | tf_op jit(solution)/shard_map/ppermute | solution.py:56
  10.2 2.6 %collective-permute-start.4 = (bf16[128,128]{1,0:T(8,128)(2,1)S(1)}, bf16[128,128]{1,0:T(8,128)(2,1)S(1)}, u32[]{:S(2)}, u32[]{:S(2)}) collective-permute-start(bf16[128,128]{1,0:T(8,128)(2,1)S(1)} %add.27), channel_id=1, source_target_pairs={{0,7},{1,6},{2,5},{3,4},{4,3},{5,2},{6,1},{7,0},{8,15},{9,14},{10,... | collective-permute-start | bytes 98312 | tf_op jit(solution)/shard_map/ppermute | solution.py:56
  12.8 0.4 %collective-permute-start.3 = (bf16[128,128]{1,0:T(8,128)(2,1)S(1)}, bf16[128,128]{1,0:T(8,128)(2,1)S(1)}, u32[]{:S(2)}, u32[]{:S(2)}) collective-permute-start(bf16[128,128]{1,0:T(8,128)(2,1)S(1)} %add.27), channel_id=1, source_target_pairs={{0,5},{1,4},{2,7},{3,6},{4,1},{5,0},{6,3},{7,2},{8,13},{9,12},{10,... | collective-permute-start | bytes 98312 | tf_op jit(solution)/shard_map/ppermute | solution.py:56
  13.2 0.2 collective-permute-start.2
  13.4 0.0 collective-permute-done.6
  13.4 0.9 %slots.1 = (s32[256,128]{1,0:T(8,128)S(1)}, s32[256,128]{1,0:T(8,128)S(1)}) custom-call(s32[64,128]{1,0:T(8,128)S(1)} %get-tuple-element.38.now_ref), custom_call_target="tpu_custom_call" | custom-call | flops 1 | bytes 1 | tf_op jit(solution)/shard_map/slots/pallas_call | solution.py:373
  14.3 1.6 %collective-permute-start.7 = (bf16[128,128]{1,0:T(8,128)(2,1)S(1)}, bf16[128,128]{1,0:T(8,128)(2,1)S(1)}, u32[]{:S(2)}, u32[]{:S(2)}) collective-permute-start(bf16[128,128]{1,0:T(8,128)(2,1)S(1)} %slice.39), channel_id=1, source_target_pairs={{0,3},{1,2},{2,1},{3,0},{4,7},{5,6},{6,5},{7,4},{8,11},{9,10},{10,... | collective-permute-start | bytes 98312 | tf_op jit(solution)/shard_map/ppermute | solution.py:56
  15.9 0.0 collective-permute-done.4
  15.9 0.2 collective-permute-done.3
  16.1 0.4 %collective-permute-done.2 = bf16[128,128]{1,0:T(8,128)(2,1)S(1)} collective-permute-done((bf16[128,128]{1,0:T(8,128)(2,1)S(1)}, bf16[128,128]{1,0:T(8,128)(2,1)S(1)}, u32[]{:S(2)}, u32[]{:S(2)}) %collective-permute-start.2) | collective-permute-done | bytes 32800 | tf_op jit(solution)/shard_map/ppermute | solution.py:56
  16.6 2.4 %collective-permute-start.5 = (bf16[128,128]{1,0:T(8,128)(2,1)S(1)}, bf16[128,128]{1,0:T(8,128)(2,1)S(1)}, u32[]{:S(2)}, u32[]{:S(2)}) collective-permute-start(bf16[128,128]{1,0:T(8,128)(2,1)S(1)} %add_add_fusion), channel_id=1, source_target_pairs={{0,9},{1,8},{2,11},{3,10},{4,13},{5,12},{6,15},{7,14},{8,1},{9,0},... | collective-permute-start | bytes 98312 | tf_op jit(solution)/shard_map/ppermute | solution.py:56
  19.0 0.0 collective-permute-done.7
  19.0 1.6 %collective-permute-start.8 = (bf16[64,128]{1,0:T(8,128)(2,1)S(1)}, bf16[64,128]{1,0:T(8,128)(2,1)S(1)}, u32[]{:S(2)}, u32[]{:S(2)}) collective-permute-start(bf16[64,128]{1,0:T(8,128)(2,1)S(1)} %slice.40), channel_id=1, source_target_pairs={{0,5},{1,4},{2,7},{3,6},{4,1},{5,0},{6,3},{7,2},{8,13},{9,12},{10,... | collective-permute-start | bytes 49160 | tf_op jit(solution)/shard_map/ppermute | solution.py:56
  20.6 0.3 collective-permute-done.5
  20.9 0.8 %values.1 = (f32[64,128]{1,0:T(8,128)S(1)}, bf16[1,1088,128]{2,1,0:T(8,128)(2,1)S(1)}) custom-call(f32[128,128]{1,0:T(8,128)S(1)} %convert_add_fusion.1.trap_ref, bf16[2,256,1024]{2,1,0:T(8,128)(2,1)S(1)} %copy-done.1, s32[64,128]{1,0:T(8,128)S(1)} %get-tuple-element.42.refs_0_.idx_ref, f32[64,128]{1,0:T(8,128)S(1)} %get-tuple-element.43.refs_1_, ...), custom_call_target="tpu_custom_call" | custom-call | flops 1 | bytes 1 | tf_op jit(solution)/shard_map/values/pallas_call | solution.py:391
  21.7 1.6 %collective-permute-start.10 = (bf16[1088,128]{1,0:T(8,128)(2,1)S(1)}, bf16[1088,128]{1,0:T(8,128)(2,1)S(1)}, u32[]{:S(2)}, u32[]{:S(2)}) collective-permute-start(bf16[1088,128]{1,0:T(8,128)(2,1)S(1)} %bitcast.14), channel_id=1, source_target_pairs={{0,16},{1,17},{2,18},{3,19},{4,20},{5,21},{6,22},{7,23},{8,24},{9,... | collective-permute-start | bytes 835592 | tf_op jit(solution)/shard_map/ppermute | solution.py:56
  23.3 0.0 collective-permute-done.8
  23.3 2.2 %collective-permute-start.9 = (bf16[32,128]{1,0:T(8,128)(2,1)S(1)}, bf16[32,128]{1,0:T(8,128)(2,1)S(1)}, u32[]{:S(2)}, u32[]{:S(2)}) collective-permute-start(bf16[32,128]{1,0:T(8,128)(2,1)S(1)} %slice.41), channel_id=1, source_target_pairs={{0,9},{1,8},{2,11},{3,10},{4,13},{5,12},{6,15},{7,14},{8,1},{9,0},... | collective-permute-start | bytes 24584 | tf_op jit(solution)/shard_map/ppermute | solution.py:56
  25.5 1.8 %collective-permute-done.9 = bf16[32,128]{1,0:T(8,128)(2,1)S(1)} collective-permute-done((bf16[32,128]{1,0:T(8,128)(2,1)S(1)}, bf16[32,128]{1,0:T(8,128)(2,1)S(1)}, u32[]{:S(2)}, u32[]{:S(2)}) %collective-permute-start.9) | collective-permute-done | bytes 8224 | tf_op jit(solution)/shard_map/ppermute | solution.py:56
  27.3 0.7 %mine.1 = (f32[128,1024]{1,0:T(8,128)S(1)}, bf16[2,16,128]{2,1,0:T(8,128)(2,1)S(1)}) custom-call(f32[64,128]{1,0:T(8,128)S(1)} %get-tuple-element.49.value_ref, s32[64,128]{1,0:T(8,128)S(1)} %get-tuple-element.42.refs_0_.idx_ref, s32[256,128]{1,0:T(8,128)S(1)} %get-tuple-element.50.slot_ref, bf16[2,256,1024]{2,1,0:T(8,128)(2,1)S(1)} %copy-done.1, ...), custom_call_target="tpu_custom_call" | custom-call | flops 1 | bytes 1 | tf_op jit(solution)/shard_map/mine/pallas_call | solution.py:401
  28.0 0.6 %copy.8 = bf16[16,2,128]{2,1,0:T(2,128)(2,1)} copy(bf16[16,2,128]{2,0,1:T(8,128)(2,1)S(1)} %bitcast.18) | data formatting | bytes 16384
  28.6 1.9 %collective-permute-done.10 = bf16[1088,128]{1,0:T(8,128)(2,1)S(1)} collective-permute-done((bf16[1088,128]{1,0:T(8,128)(2,1)S(1)}, bf16[1088,128]{1,0:T(8,128)(2,1)S(1)}, u32[]{:S(2)}, u32[]{:S(2)}) %collective-permute-start.10) | collective-permute-done | bytes 278560 | tf_op jit(solution)/shard_map/ppermute | solution.py:56
  30.5 1.1 %final.1 = (f32[2,64,1024]{2,1,0:T(8,128)}, f32[64,128]{1,0:T(8,128)}) custom-call(f32[64,128]{1,0:T(8,128)S(1)} %get-tuple-element.54.old_ref, f32[128,1024]{1,0:T(8,128)S(1)} %get-tuple-element.55.mine_ref, bf16[1,1088,128]{2,1,0:T(8,128)(2,1)S(1)} %get-tuple-element.56.sent_ref, bf16[1,1088,128]{2,1,0:T(8,128)(2,1)S(1)} %bitcast.15), custom_call_target="tpu_custom_call" | custom-call | flops 1 | bytes 1 | tf_op jit(solution)/shard_map/final/pallas_call | solution.py:409
  (10 shorter events, 0.1 us)
Async XLA Ops:
  0.6 4.3 %copy-start.2 = (f32[1024,64]{0,1:T(8,128)S(1)}, f32[1024,64]{0,1:T(8,128)}, u32[]{:S(2)}) copy-start(f32[1024,64]{0,1:T(8,128)} %param.6) | copy-start | bytes 786436
  0.6 4.1 %copy-start.3 = (s32[128,64]{0,1:T(8,128)S(1)}, s32[128,64]{0,1:T(8,128)}, u32[]{:S(2)}) copy-start(s32[128,64]{0,1:T(8,128)} %param.7) | copy-start | bytes 98308
  0.7 4.1 %copy-start.4 = (s32[128,64]{0,1:T(8,128)S(1)}, s32[128,64]{0,1:T(8,128)}, u32[]{:S(2)}) copy-start(s32[128,64]{0,1:T(8,128)} %param.8) | copy-start | bytes 98308
  0.7 4.1 %copy-start.5 = (f32[128,64]{0,1:T(8,128)S(1)}, f32[128,64]{0,1:T(8,128)}, u32[]{:S(2)}) copy-start(f32[128,64]{0,1:T(8,128)} %param.9) | copy-start | bytes 98308
  1.7 6.5 %collective-permute-start = (bf16[64,1024]{1,0:T(8,128)(2,1)S(1)}, bf16[64,1024]{1,0:T(8,128)(2,1)S(1)}, u32[]{:S(2)}, u32[]{:S(2)}) collective-permute-start(bf16[64,1024]{1,0:T(8,128)(2,1)S(1)} %multiply_convert_fusion), channel_id=1, source_target_pairs={{0,16},{1,17},{2,18},{3,19},{4,20},{5,21},{6,22},{7,23},{8,24},{9,... | collective-permute-start | bytes 393224 | tf_op jit(solution)/shard_map/ppermute | solution.py:56
  5.0 1.2 %copy-start = (bf16[2,256,1024]{2,1,0:T(8,128)(2,1)S(1)}, bf16[2,256,1024]{2,1,0:T(8,128)(2,1)}, u32[]{:S(2)}) copy-start(bf16[2,256,1024]{2,1,0:T(8,128)(2,1)} %t_ref.7) | copy-start | bytes 3145732
  6.2 2.1 %copy-start.1 = (bf16[2,256,1024]{2,1,0:T(8,128)(2,1)S(1)}, bf16[2,256,1024]{2,1,0:T(8,128)(2,1)}, u32[]{:S(2)}) copy-start(bf16[2,256,1024]{2,1,0:T(8,128)(2,1)} %t_ref.7) | copy-start | bytes 3145732
  8.9 1.3 %collective-permute-start.1 = (f32[128,128]{1,0:T(8,128)S(1)}, f32[128,128]{1,0:T(8,128)S(1)}, u32[]{:S(2)}, u32[]{:S(2)}) collective-permute-start(f32[128,128]{1,0:T(8,128)S(1)} %get-tuple-element.35), channel_id=1, source_target_pairs={{0,1},{1,0},{2,3},{3,2},{4,5},{5,4},{6,7},{7,6},{8,9},{9,8},{10,11... | collective-permute-start | bytes 196616 | tf_op jit(solution)/shard_map/ppermute | solution.py:56
  9.0 4.4 %collective-permute-start.6 = (bf16[256,128]{1,0:T(8,128)(2,1)S(1)}, bf16[256,128]{1,0:T(8,128)(2,1)S(1)}, u32[]{:S(2)}, u32[]{:S(2)}) collective-permute-start(bf16[256,128]{1,0:T(8,128)(2,1)S(1)} %get-tuple-element.52), channel_id=1, source_target_pairs={{0,1},{1,0},{2,3},{3,2},{4,5},{5,4},{6,7},{7,6},{8,9},{9,8},{10,11... | collective-permute-start | bytes 196616 | tf_op jit(solution)/shard_map/ppermute | solution.py:56
  10.2 5.7 %collective-permute-start.4 = (bf16[128,128]{1,0:T(8,128)(2,1)S(1)}, bf16[128,128]{1,0:T(8,128)(2,1)S(1)}, u32[]{:S(2)}, u32[]{:S(2)}) collective-permute-start(bf16[128,128]{1,0:T(8,128)(2,1)S(1)} %add.27), channel_id=1, source_target_pairs={{0,7},{1,6},{2,5},{3,4},{4,3},{5,2},{6,1},{7,0},{8,15},{9,14},{10,... | collective-permute-start | bytes 98312 | tf_op jit(solution)/shard_map/ppermute | solution.py:56
  12.8 3.3 %collective-permute-start.3 = (bf16[128,128]{1,0:T(8,128)(2,1)S(1)}, bf16[128,128]{1,0:T(8,128)(2,1)S(1)}, u32[]{:S(2)}, u32[]{:S(2)}) collective-permute-start(bf16[128,128]{1,0:T(8,128)(2,1)S(1)} %add.27), channel_id=1, source_target_pairs={{0,5},{1,4},{2,7},{3,6},{4,1},{5,0},{6,3},{7,2},{8,13},{9,12},{10,... | collective-permute-start | bytes 98312 | tf_op jit(solution)/shard_map/ppermute | solution.py:56
  13.2 3.4 %collective-permute-start.2 = (bf16[128,128]{1,0:T(8,128)(2,1)S(1)}, bf16[128,128]{1,0:T(8,128)(2,1)S(1)}, u32[]{:S(2)}, u32[]{:S(2)}) collective-permute-start(bf16[128,128]{1,0:T(8,128)(2,1)S(1)} %add.27), channel_id=1, source_target_pairs={{0,3},{1,2},{2,1},{3,0},{4,7},{5,6},{6,5},{7,4},{8,11},{9,10},{10,... | collective-permute-start | bytes 98312 | tf_op jit(solution)/shard_map/ppermute | solution.py:56
  14.3 4.7 %collective-permute-start.7 = (bf16[128,128]{1,0:T(8,128)(2,1)S(1)}, bf16[128,128]{1,0:T(8,128)(2,1)S(1)}, u32[]{:S(2)}, u32[]{:S(2)}) collective-permute-start(bf16[128,128]{1,0:T(8,128)(2,1)S(1)} %slice.39), channel_id=1, source_target_pairs={{0,3},{1,2},{2,1},{3,0},{4,7},{5,6},{6,5},{7,4},{8,11},{9,10},{10,... | collective-permute-start | bytes 98312 | tf_op jit(solution)/shard_map/ppermute | solution.py:56
  16.6 4.3 %collective-permute-start.5 = (bf16[128,128]{1,0:T(8,128)(2,1)S(1)}, bf16[128,128]{1,0:T(8,128)(2,1)S(1)}, u32[]{:S(2)}, u32[]{:S(2)}) collective-permute-start(bf16[128,128]{1,0:T(8,128)(2,1)S(1)} %add_add_fusion), channel_id=1, source_target_pairs={{0,9},{1,8},{2,11},{3,10},{4,13},{5,12},{6,15},{7,14},{8,1},{9,0},... | collective-permute-start | bytes 98312 | tf_op jit(solution)/shard_map/ppermute | solution.py:56
  19.0 4.3 %collective-permute-start.8 = (bf16[64,128]{1,0:T(8,128)(2,1)S(1)}, bf16[64,128]{1,0:T(8,128)(2,1)S(1)}, u32[]{:S(2)}, u32[]{:S(2)}) collective-permute-start(bf16[64,128]{1,0:T(8,128)(2,1)S(1)} %slice.40), channel_id=1, source_target_pairs={{0,5},{1,4},{2,7},{3,6},{4,1},{5,0},{6,3},{7,2},{8,13},{9,12},{10,... | collective-permute-start | bytes 49160 | tf_op jit(solution)/shard_map/ppermute | solution.py:56
  21.7 8.8 %collective-permute-start.10 = (bf16[1088,128]{1,0:T(8,128)(2,1)S(1)}, bf16[1088,128]{1,0:T(8,128)(2,1)S(1)}, u32[]{:S(2)}, u32[]{:S(2)}) collective-permute-start(bf16[1088,128]{1,0:T(8,128)(2,1)S(1)} %bitcast.14), channel_id=1, source_target_pairs={{0,16},{1,17},{2,18},{3,19},{4,20},{5,21},{6,22},{7,23},{8,24},{9,... | collective-permute-start | bytes 835592 | tf_op jit(solution)/shard_map/ppermute | solution.py:56
  23.3 4.0 %collective-permute-start.9 = (bf16[32,128]{1,0:T(8,128)(2,1)S(1)}, bf16[32,128]{1,0:T(8,128)(2,1)S(1)}, u32[]{:S(2)}, u32[]{:S(2)}) collective-permute-start(bf16[32,128]{1,0:T(8,128)(2,1)S(1)} %slice.41), channel_id=1, source_target_pairs={{0,9},{1,8},{2,11},{3,10},{4,13},{5,12},{6,15},{7,14},{8,1},{9,0},... | collective-permute-start | bytes 24584 | tf_op jit(solution)/shard_map/ppermute | solution.py:56

commit v4 on v3

--- a/solution.py
+++ b/solution.py
@@ -18,6 +18,7 @@
 COS = (0.999999989217114, -0.49999989221470714, 0.041666490704389186, -0.0013887810304225767, 2.4770020037729276e-05,
        -2.708030902998698e-07, 1.7249574387300172e-09)
 STEEP = 25.0
+CROSS = 6
 NT = (((1,), (1,)), ((), ()))
 NN = (((1,), (0,)), ((), ()))
 VMEM = pl.BlockSpec(memory_space=pltpu.VMEM)
@@ -163,6 +164,9 @@
     mine = relative(index_ref[...], row, per_row) - row * rows
     now_ref[...] = mine
     refs[0][...] = old
+    theirs = mine + (2 * row - 1) * rows
+    refs[-2][...] = theirs
+    refs[-1][...] = spread(theirs, 0, per_row)
     inverse = 1.0 / target
     numer = old * (target * target)
     for s, (base, n) in enumerate(((0, per_row), (per_row, count - per_row))):
@@ -172,7 +176,7 @@
         num_ref[...] = spread(numer, base, n)
 
 
-def slot_kernel(per_row, now_ref, *slot_refs):
+def slot_kernel(sets, now_ref, *slot_refs):
     traps, count = now_ref.shape
     group = 8
 
@@ -185,7 +189,7 @@
             for i in range(group):
                 acc[i] = jnp.where(ind == pixels[i], k, acc[i])
         for i in range(group):
-            for ref, (base, n) in zip(slot_refs, ((0, per_row), (per_row, count - per_row))):
+            for ref, (base, n) in zip(slot_refs, sets):
                 ref[pl.ds(start + 8 * i, 8), :] = spread(acc[i], base, n)
         return carry
 
@@ -209,18 +213,18 @@
         for g in range(traps // 8):
             got = jnp.where(high == g, jnp.take_along_axis(acc[g], low, axis=0), got)
         px_ref[h * 8:(h + 1) * 8, :] = got
-    proj = px_ref[...].T.astype(BF)
+    proj = px_ref[...].astype(BF).T
     turned = [proj[n:2 * n], -proj[:n]] + ([proj[2 * n:]] if lanes > 2 * n else [])
     return proj, jnp.concatenate(turned, axis=0)
 
 
-def back_through(pair, t_ref):
-    return lax.dot_general(pair[0], t_ref[0], NN, preferred_element_type=F32) + lax.dot_general(
-        pair[1], t_ref[1], NN, preferred_element_type=F32
+def back_through(pair, t_ref, first, last):
+    return lax.dot_general(pair[0], t_ref[0, :, first:last], NN, preferred_element_type=F32) + lax.dot_general(
+        pair[1], t_ref[1, :, first:last], NN, preferred_element_type=F32
     )
 
 
-def values_kernel(per_row, trap_ref, t_ref, *refs):
+def values_kernel(per_row, crossing, trap_ref, t_ref, *refs):
     sets = (refs[0:3], refs[3:6])
     slot_ref, value_own_ref, away_ref, value_oth_ref, px_ref = refs[6:]
     rows, modes = t_ref.shape[1:]
@@ -242,11 +246,14 @@
     own_lanes = lane_of(ratios[0][:, :LANES]) < per_row
     q = jnp.where(own_lanes, ratios[0][:, :LANES], turn(ratios[1][:, :LANES], -per_row)).astype(BF)
     n = LANES - per_row
-    back = back_through(scatter(sets[1][0], value_oth_ref, slot_ref, px_ref, n), t_ref)
+    back = back_through(scatter(sets[1][0], value_oth_ref, slot_ref, px_ref, n), t_ref, crossing, modes)
     for j in range(n // per_row):
         away_ref[j, :traps, :] = q
         at = traps
-        for w in range(modes // LANES):
+        if crossing:
+            away_ref[j, at:at + traps, :] = value_oth_ref[...].astype(BF)
+            at += traps
+        for w in range((modes - crossing) // LANES):
             lanes = slice(w * LANES, (w + 1) * LANES)
             away_ref[j, at:at + per_row, :] = back[j * per_row:(j + 1) * per_row, lanes].astype(BF)
             at += per_row
@@ -254,7 +261,7 @@
             at += per_row
 
 
-def mine_kernel(per_row, value_ref, idx_ref, slot_ref, t_ref, far_ref, mine_ref, field_ref, px_ref):
+def far_kernel(per_row, far_ref, field_ref):
     px = field_ref.shape[1]
     own = far_ref[:px, :]
     others = [far_ref[at:at + px, :] for at in range(px, far_ref.shape[0], px)]
@@ -265,11 +272,15 @@
         theirs = turn(turn(others, part * n)[:, :LANES], -per_row)
         both = jnp.where(first, turn(own, part * per_row), theirs)
         field_ref[part] = relative(both, lax.axis_index("row"), per_row).astype(BF)
+
+
+def mine_kernel(per_row, value_ref, idx_ref, slot_ref, t_ref, mine_ref, px_ref):
     pair = scatter(idx_ref, value_ref, slot_ref, px_ref, per_row)
-    mine_ref[...] = back_through(pair, t_ref)[:2 * per_row]
-
-
-def final_kernel(per_row, old_ref, mine_ref, sent_ref, got_ref, slm_ref, weights_ref, out_ref, scaled_ref, sems):
+    mine_ref[...] = back_through(pair, t_ref, 0, t_ref.shape[2])[:2 * per_row]
+
+
+def final_kernel(per_row, crossing, old_ref, mine_ref, sent_ref, got_ref, *refs):
+    slm_ref, weights_ref, out_ref, scaled_ref, sems = refs[3:8] if crossing else refs
     traps, count = old_ref.shape
     n_rows = count // per_row
     modes = mine_ref.shape[1]
@@ -282,20 +293,25 @@
         q.append(x)
     q = tree_sum(q)
     mean = jnp.sum(q, axis=0, keepdims=True) / TRAPS
-    scaled_ref[...] = relative(old_ref[...] * mean / q, lax.axis_index("row"), per_row)
-    copies = [pltpu.make_async_copy(scaled_ref, weights_ref, sems.at[0])]
-    copies[0].start()
+    copies = []
     scale = jnp.broadcast_to(mean, (count, count)).T[:per_row, 0:1]
     scale = scale * jnp.sqrt(jnp.float32(MODES) / jnp.float32(TRAPS))
     at = traps
+    across = []
+    if crossing:
+        idx_ref, slot_ref, t_ref = refs[:3]
+        px_ref, value_ref = refs[8:]
+        value_ref[...] = got_ref[0, at:at + traps, :].astype(F32)
+        at += traps
+        across = [back_through(scatter(idx_ref, value_ref, slot_ref, px_ref, per_row), t_ref, 0, crossing)]
     step = 16
     for i in range(per_row // step):
         halves = []
         for part in range(2):
             first = part * per_row + i * step
             total = mine_ref[first:first + step, :]
-            theirs = []
-            for w in range(modes // LANES):
+            theirs = [x[first:first + step] for x in across]
+            for w in range((modes - crossing) // LANES):
                 piece = 0.0
                 for m in range(n_rows - 1):
                     piece = piece + got_ref[m, at + 2 * w * per_row + first:at + 2 * w * per_row + first + step, :].astype(F32)
@@ -308,6 +324,10 @@
         piece = pl.ds(i * step, step)
         copies.append(pltpu.make_async_copy(out_ref.at[:, piece, :], slm_ref.at[:, piece, :], sems.at[i + 1]))
         copies[-1].start()
+        if i == 0:
+            scaled_ref[...] = relative(old_ref[...] * mean / q, lax.axis_index("row"), per_row)
+            copies.append(pltpu.make_async_copy(scaled_ref, weights_ref, sems.at[0]))
+            copies[-1].start()
     for copy in copies:
         copy.wait()
 
@@ -330,6 +350,7 @@
         order.append(j)
     wide_own, wide_oth = padded(per_row), padded(count - per_row)
     parts = (wide_own + wide_oth) // LANES
+    crossing = modes * CROSS // 8 // LANES * LANES if n_rows == 2 else 0
     phase_t = phase.T
     code = jnp.where(phase_t < 0, -1.0, 1.0) * jnp.exp(STEEP * jnp.abs(phase_t))
     code = code.astype(BF)
@@ -340,15 +361,18 @@
     index, target, old = trap_index.T, levels.T, weights_old.T
     any_space = pl.BlockSpec(memory_space=pl.ANY)
     sets = (wide_own, wide_oth)
-    now, old, *tables = call(
+    now, old, *tables, now_cross, idx_cross = call(
         functools.partial(plan_kernel, per_row, rows),
         "plan",
         [((traps, count), jnp.int32), ((traps, count), F32)]
-        + [((traps, wide), d) for wide in sets for d in (jnp.int32, F32, F32)],
+        + [((traps, wide), d) for wide in sets for d in (jnp.int32, F32, F32)]
+        + [((traps, count), jnp.int32), ((traps, wide_own), jnp.int32)],
         [VMEM] * 3,
         **cost,
     )(index, target, old)
 
+    if crossing:
+        t_across = swap_pairs(transfer[:, :, :crossing], n_cols)
     other, now = lax.optimization_barrier((other, now))
     own_out, own_trap = call(
         own_kernel,
@@ -365,31 +389,60 @@
         [((n_trap, LANES), F32), ((n_half, LANES), F32), ((n_half, LANES), BF)],
         [VMEM] * 5,
         scratch=[pltpu.VMEM((rows, wide_oth), F32)],
-        **cost,
+        flops=3 * 10**10,
+        size=1,
     )(other, index, transfer, own_out, own_trap)
 
-    trap = trap + swap_pairs(trap, 1)
-    trap, now = lax.optimization_barrier((trap, now))
-    slots = call(
-        functools.partial(slot_kernel, per_row), "slots", [((rows, wide), jnp.int32) for wide in sets], [VMEM], **cost
-    )(now)
-    for group in (range(1, min(3, steps)), *[[b] for b in range(3, steps)]):
-        short = trap.astype(BF)
-        chips = [0]
-        for b in group:
-            chips += [m | 1 << b for m in chips]
-        got = [swap_pairs(short, m | 1) if m else short for m in chips]
-        trap = tree_sum([x.astype(F32) for x in got])
-        if group[0] == 1:
-            trap, *slots = lax.optimization_barrier((trap, *slots))
-    for k in range(steps):
-        block = keep + swap_pairs(send, masks[k]).astype(F32)
-        half = block.shape[0] // 2
-        keep, send = block[:half], block[half:].astype(BF)
-
-    n_away = traps + 2 * per_row * modes // LANES
+    own_set, oth_set = (0, per_row), (per_row, count - per_row)
+
+    def plan_slots(now, *which):
+        return call(
+            functools.partial(slot_kernel, which),
+            "slots",
+            [((rows, padded(n)), jnp.int32) for _, n in which],
+            [VMEM],
+            **cost,
+        )(now)
+
+    groups = [list(range(1, min(3, steps)))] + [[b] for b in range(3, steps)]
+
+    def sums(trap, keep, send, now):
+        block = keep + swap_pairs(send, masks[0]).astype(F32)
+        trap = trap + swap_pairs(trap, masks[0])
+        trap, now = lax.optimization_barrier((trap, now))
+        slots = plan_slots(now, own_set, oth_set)
+        for group in groups:
+            short = trap.astype(BF)
+            ways = 1 << len(group)
+            part = block.shape[0] // ways
+            whole = block
+            fields, traps_of = [whole[:part]], [short]
+            for way in range(1, ways):
+                mask = 0
+                for i, b in enumerate(group):
+                    if (way >> (len(group) - 1 - i)) & 1:
+                        mask ^= masks[b]
+                load = jnp.concatenate([short, whole[way * part:(way + 1) * part].astype(BF)], axis=0)
+                got = swap_pairs(load, mask)
+                traps_of.append(got[:short.shape[0]])
+                fields.append(got[short.shape[0]:])
+            trap = tree_sum([x.astype(F32) for x in traps_of])
+            block = tree_sum([x.astype(F32) for x in fields])
+            if group[0] == 1:
+                trap, *slots = lax.optimization_barrier((trap, *slots))
+        return (trap, block, *slots)
+
+    if crossing:
+        shapes = jax.eval_shape(sums, trap, keep, send, now)
+        trap, block, *slots = lax.cond(
+            trap_index[0, 0] >= 0, sums, lambda *args: tuple(jnp.zeros(x.shape, x.dtype) for x in shapes), trap, keep, send, now
+        )
+    else:
+        trap, block, *slots = sums(trap, keep, send, now)
+
+    n_away = traps * (2 if crossing else 1) + 2 * per_row * (modes - crossing) // LANES
     value_own, away = call(
-        functools.partial(values_kernel, per_row),
+        functools.partial(values_kernel, per_row, crossing),
         "values",
         [((traps, wide_own), F32), ((n_rows - 1, n_away, LANES), BF)],
         [VMEM] * 9,
@@ -398,27 +451,34 @@
     )(trap, transfer, *tables, slots[1])
     back = [swap_pairs(away[m - 1], m * n_cols)[None] for m in range(1, n_rows)]
     back = back[0] if n_rows == 2 else jnp.concatenate(back, axis=0)
-    mine, field = call(
+    (field,) = call(functools.partial(far_kernel, per_row), "far", [((2, px, count), BF)], [VMEM], **cost)(block)
+    (mine,) = call(
         functools.partial(mine_kernel, per_row),
         "mine",
-        [((2 * per_row, modes), F32), ((2, px, count), BF)],
-        [VMEM] * 5,
+        [((2 * per_row, modes), F32)],
+        [VMEM] * 4,
         scratch=[pltpu.VMEM((rows, wide_own), F32)],
         **cost,
-    )(value_own, tables[0], slots[0], transfer, block)
+    )(value_own, tables[0], slots[0], transfer)
+    if crossing:
+        mine, now_cross = lax.optimization_barrier((mine, now_cross))
+        (slots_cross,) = plan_slots(now_cross, own_set)
+    extra = [idx_cross, slots_cross, t_across] if crossing else []
+    room = [pltpu.VMEM((rows, wide_own), F32), pltpu.VMEM((traps, wide_own), F32)] if crossing else []
     slm, weights = call(
-        functools.partial(final_kernel, per_row),
+        functools.partial(final_kernel, per_row, crossing),
         "final",
         [((2, per_row, modes), F32), ((traps, count), F32)],
-        [VMEM] * 4,
+        [VMEM] * (4 + len(extra)),
         out_specs=[any_space, any_space],
         scratch=[
             pltpu.VMEM((2, per_row, modes), F32),
             pltpu.VMEM((traps, count), F32),
             pltpu.SemaphoreType.DMA((1 + per_row // 16,)),
-        ],
+        ]
+        + room,
         **cost,
-    )(old, mine, away, back)
+    )(old, mine, away, back, *extra)
 
     return jnp.transpose(field, (1, 0, 2)), weights.T, jnp.transpose(slm, (2, 0, 1))
 

time: 31.8 us -> 31.3 us (0.984)
  starting transfers between devices: 16.2 us -> 11.6 us
  Pallas kernels: 4.8 us -> 6.08 us
  waiting for transfers between devices: 6.89 us -> 8.11 us
  local copies, waits for them, and re-layouts: 1.86 us -> 2.55 us
  between operations: 0.78 us -> 1.4 us
    ppermute x11 -> x9, starting transfers between devices: 16.2 us -> 11.6 us  [swap_pairs(): return lax.ppermute(x, AXES, [(i, i ^ mask) for i in range(n)])]
    slice x3 -> x4, local copies, waits for them, and re-layouts: 0.02 us -> 1.71 us  [the longest x1 1.18 us: body(): t_across = swap_pairs(transfer[:, :, :crossing], n_cols)]
    pallas_call x3 -> x5, Pallas kernels: 2.81 us -> 4.11 us  [the longest x2 1.76 us: plan_slots(): call(functools.partial(slot_kernel, which), 'slots', [((rows, padded(n)),...]
    ppermute x11 -> x9, waiting for transfers between devices: 6.89 us -> 8.11 us  [swap_pairs(): return lax.ppermute(x, AXES, [(i, i ^ mask) for i in range(n)])]
    unnamed x13 -> x11, local copies, waits for them, and re-layouts: 1.85 us -> 0.85 us
  transfers between devices with their start and end apart: 11 -> 9, of which waited for: 7 -> 7; matrix products, arithmetic and copies ran while one was open for 2% -> 8% of each run, Pallas kernels for 10% -> 15%
where the time goes in v4:
time: 31.3 us; the launch traced here: 31.1 us
  starting transfers between devices  11.6 us (37%)
  waiting for transfers between devices  8.11 us (26%)
  Pallas kernels  6.08 us (19%)
  local copies, waits for them, and re-layouts  2.55 us (8%)
  between operations  1.4 us (4%)
  other arithmetic  1.21 us (4%)
    ppermute x9, starting transfers between devices, swap_pairs(): return lax.ppermute(x, AXES, [(i, i ^ mask) for i in range(n)])  11.6 us
    ppermute x9, waiting for transfers between devices, swap_pairs(): return lax.ppermute(x, AXES, [(i, i ^ mask) for i in range(n)])  8.11 us
    pallas_call x2, Pallas kernels, plan_slots(): call(functools.partial(slot_kernel, which), 'slots', [((rows, padded(n)),...  1.76 us
    pallas_call x1, Pallas kernels, body(): call(functools.partial(final_kernel, per_row, crossing), 'final', [((2, p...  1.5 us
    slice x1, local copies, waits for them, and re-layouts, body(): t_across = swap_pairs(transfer[:, :, :crossing], n_cols)  1.18 us
    convert_element_type x1, other arithmetic, body(): code = code.astype(BF)  1.11 us
    unnamed x11, local copies, waits for them, and re-layouts  0.85 us
    pallas_call x1, Pallas kernels, body(): call(functools.partial(mine_kernel, per_row), 'mine', [((2 * per_row, mod...  0.65 us
  transfers between devices with their start and end apart: 9, of which 7 were waited for; matrix products, arithmetic and copies ran while one was open for 8% of the time, Pallas kernels for 15%

profile of v4, /device:TPU:0, one launch (start us, length us, event | category | flops | bytes accessed | tf_op | source)
XLA Modules:
  0.0 31.1 jit_solution(8448023006512733792)
XLA Ops:
  0.6 0.0 copy-start
  0.6 1.1 %multiply_convert_fusion = bf16[64,1024]{1,0:T(8,128)(2,1)S(1)} fusion(f32[1024,64]{0,1:T(8,128)} %param.8), kind=kLoop, calls=%fused_computation.11 | loop fusion | flops 393216 | bytes 393216 | tf_op jit(solution)/shard_map/convert_element_type | solution.py:356
  1.8 0.0 copy-start.1
  1.8 0.0 copy-start.2
  1.8 3.0 %collective-permute-start.6 = (bf16[64,1024]{1,0:T(8,128)(2,1)S(1)}, bf16[64,1024]{1,0:T(8,128)(2,1)S(1)}, u32[]{:S(2)}, u32[]{:S(2)}) collective-permute-start(bf16[64,1024]{1,0:T(8,128)(2,1)S(1)} %multiply_convert_fusion), channel_id=1, source_target_pairs={{0,16},{1,17},{2,18},{3,19},{4,20},{5,21},{6,22},{7,23},{8,24},{9,... | collective-permute-start | bytes 393224 | tf_op jit(solution)/shard_map/ppermute | solution.py:57
  4.8 1.2 %slice.53 = bf16[2,256,768]{2,1,0:T(8,128)(2,1)S(1)} slice(bf16[2,256,1024]{2,1,0:T(8,128)(2,1)} %t_ref.7), slice={[0:2], [0:256], [0:768]} | slice | bytes 1572864 | tf_op jit(solution)/shard_map/slice | solution.py:375
  6.0 0.1 collective-permute-start.8
  6.1 0.0 copy-done
  6.1 0.0 copy-done.1
  6.1 0.0 copy-done.2
  6.1 0.0 copy-start.3
  6.1 0.0 copy-start.4
  6.1 0.5 %own.1 = (f32[256,128]{1,0:T(8,128)S(1)}, f32[64,128]{1,0:T(8,128)S(1)}) custom-call(f32[64,1024]{1,0:T(8,128)S(1)} %bitcast.11, s32[64,128]{1,0:T(8,128)S(1)} %bitcast.12, bf16[2,256,1024]{2,1,0:T(8,128)(2,1)S(1)} %copy-done), custom_call_target="tpu_custom_call" | custom-call | flops 1 | bytes 1 | tf_op jit(solution)/shard_map/own/pallas_call | solution.py:377
  6.7 0.2 copy-done.3
  6.9 0.0 copy-done.4
  6.9 0.2 plan.1
  7.1 0.5 %slice.52 = s32[1,1]{0,1:T(1,128)} slice(s32[128,64]{0,1:T(8,128)S(1)} %copy-done.2), slice={[0:1], [0:1]} | slice | bytes 8 | tf_op jit(solution)/shard_map/slice | solution.py:438
  8.2 0.5 %collective-permute-done.6.code_ref = bf16[64,1024]{1,0:T(8,128)(2,1)S(1)} collective-permute-done((bf16[64,1024]{1,0:T(8,128)(2,1)S(1)}, bf16[64,1024]{1,0:T(8,128)(2,1)S(1)}, u32[]{:S(2)}, u32[]{:S(2)}) %collective-permute-start.6) | collective-permute-done | bytes 131104 | tf_op jit(solution)/shard_map/ppermute | solution.py:57
  8.7 0.6 %other.1 = (f32[128,128]{1,0:T(8,128)S(1)}, f32[256,128]{1,0:T(8,128)S(1)}, bf16[256,128]{1,0:T(8,128)(2,1)S(1)}) custom-call(bf16[64,1024]{1,0:T(8,128)(2,1)S(1)} %collective-permute-done.6.code_ref, s32[64,128]{1,0:T(8,128)S(1)} %bitcast.14, bf16[2,256,1024]{2,1,0:T(8,128)(2,1)S(1)} %copy-done, f32[256,128]{1,0:T(8,128)S(1)} %get-tuple-element.51.own_ref, ...), custom_call_target="tpu_custom_call" | custom-call | flops 30000001024 | bytes 1 | tf_op jit(solution)/shard_map/other/pallas_call | solution.py:386
  9.3 13.8 %conditional.1 = (f32[128,128]{1,0:T(8,128)S(1)}, f32[32,128]{1,0:T(8,128)S(1)}, s32[256,128]{1,0:T(8,128)S(1)}, s32[256,128]{1,0:T(8,128)S(1)}) conditional(s32[]{:T(128)} %bitcast, () %tuple.20, (f32[128,128]{1,0:T(8,128)S(1)}, s32[64,128]{1,0:T(8,128)S(1)}, bf16[256,128]{1,0:T(8,128)(2,1)S(1)}, f32[256,128]{1,0:T(8,128)S(1)}) %tuple.22), branch_computations={%region_0.1_spmd, %region_1.2_spmd} | conditional | flops 679937 | bytes 2711825 | solution.py:437
  9.4 0.1 collective-permute-start.1
  9.4 0.5 %collective-permute-start = (f32[128,128]{1,0:T(8,128)S(1)}, f32[128,128]{1,0:T(8,128)S(1)}, u32[]{:S(2)}, u32[]{:S(2)}) collective-permute-start(f32[128,128]{1,0:T(8,128)S(1)} %get-tuple-element.8), channel_id=1, source_target_pairs={{0,1},{1,0},{2,3},{3,2},{4,5},{5,4},{6,7},{7,6},{8,9},{9,8},{10,11... | collective-permute-start | bytes 196616 | tf_op jit(solution)/shard_map/cond/branch_1_fun/ppermute | solution.py:57
  9.9 0.7 %collective-permute-done.1 = bf16[256,128]{1,0:T(8,128)(2,1)S(1)} collective-permute-done((bf16[256,128]{1,0:T(8,128)(2,1)S(1)}, bf16[256,128]{1,0:T(8,128)(2,1)S(1)}, u32[]{:S(2)}, u32[]{:S(2)}) %collective-permute-start.1) | collective-permute-done | bytes 65568 | tf_op jit(solution)/shard_map/cond/branch_1_fun/ppermute | solution.py:57
  10.7 0.1 collective-permute-done
  10.9 1.7 %collective-permute-start.2 = (bf16[192,128]{1,0:T(8,128)(2,1)S(1)}, bf16[192,128]{1,0:T(8,128)(2,1)S(1)}, u32[]{:S(2)}, u32[]{:S(2)}) collective-permute-start(bf16[192,128]{1,0:T(8,128)(2,1)S(1)} %get-tuple-element.84), channel_id=1, source_target_pairs={{0,5},{1,4},{2,7},{3,6},{4,1},{5,0},{6,3},{7,2},{8,13},{9,12},{10,... | collective-permute-start | bytes 147464 | tf_op jit(solution)/shard_map/cond/branch_1_fun/ppermute | solution.py:57
  12.5 1.4 %collective-permute-start.4 = (bf16[192,128]{1,0:T(8,128)(2,1)S(1)}, bf16[192,128]{1,0:T(8,128)(2,1)S(1)}, u32[]{:S(2)}, u32[]{:S(2)}) collective-permute-start(bf16[192,128]{1,0:T(8,128)(2,1)S(1)} %get-tuple-element.85), channel_id=1, source_target_pairs={{0,6},{1,7},{2,4},{3,5},{4,2},{5,3},{6,0},{7,1},{8,14},{9,15},{10,... | collective-permute-start | bytes 147464 | tf_op jit(solution)/shard_map/cond/branch_1_fun/ppermute | solution.py:57
  13.9 0.0 collective-permute-start.3
  13.9 0.9 %slots.2 = (s32[256,128]{1,0:T(8,128)S(1)}, s32[256,128]{1,0:T(8,128)S(1)}) custom-call(s32[64,128]{1,0:T(8,128)S(1)} %get-tuple-element.13.now_ref), custom_call_target="tpu_custom_call" | custom-call | flops 1 | bytes 1 | tf_op jit(solution)/shard_map/cond/branch_1_fun/slots/pallas_call | solution.py:399
  14.8 0.0 collective-permute-done.2
  14.8 2.8 %collective-permute-done.4 = bf16[192,128]{1,0:T(8,128)(2,1)S(1)} collective-permute-done((bf16[192,128]{1,0:T(8,128)(2,1)S(1)}, bf16[192,128]{1,0:T(8,128)(2,1)S(1)}, u32[]{:S(2)}, u32[]{:S(2)}) %collective-permute-start.4) | collective-permute-done | bytes 49184 | tf_op jit(solution)/shard_map/cond/branch_1_fun/ppermute | solution.py:57
  17.6 0.8 %collective-permute-done.3 = bf16[192,128]{1,0:T(8,128)(2,1)S(1)} collective-permute-done((bf16[192,128]{1,0:T(8,128)(2,1)S(1)}, bf16[192,128]{1,0:T(8,128)(2,1)S(1)}, u32[]{:S(2)}, u32[]{:S(2)}) %collective-permute-start.3) | collective-permute-done | bytes 49184 | tf_op jit(solution)/shard_map/cond/branch_1_fun/ppermute | solution.py:57
  18.5 2.4 %collective-permute-start.5 = (bf16[160,128]{1,0:T(8,128)(2,1)S(1)}, bf16[160,128]{1,0:T(8,128)(2,1)S(1)}, u32[]{:S(2)}, u32[]{:S(2)}) collective-permute-start(bf16[160,128]{1,0:T(8,128)(2,1)S(1)} %pad_maximum_fusion.3), channel_id=1, source_target_pairs={{0,9},{1,8},{2,11},{3,10},{4,13},{5,12},{6,15},{7,14},{8,1},{9,0},... | collective-permute-start | bytes 122888 | tf_op jit(solution)/shard_map/cond/branch_1_fun/ppermute | solution.py:57
  20.9 2.1 %collective-permute-done.5 = bf16[160,128]{1,0:T(8,128)(2,1)S(1)} collective-permute-done((bf16[160,128]{1,0:T(8,128)(2,1)S(1)}, bf16[160,128]{1,0:T(8,128)(2,1)S(1)}, u32[]{:S(2)}, u32[]{:S(2)}) %collective-permute-start.5) | collective-permute-done | bytes 40992 | tf_op jit(solution)/shard_map/cond/branch_1_fun/ppermute | solution.py:57
  23.1 0.6 %values.1 = (f32[64,128]{1,0:T(8,128)S(1)}, bf16[1,384,128]{2,1,0:T(8,128)(2,1)S(1)}) custom-call(f32[128,128]{1,0:T(8,128)S(1)} %get-tuple-element.59.trap_ref, bf16[2,256,1024]{2,1,0:T(8,128)(2,1)S(1)} %copy-done, s32[64,128]{1,0:T(8,128)S(1)} %get-tuple-element.60.refs_0_.idx_ref, f32[64,128]{1,0:T(8,128)S(1)} %get-tuple-element.61.refs_1_, ...), custom_call_target="tpu_custom_call" | custom-call | flops 1 | bytes 1 | tf_op jit(solution)/shard_map/values/pallas_call | solution.py:444
  23.7 2.5 %collective-permute-start.7 = (bf16[384,128]{1,0:T(8,128)(2,1)S(1)}, bf16[384,128]{1,0:T(8,128)(2,1)S(1)}, u32[]{:S(2)}, u32[]{:S(2)}) collective-permute-start(bf16[384,128]{1,0:T(8,128)(2,1)S(1)} %bitcast.15), channel_id=1, source_target_pairs={{0,16},{1,17},{2,18},{3,19},{4,20},{5,21},{6,22},{7,23},{8,24},{9,... | collective-permute-start | bytes 294920 | tf_op jit(solution)/shard_map/ppermute | solution.py:57
  26.2 0.2 far.1
  26.4 0.7 %mine.1.mine_ref = f32[128,1024]{1,0:T(8,128)S(1)} custom-call(f32[64,128]{1,0:T(8,128)S(1)} %get-tuple-element.67.value_ref, s32[64,128]{1,0:T(8,128)S(1)} %get-tuple-element.60.refs_0_.idx_ref, s32[256,128]{1,0:T(8,128)S(1)} %get-tuple-element.68.slot_ref, bf16[2,256,1024]{2,1,0:T(8,128)(2,1)S(1)} %copy-done), custom_call_target="tpu_custom_call" | custom-call | flops 1 | bytes 1 | tf_op jit(solution)/shard_map/mine/pallas_call | solution.py:455
  27.1 0.9 %slots.3.refs_1_ = s32[256,128]{1,0:T(8,128)S(1)} custom-call(s32[64,128]{1,0:T(8,128)S(1)} %get-tuple-element.73.now_ref), custom_call_target="tpu_custom_call" | custom-call | flops 1 | bytes 1 | tf_op jit(solution)/shard_map/slots/pallas_call | solution.py:399
  28.0 0.6 %copy.8 = bf16[16,2,128]{2,1,0:T(2,128)(2,1)} copy(bf16[16,2,128]{2,0,1:T(8,128)(2,1)S(1)} %bitcast.19) | data formatting | bytes 16384
  28.6 1.0 %collective-permute-done.7 = bf16[384,128]{1,0:T(8,128)(2,1)S(1)} collective-permute-done((bf16[384,128]{1,0:T(8,128)(2,1)S(1)}, bf16[384,128]{1,0:T(8,128)(2,1)S(1)}, u32[]{:S(2)}, u32[]{:S(2)}) %collective-permute-start.7) | collective-permute-done | bytes 98336 | tf_op jit(solution)/shard_map/ppermute | solution.py:57
  29.6 0.0 collective-permute-done.8.refs_2_
  29.6 1.5 %final.1 = (f32[2,64,1024]{2,1,0:T(8,128)}, f32[64,128]{1,0:T(8,128)}) custom-call(f32[64,128]{1,0:T(8,128)S(1)} %get-tuple-element.58.old_ref, f32[128,1024]{1,0:T(8,128)S(1)} %mine.1.mine_ref, bf16[1,384,128]{2,1,0:T(8,128)(2,1)S(1)} %get-tuple-element.71.sent_ref, bf16[1,384,128]{2,1,0:T(8,128)(2,1)S(1)} %bitcast.16, ...), custom_call_target="tpu_custom_call" | custom-call | flops 1 | bytes 1 | tf_op jit(solution)/shard_map/final/pallas_call | solution.py:468
  (10 shorter events, 0.1 us)
Async XLA Ops:
  0.6 5.5 %copy-start = (bf16[2,256,1024]{2,1,0:T(8,128)(2,1)S(1)}, bf16[2,256,1024]{2,1,0:T(8,128)(2,1)}, u32[]{:S(2)}) copy-start(bf16[2,256,1024]{2,1,0:T(8,128)(2,1)} %t_ref.7) | copy-start | bytes 3145732
  1.8 4.3 %copy-start.1 = (f32[1024,64]{0,1:T(8,128)S(1)}, f32[1024,64]{0,1:T(8,128)}, u32[]{:S(2)}) copy-start(f32[1024,64]{0,1:T(8,128)} %param.8) | copy-start | bytes 786436
  1.8 4.3 %copy-start.2 = (s32[128,64]{0,1:T(8,128)S(1)}, s32[128,64]{0,1:T(8,128)}, u32[]{:S(2)}) copy-start(s32[128,64]{0,1:T(8,128)} %param.9) | copy-start | bytes 98308
  1.8 6.9 %collective-permute-start.6 = (bf16[64,1024]{1,0:T(8,128)(2,1)S(1)}, bf16[64,1024]{1,0:T(8,128)(2,1)S(1)}, u32[]{:S(2)}, u32[]{:S(2)}) collective-permute-start(bf16[64,1024]{1,0:T(8,128)(2,1)S(1)} %multiply_convert_fusion), channel_id=1, source_target_pairs={{0,16},{1,17},{2,18},{3,19},{4,20},{5,21},{6,22},{7,23},{8,24},{9,... | collective-permute-start | bytes 393224 | tf_op jit(solution)/shard_map/ppermute | solution.py:57
  6.0 23.6 %collective-permute-start.8 = (bf16[2,256,768]{2,1,0:T(8,128)(2,1)S(1)}, bf16[2,256,768]{2,1,0:T(8,128)(2,1)S(1)}, u32[]{:S(2)}, u32[]{:S(2)}) collective-permute-start(bf16[2,256,768]{2,1,0:T(8,128)(2,1)S(1)} %slice.53), channel_id=1, source_target_pairs={{0,16},{1,17},{2,18},{3,19},{4,20},{5,21},{6,22},{7,23},{8,24},{9,... | collective-permute-start | bytes 2359304 | tf_op jit(solution)/shard_map/ppermute | solution.py:57
  6.1 0.8 %copy-start.3 = (s32[128,64]{0,1:T(8,128)S(1)}, s32[128,64]{0,1:T(8,128)}, u32[]{:S(2)}) copy-start(s32[128,64]{0,1:T(8,128)} %param.10) | copy-start | bytes 98308
  6.1 0.8 %copy-start.4 = (f32[128,64]{0,1:T(8,128)S(1)}, f32[128,64]{0,1:T(8,128)}, u32[]{:S(2)}) copy-start(f32[128,64]{0,1:T(8,128)} %param.11) | copy-start | bytes 98308
  9.4 1.3 %collective-permute-start.1 = (bf16[256,128]{1,0:T(8,128)(2,1)S(1)}, bf16[256,128]{1,0:T(8,128)(2,1)S(1)}, u32[]{:S(2)}, u32[]{:S(2)}) collective-permute-start(bf16[256,128]{1,0:T(8,128)(2,1)S(1)} %get-tuple-element.12), channel_id=1, source_target_pairs={{0,1},{1,0},{2,3},{3,2},{4,5},{5,4},{6,7},{7,6},{8,9},{9,8},{10,11... | collective-permute-start | bytes 196616 | tf_op jit(solution)/shard_map/cond/branch_1_fun/ppermute | solution.py:57
  9.4 1.4 %collective-permute-start = (f32[128,128]{1,0:T(8,128)S(1)}, f32[128,128]{1,0:T(8,128)S(1)}, u32[]{:S(2)}, u32[]{:S(2)}) collective-permute-start(f32[128,128]{1,0:T(8,128)S(1)} %get-tuple-element.8), channel_id=1, source_target_pairs={{0,1},{1,0},{2,3},{3,2},{4,5},{5,4},{6,7},{7,6},{8,9},{9,8},{10,11... | collective-permute-start | bytes 196616 | tf_op jit(solution)/shard_map/cond/branch_1_fun/ppermute | solution.py:57
  10.9 3.9 %collective-permute-start.2 = (bf16[192,128]{1,0:T(8,128)(2,1)S(1)}, bf16[192,128]{1,0:T(8,128)(2,1)S(1)}, u32[]{:S(2)}, u32[]{:S(2)}) collective-permute-start(bf16[192,128]{1,0:T(8,128)(2,1)S(1)} %get-tuple-element.84), channel_id=1, source_target_pairs={{0,5},{1,4},{2,7},{3,6},{4,1},{5,0},{6,3},{7,2},{8,13},{9,12},{10,... | collective-permute-start | bytes 147464 | tf_op jit(solution)/shard_map/cond/branch_1_fun/ppermute | solution.py:57
  12.5 5.1 %collective-permute-start.4 = (bf16[192,128]{1,0:T(8,128)(2,1)S(1)}, bf16[192,128]{1,0:T(8,128)(2,1)S(1)}, u32[]{:S(2)}, u32[]{:S(2)}) collective-permute-start(bf16[192,128]{1,0:T(8,128)(2,1)S(1)} %get-tuple-element.85), channel_id=1, source_target_pairs={{0,6},{1,7},{2,4},{3,5},{4,2},{5,3},{6,0},{7,1},{8,14},{9,15},{10,... | collective-permute-start | bytes 147464 | tf_op jit(solution)/shard_map/cond/branch_1_fun/ppermute | solution.py:57
  13.9 4.5 %collective-permute-start.3 = (bf16[192,128]{1,0:T(8,128)(2,1)S(1)}, bf16[192,128]{1,0:T(8,128)(2,1)S(1)}, u32[]{:S(2)}, u32[]{:S(2)}) collective-permute-start(bf16[192,128]{1,0:T(8,128)(2,1)S(1)} %get-tuple-element.86), channel_id=1, source_target_pairs={{0,3},{1,2},{2,1},{3,0},{4,7},{5,6},{6,5},{7,4},{8,11},{9,10},{10,... | collective-permute-start | bytes 147464 | tf_op jit(solution)/shard_map/cond/branch_1_fun/ppermute | solution.py:57
  18.5 4.6 %collective-permute-start.5 = (bf16[160,128]{1,0:T(8,128)(2,1)S(1)}, bf16[160,128]{1,0:T(8,128)(2,1)S(1)}, u32[]{:S(2)}, u32[]{:S(2)}) collective-permute-start(bf16[160,128]{1,0:T(8,128)(2,1)S(1)} %pad_maximum_fusion.3), channel_id=1, source_target_pairs={{0,9},{1,8},{2,11},{3,10},{4,13},{5,12},{6,15},{7,14},{8,1},{9,0},... | collective-permute-start | bytes 122888 | tf_op jit(solution)/shard_map/cond/branch_1_fun/ppermute | solution.py:57
  23.7 5.8 %collective-permute-start.7 = (bf16[384,128]{1,0:T(8,128)(2,1)S(1)}, bf16[384,128]{1,0:T(8,128)(2,1)S(1)}, u32[]{:S(2)}, u32[]{:S(2)}) collective-permute-start(bf16[384,128]{1,0:T(8,128)(2,1)S(1)} %bitcast.15), channel_id=1, source_target_pairs={{0,16},{1,17},{2,18},{3,19},{4,20},{5,21},{6,22},{7,23},{8,24},{9,... | collective-permute-start | bytes 294920 | tf_op jit(solution)/shard_map/ppermute | solution.py:57

commit v5 on v4

--- a/solution.py
+++ b/solution.py
@@ -165,8 +165,7 @@
     now_ref[...] = mine
     refs[0][...] = old
     theirs = mine + (2 * row - 1) * rows
-    refs[-2][...] = theirs
-    refs[-1][...] = spread(theirs, 0, per_row)
+    refs[-1][...] = theirs
     inverse = 1.0 / target
     numer = old * (target * target)
     for s, (base, n) in enumerate(((0, per_row), (per_row, count - per_row))):
@@ -196,7 +195,7 @@
     lax.fori_loop(0, slot_refs[0].shape[0] // (8 * group), find, 0)
 
 
-def scatter(idx_ref, value_ref, slot_ref, px_ref, n):
+def joined(idx_ref, value_ref):
     traps, lanes = idx_ref.shape
     index = idx_ref[...]
     acc = [jnp.zeros((8, lanes), F32) for _ in range(traps // 8)]
@@ -205,12 +204,17 @@
         val = jnp.broadcast_to(value_ref[k:k + 1, :], (8, lanes))
         for g in range(traps // 8):
             acc[g] += jnp.where(index[g * 8:(g + 1) * 8, :] == ind, val, 0.0)
+    return acc
+
+
+def scatter(acc, slot_ref, px_ref, n):
+    lanes = slot_ref.shape[1]
     for h in range(slot_ref.shape[0] // 8):
         slot = slot_ref[h * 8:(h + 1) * 8, :]
         high = slot >> 3
         low = slot & 7
         got = jnp.zeros((8, lanes), F32)
-        for g in range(traps // 8):
+        for g in range(len(acc)):
             got = jnp.where(high == g, jnp.take_along_axis(acc[g], low, axis=0), got)
         px_ref[h * 8:(h + 1) * 8, :] = got
     proj = px_ref[...].astype(BF).T
@@ -246,12 +250,13 @@
     own_lanes = lane_of(ratios[0][:, :LANES]) < per_row
     q = jnp.where(own_lanes, ratios[0][:, :LANES], turn(ratios[1][:, :LANES], -per_row)).astype(BF)
     n = LANES - per_row
-    back = back_through(scatter(sets[1][0], value_oth_ref, slot_ref, px_ref, n), t_ref, crossing, modes)
+    acc = joined(sets[1][0], value_oth_ref)
+    back = back_through(scatter(acc, slot_ref, px_ref, n), t_ref, crossing, modes)
     for j in range(n // per_row):
         away_ref[j, :traps, :] = q
         at = traps
         if crossing:
-            away_ref[j, at:at + traps, :] = value_oth_ref[...].astype(BF)
+            away_ref[j, at:at + traps, :] = jnp.concatenate(acc, axis=0).astype(BF)
             at += traps
         for w in range((modes - crossing) // LANES):
             lanes = slice(w * LANES, (w + 1) * LANES)
@@ -275,12 +280,12 @@
 
 
 def mine_kernel(per_row, value_ref, idx_ref, slot_ref, t_ref, mine_ref, px_ref):
-    pair = scatter(idx_ref, value_ref, slot_ref, px_ref, per_row)
+    pair = scatter(joined(idx_ref, value_ref), slot_ref, px_ref, per_row)
     mine_ref[...] = back_through(pair, t_ref, 0, t_ref.shape[2])[:2 * per_row]
 
 
 def final_kernel(per_row, crossing, old_ref, mine_ref, sent_ref, got_ref, *refs):
-    slm_ref, weights_ref, out_ref, scaled_ref, sems = refs[3:8] if crossing else refs
+    slm_ref, weights_ref, out_ref, scaled_ref, sems = refs[2:7] if crossing else refs
     traps, count = old_ref.shape
     n_rows = count // per_row
     modes = mine_ref.shape[1]
@@ -299,11 +304,10 @@
     at = traps
     across = []
     if crossing:
-        idx_ref, slot_ref, t_ref = refs[:3]
-        px_ref, value_ref = refs[8:]
-        value_ref[...] = got_ref[0, at:at + traps, :].astype(F32)
+        slot_ref, t_ref = refs[:2]
+        acc = [got_ref[0, at + g * 8:at + (g + 1) * 8, :].astype(F32) for g in range(traps // 8)]
         at += traps
-        across = [back_through(scatter(idx_ref, value_ref, slot_ref, px_ref, per_row), t_ref, 0, crossing)]
+        across = [back_through(scatter(acc, slot_ref, refs[7], per_row), t_ref, 0, crossing)]
     step = 16
     for i in range(per_row // step):
         halves = []
@@ -361,12 +365,12 @@
     index, target, old = trap_index.T, levels.T, weights_old.T
     any_space = pl.BlockSpec(memory_space=pl.ANY)
     sets = (wide_own, wide_oth)
-    now, old, *tables, now_cross, idx_cross = call(
+    now, old, *tables, now_cross = call(
         functools.partial(plan_kernel, per_row, rows),
         "plan",
         [((traps, count), jnp.int32), ((traps, count), F32)]
         + [((traps, wide), d) for wide in sets for d in (jnp.int32, F32, F32)]
-        + [((traps, count), jnp.int32), ((traps, wide_own), jnp.int32)],
+        + [((traps, count), jnp.int32)],
         [VMEM] * 3,
         **cost,
     )(index, target, old)
@@ -463,8 +467,8 @@
     if crossing:
         mine, now_cross = lax.optimization_barrier((mine, now_cross))
         (slots_cross,) = plan_slots(now_cross, own_set)
-    extra = [idx_cross, slots_cross, t_across] if crossing else []
-    room = [pltpu.VMEM((rows, wide_own), F32), pltpu.VMEM((traps, wide_own), F32)] if crossing else []
+    extra = [slots_cross, t_across] if crossing else []
+    room = [pltpu.VMEM((rows, wide_own), F32)] if crossing else []
     slm, weights = call(
         functools.partial(final_kernel, per_row, crossing),
         "final",

time: 31.3 us -> 31.1 us (level)
  no operation moved by 1% of the time
where the time goes in v5:
time: 31.1 us; the launch traced here: 30.9 us
  starting transfers between devices  11.6 us (37%)
  waiting for transfers between devices  8.12 us (26%)
  Pallas kernels  5.88 us (19%)
  local copies, waits for them, and re-layouts  2.55 us (8%)
  between operations  1.4 us (5%)
  other arithmetic  1.21 us (4%)
    ppermute x9, starting transfers between devices, swap_pairs(): return lax.ppermute(x, AXES, [(i, i ^ mask) for i in range(n)])  11.6 us
    ppermute x9, waiting for transfers between devices, swap_pairs(): return lax.ppermute(x, AXES, [(i, i ^ mask) for i in range(n)])  8.12 us
    pallas_call x2, Pallas kernels, plan_slots(): call(functools.partial(slot_kernel, which), 'slots', [((rows, padded(n)),...  1.76 us
    pallas_call x1, Pallas kernels, body(): call(functools.partial(final_kernel, per_row, crossing), 'final', [((2, p...  1.3 us
    slice x1, local copies, waits for them, and re-layouts, body(): t_across = swap_pairs(transfer[:, :, :crossing], n_cols)  1.18 us
    convert_element_type x1, other arithmetic, body(): code = code.astype(BF)  1.11 us
    unnamed x11, local copies, waits for them, and re-layouts  0.85 us
    pallas_call x1, Pallas kernels, body(): call(functools.partial(mine_kernel, per_row), 'mine', [((2 * per_row, mod...  0.65 us
  transfers between devices with their start and end apart: 9, of which 7 were waited for; matrix products, arithmetic and copies ran while one was open for 8% of the time, Pallas kernels for 15%

profile of v5, /device:TPU:0, one launch (start us, length us, event | category | flops | bytes accessed | tf_op | source)
XLA Modules:
  0.0 30.9 jit_solution(14806332115188966498)
XLA Ops:
  0.6 0.0 copy-start
  0.6 1.1 %multiply_convert_fusion = bf16[64,1024]{1,0:T(8,128)(2,1)S(1)} fusion(f32[1024,64]{0,1:T(8,128)} %param.8), kind=kLoop, calls=%fused_computation.11 | loop fusion | flops 393216 | bytes 393216 | tf_op jit(solution)/shard_map/convert_element_type | solution.py:360
  1.8 0.0 copy-start.1
  1.8 0.0 copy-start.2
  1.8 3.0 %collective-permute-start.6 = (bf16[64,1024]{1,0:T(8,128)(2,1)S(1)}, bf16[64,1024]{1,0:T(8,128)(2,1)S(1)}, u32[]{:S(2)}, u32[]{:S(2)}) collective-permute-start(bf16[64,1024]{1,0:T(8,128)(2,1)S(1)} %multiply_convert_fusion), channel_id=1, source_target_pairs={{0,16},{1,17},{2,18},{3,19},{4,20},{5,21},{6,22},{7,23},{8,24},{9,... | collective-permute-start | bytes 393224 | tf_op jit(solution)/shard_map/ppermute | solution.py:57
  4.8 1.2 %slice.53 = bf16[2,256,768]{2,1,0:T(8,128)(2,1)S(1)} slice(bf16[2,256,1024]{2,1,0:T(8,128)(2,1)} %t_ref.7), slice={[0:2], [0:256], [0:768]} | slice | bytes 1572864 | tf_op jit(solution)/shard_map/slice | solution.py:379
  6.0 0.1 collective-permute-start.8
  6.1 0.0 copy-done
  6.1 0.0 copy-done.1
  6.1 0.0 copy-done.2
  6.1 0.0 copy-start.3
  6.1 0.0 copy-start.4
  6.1 0.5 %own.1 = (f32[256,128]{1,0:T(8,128)S(1)}, f32[64,128]{1,0:T(8,128)S(1)}) custom-call(f32[64,1024]{1,0:T(8,128)S(1)} %bitcast.11, s32[64,128]{1,0:T(8,128)S(1)} %bitcast.12, bf16[2,256,1024]{2,1,0:T(8,128)(2,1)S(1)} %copy-done), custom_call_target="tpu_custom_call" | custom-call | flops 1 | bytes 1 | tf_op jit(solution)/shard_map/own/pallas_call | solution.py:381
  6.7 0.2 copy-done.3
  6.9 0.0 copy-done.4
  6.9 0.2 plan.1
  7.1 0.5 %slice.52 = s32[1,1]{0,1:T(1,128)} slice(s32[128,64]{0,1:T(8,128)S(1)} %copy-done.2), slice={[0:1], [0:1]} | slice | bytes 8 | tf_op jit(solution)/shard_map/slice | solution.py:442
  8.2 0.5 %collective-permute-done.6.code_ref = bf16[64,1024]{1,0:T(8,128)(2,1)S(1)} collective-permute-done((bf16[64,1024]{1,0:T(8,128)(2,1)S(1)}, bf16[64,1024]{1,0:T(8,128)(2,1)S(1)}, u32[]{:S(2)}, u32[]{:S(2)}) %collective-permute-start.6) | collective-permute-done | bytes 131104 | tf_op jit(solution)/shard_map/ppermute | solution.py:57
  8.7 0.6 %other.1 = (f32[128,128]{1,0:T(8,128)S(1)}, f32[256,128]{1,0:T(8,128)S(1)}, bf16[256,128]{1,0:T(8,128)(2,1)S(1)}) custom-call(bf16[64,1024]{1,0:T(8,128)(2,1)S(1)} %collective-permute-done.6.code_ref, s32[64,128]{1,0:T(8,128)S(1)} %bitcast.14, bf16[2,256,1024]{2,1,0:T(8,128)(2,1)S(1)} %copy-done, f32[256,128]{1,0:T(8,128)S(1)} %get-tuple-element.50.own_ref, ...), custom_call_target="tpu_custom_call" | custom-call | flops 30000001024 | bytes 1 | tf_op jit(solution)/shard_map/other/pallas_call | solution.py:390
  9.3 13.8 %conditional.1 = (f32[128,128]{1,0:T(8,128)S(1)}, f32[32,128]{1,0:T(8,128)S(1)}, s32[256,128]{1,0:T(8,128)S(1)}, s32[256,128]{1,0:T(8,128)S(1)}) conditional(s32[]{:T(128)} %bitcast, () %tuple.20, (f32[128,128]{1,0:T(8,128)S(1)}, s32[64,128]{1,0:T(8,128)S(1)}, bf16[256,128]{1,0:T(8,128)(2,1)S(1)}, f32[256,128]{1,0:T(8,128)S(1)}) %tuple.22), branch_computations={%region_0.1_spmd, %region_1.2_spmd} | conditional | flops 679937 | bytes 2711825 | solution.py:441
  9.4 0.1 collective-permute-start.1
  9.4 0.5 %collective-permute-start = (f32[128,128]{1,0:T(8,128)S(1)}, f32[128,128]{1,0:T(8,128)S(1)}, u32[]{:S(2)}, u32[]{:S(2)}) collective-permute-start(f32[128,128]{1,0:T(8,128)S(1)} %get-tuple-element.8), channel_id=1, source_target_pairs={{0,1},{1,0},{2,3},{3,2},{4,5},{5,4},{6,7},{7,6},{8,9},{9,8},{10,11... | collective-permute-start | bytes 196616 | tf_op jit(solution)/shard_map/cond/branch_1_fun/ppermute | solution.py:57
  9.9 0.7 %collective-permute-done.1 = bf16[256,128]{1,0:T(8,128)(2,1)S(1)} collective-permute-done((bf16[256,128]{1,0:T(8,128)(2,1)S(1)}, bf16[256,128]{1,0:T(8,128)(2,1)S(1)}, u32[]{:S(2)}, u32[]{:S(2)}) %collective-permute-start.1) | collective-permute-done | bytes 65568 | tf_op jit(solution)/shard_map/cond/branch_1_fun/ppermute | solution.py:57
  10.7 0.1 collective-permute-done
  10.9 1.7 %collective-permute-start.2 = (bf16[192,128]{1,0:T(8,128)(2,1)S(1)}, bf16[192,128]{1,0:T(8,128)(2,1)S(1)}, u32[]{:S(2)}, u32[]{:S(2)}) collective-permute-start(bf16[192,128]{1,0:T(8,128)(2,1)S(1)} %get-tuple-element.82), channel_id=1, source_target_pairs={{0,5},{1,4},{2,7},{3,6},{4,1},{5,0},{6,3},{7,2},{8,13},{9,12},{10,... | collective-permute-start | bytes 147464 | tf_op jit(solution)/shard_map/cond/branch_1_fun/ppermute | solution.py:57
  12.5 1.4 %collective-permute-start.4 = (bf16[192,128]{1,0:T(8,128)(2,1)S(1)}, bf16[192,128]{1,0:T(8,128)(2,1)S(1)}, u32[]{:S(2)}, u32[]{:S(2)}) collective-permute-start(bf16[192,128]{1,0:T(8,128)(2,1)S(1)} %get-tuple-element.83), channel_id=1, source_target_pairs={{0,6},{1,7},{2,4},{3,5},{4,2},{5,3},{6,0},{7,1},{8,14},{9,15},{10,... | collective-permute-start | bytes 147464 | tf_op jit(solution)/shard_map/cond/branch_1_fun/ppermute | solution.py:57
  13.9 0.0 collective-permute-start.3
  13.9 0.9 %slots.2 = (s32[256,128]{1,0:T(8,128)S(1)}, s32[256,128]{1,0:T(8,128)S(1)}) custom-call(s32[64,128]{1,0:T(8,128)S(1)} %get-tuple-element.13.now_ref), custom_call_target="tpu_custom_call" | custom-call | flops 1 | bytes 1 | tf_op jit(solution)/shard_map/cond/branch_1_fun/slots/pallas_call | solution.py:403
  14.8 0.0 collective-permute-done.2
  14.8 2.8 %collective-permute-done.4 = bf16[192,128]{1,0:T(8,128)(2,1)S(1)} collective-permute-done((bf16[192,128]{1,0:T(8,128)(2,1)S(1)}, bf16[192,128]{1,0:T(8,128)(2,1)S(1)}, u32[]{:S(2)}, u32[]{:S(2)}) %collective-permute-start.4) | collective-permute-done | bytes 49184 | tf_op jit(solution)/shard_map/cond/branch_1_fun/ppermute | solution.py:57
  17.6 0.8 %collective-permute-done.3 = bf16[192,128]{1,0:T(8,128)(2,1)S(1)} collective-permute-done((bf16[192,128]{1,0:T(8,128)(2,1)S(1)}, bf16[192,128]{1,0:T(8,128)(2,1)S(1)}, u32[]{:S(2)}, u32[]{:S(2)}) %collective-permute-start.3) | collective-permute-done | bytes 49184 | tf_op jit(solution)/shard_map/cond/branch_1_fun/ppermute | solution.py:57
  18.5 2.4 %collective-permute-start.5 = (bf16[160,128]{1,0:T(8,128)(2,1)S(1)}, bf16[160,128]{1,0:T(8,128)(2,1)S(1)}, u32[]{:S(2)}, u32[]{:S(2)}) collective-permute-start(bf16[160,128]{1,0:T(8,128)(2,1)S(1)} %pad_maximum_fusion.3), channel_id=1, source_target_pairs={{0,9},{1,8},{2,11},{3,10},{4,13},{5,12},{6,15},{7,14},{8,1},{9,0},... | collective-permute-start | bytes 122888 | tf_op jit(solution)/shard_map/cond/branch_1_fun/ppermute | solution.py:57
  20.9 2.1 %collective-permute-done.5 = bf16[160,128]{1,0:T(8,128)(2,1)S(1)} collective-permute-done((bf16[160,128]{1,0:T(8,128)(2,1)S(1)}, bf16[160,128]{1,0:T(8,128)(2,1)S(1)}, u32[]{:S(2)}, u32[]{:S(2)}) %collective-permute-start.5) | collective-permute-done | bytes 40992 | tf_op jit(solution)/shard_map/cond/branch_1_fun/ppermute | solution.py:57
  23.1 0.6 %values.1 = (f32[64,128]{1,0:T(8,128)S(1)}, bf16[1,384,128]{2,1,0:T(8,128)(2,1)S(1)}) custom-call(f32[128,128]{1,0:T(8,128)S(1)} %get-tuple-element.58.trap_ref, bf16[2,256,1024]{2,1,0:T(8,128)(2,1)S(1)} %copy-done, s32[64,128]{1,0:T(8,128)S(1)} %get-tuple-element.59.refs_0_.idx_ref, f32[64,128]{1,0:T(8,128)S(1)} %get-tuple-element.60.refs_1_, ...), custom_call_target="tpu_custom_call" | custom-call | flops 1 | bytes 1 | tf_op jit(solution)/shard_map/values/pallas_call | solution.py:448
  23.7 2.5 %collective-permute-start.7 = (bf16[384,128]{1,0:T(8,128)(2,1)S(1)}, bf16[384,128]{1,0:T(8,128)(2,1)S(1)}, u32[]{:S(2)}, u32[]{:S(2)}) collective-permute-start(bf16[384,128]{1,0:T(8,128)(2,1)S(1)} %bitcast.15), channel_id=1, source_target_pairs={{0,16},{1,17},{2,18},{3,19},{4,20},{5,21},{6,22},{7,23},{8,24},{9,... | collective-permute-start | bytes 294920 | tf_op jit(solution)/shard_map/ppermute | solution.py:57
  26.2 0.2 far.1
  26.4 0.6 %mine.1.mine_ref = f32[128,1024]{1,0:T(8,128)S(1)} custom-call(f32[64,128]{1,0:T(8,128)S(1)} %get-tuple-element.66.value_ref, s32[64,128]{1,0:T(8,128)S(1)} %get-tuple-element.59.refs_0_.idx_ref, s32[256,128]{1,0:T(8,128)S(1)} %get-tuple-element.67.slot_ref, bf16[2,256,1024]{2,1,0:T(8,128)(2,1)S(1)} %copy-done), custom_call_target="tpu_custom_call" | custom-call | flops 1 | bytes 1 | tf_op jit(solution)/shard_map/mine/pallas_call | solution.py:459
  27.1 0.9 %slots.3.refs_0_ = s32[256,128]{1,0:T(8,128)S(1)} custom-call(s32[64,128]{1,0:T(8,128)S(1)} %get-tuple-element.71.now_ref), custom_call_target="tpu_custom_call" | custom-call | flops 1 | bytes 1 | tf_op jit(solution)/shard_map/slots/pallas_call | solution.py:403
  27.9 0.6 %copy.8 = bf16[16,2,128]{2,1,0:T(2,128)(2,1)} copy(bf16[16,2,128]{2,0,1:T(8,128)(2,1)S(1)} %bitcast.19) | data formatting | bytes 16384
  28.6 1.0 %collective-permute-done.7 = bf16[384,128]{1,0:T(8,128)(2,1)S(1)} collective-permute-done((bf16[384,128]{1,0:T(8,128)(2,1)S(1)}, bf16[384,128]{1,0:T(8,128)(2,1)S(1)}, u32[]{:S(2)}, u32[]{:S(2)}) %collective-permute-start.7) | collective-permute-done | bytes 98336 | tf_op jit(solution)/shard_map/ppermute | solution.py:57
  29.6 0.0 collective-permute-done.8.refs_1_
  29.6 1.3 %final.1 = (f32[2,64,1024]{2,1,0:T(8,128)}, f32[64,128]{1,0:T(8,128)}) custom-call(f32[64,128]{1,0:T(8,128)S(1)} %get-tuple-element.57.old_ref, f32[128,1024]{1,0:T(8,128)S(1)} %mine.1.mine_ref, bf16[1,384,128]{2,1,0:T(8,128)(2,1)S(1)} %get-tuple-element.70.sent_ref, bf16[1,384,128]{2,1,0:T(8,128)(2,1)S(1)} %bitcast.16, s32[256,128]{1,0:T(8,128)S(1)} %slots.3.refs_0_, ...), custom_call_target="tpu_custom_call" | custom-call | flops 1 | bytes 1 | tf_op jit(solution)/shard_map/final/pallas_call | solution.py:472
  (10 shorter events, 0.1 us)
Async XLA Ops:
  0.6 5.5 %copy-start = (bf16[2,256,1024]{2,1,0:T(8,128)(2,1)S(1)}, bf16[2,256,1024]{2,1,0:T(8,128)(2,1)}, u32[]{:S(2)}) copy-start(bf16[2,256,1024]{2,1,0:T(8,128)(2,1)} %t_ref.7) | copy-start | bytes 3145732
  1.8 4.3 %copy-start.1 = (f32[1024,64]{0,1:T(8,128)S(1)}, f32[1024,64]{0,1:T(8,128)}, u32[]{:S(2)}) copy-start(f32[1024,64]{0,1:T(8,128)} %param.8) | copy-start | bytes 786436
  1.8 4.3 %copy-start.2 = (s32[128,64]{0,1:T(8,128)S(1)}, s32[128,64]{0,1:T(8,128)}, u32[]{:S(2)}) copy-start(s32[128,64]{0,1:T(8,128)} %param.9) | copy-start | bytes 98308
  1.8 6.9 %collective-permute-start.6 = (bf16[64,1024]{1,0:T(8,128)(2,1)S(1)}, bf16[64,1024]{1,0:T(8,128)(2,1)S(1)}, u32[]{:S(2)}, u32[]{:S(2)}) collective-permute-start(bf16[64,1024]{1,0:T(8,128)(2,1)S(1)} %multiply_convert_fusion), channel_id=1, source_target_pairs={{0,16},{1,17},{2,18},{3,19},{4,20},{5,21},{6,22},{7,23},{8,24},{9,... | collective-permute-start | bytes 393224 | tf_op jit(solution)/shard_map/ppermute | solution.py:57
  6.0 23.6 %collective-permute-start.8 = (bf16[2,256,768]{2,1,0:T(8,128)(2,1)S(1)}, bf16[2,256,768]{2,1,0:T(8,128)(2,1)S(1)}, u32[]{:S(2)}, u32[]{:S(2)}) collective-permute-start(bf16[2,256,768]{2,1,0:T(8,128)(2,1)S(1)} %slice.53), channel_id=1, source_target_pairs={{0,16},{1,17},{2,18},{3,19},{4,20},{5,21},{6,22},{7,23},{8,24},{9,... | collective-permute-start | bytes 2359304 | tf_op jit(solution)/shard_map/ppermute | solution.py:57
  6.1 0.8 %copy-start.3 = (s32[128,64]{0,1:T(8,128)S(1)}, s32[128,64]{0,1:T(8,128)}, u32[]{:S(2)}) copy-start(s32[128,64]{0,1:T(8,128)} %param.10) | copy-start | bytes 98308
  6.1 0.8 %copy-start.4 = (f32[128,64]{0,1:T(8,128)S(1)}, f32[128,64]{0,1:T(8,128)}, u32[]{:S(2)}) copy-start(f32[128,64]{0,1:T(8,128)} %param.11) | copy-start | bytes 98308
  9.4 1.3 %collective-permute-start.1 = (bf16[256,128]{1,0:T(8,128)(2,1)S(1)}, bf16[256,128]{1,0:T(8,128)(2,1)S(1)}, u32[]{:S(2)}, u32[]{:S(2)}) collective-permute-start(bf16[256,128]{1,0:T(8,128)(2,1)S(1)} %get-tuple-element.12), channel_id=1, source_target_pairs={{0,1},{1,0},{2,3},{3,2},{4,5},{5,4},{6,7},{7,6},{8,9},{9,8},{10,11... | collective-permute-start | bytes 196616 | tf_op jit(solution)/shard_map/cond/branch_1_fun/ppermute | solution.py:57
  9.4 1.4 %collective-permute-start = (f32[128,128]{1,0:T(8,128)S(1)}, f32[128,128]{1,0:T(8,128)S(1)}, u32[]{:S(2)}, u32[]{:S(2)}) collective-permute-start(f32[128,128]{1,0:T(8,128)S(1)} %get-tuple-element.8), channel_id=1, source_target_pairs={{0,1},{1,0},{2,3},{3,2},{4,5},{5,4},{6,7},{7,6},{8,9},{9,8},{10,11... | collective-permute-start | bytes 196616 | tf_op jit(solution)/shard_map/cond/branch_1_fun/ppermute | solution.py:57
  10.9 3.9 %collective-permute-start.2 = (bf16[192,128]{1,0:T(8,128)(2,1)S(1)}, bf16[192,128]{1,0:T(8,128)(2,1)S(1)}, u32[]{:S(2)}, u32[]{:S(2)}) collective-permute-start(bf16[192,128]{1,0:T(8,128)(2,1)S(1)} %get-tuple-element.82), channel_id=1, source_target_pairs={{0,5},{1,4},{2,7},{3,6},{4,1},{5,0},{6,3},{7,2},{8,13},{9,12},{10,... | collective-permute-start | bytes 147464 | tf_op jit(solution)/shard_map/cond/branch_1_fun/ppermute | solution.py:57
  12.5 5.1 %collective-permute-start.4 = (bf16[192,128]{1,0:T(8,128)(2,1)S(1)}, bf16[192,128]{1,0:T(8,128)(2,1)S(1)}, u32[]{:S(2)}, u32[]{:S(2)}) collective-permute-start(bf16[192,128]{1,0:T(8,128)(2,1)S(1)} %get-tuple-element.83), channel_id=1, source_target_pairs={{0,6},{1,7},{2,4},{3,5},{4,2},{5,3},{6,0},{7,1},{8,14},{9,15},{10,... | collective-permute-start | bytes 147464 | tf_op jit(solution)/shard_map/cond/branch_1_fun/ppermute | solution.py:57
  13.9 4.5 %collective-permute-start.3 = (bf16[192,128]{1,0:T(8,128)(2,1)S(1)}, bf16[192,128]{1,0:T(8,128)(2,1)S(1)}, u32[]{:S(2)}, u32[]{:S(2)}) collective-permute-start(bf16[192,128]{1,0:T(8,128)(2,1)S(1)} %get-tuple-element.84), channel_id=1, source_target_pairs={{0,3},{1,2},{2,1},{3,0},{4,7},{5,6},{6,5},{7,4},{8,11},{9,10},{10,... | collective-permute-start | bytes 147464 | tf_op jit(solution)/shard_map/cond/branch_1_fun/ppermute | solution.py:57
  18.5 4.6 %collective-permute-start.5 = (bf16[160,128]{1,0:T(8,128)(2,1)S(1)}, bf16[160,128]{1,0:T(8,128)(2,1)S(1)}, u32[]{:S(2)}, u32[]{:S(2)}) collective-permute-start(bf16[160,128]{1,0:T(8,128)(2,1)S(1)} %pad_maximum_fusion.3), channel_id=1, source_target_pairs={{0,9},{1,8},{2,11},{3,10},{4,13},{5,12},{6,15},{7,14},{8,1},{9,0},... | collective-permute-start | bytes 122888 | tf_op jit(solution)/shard_map/cond/branch_1_fun/ppermute | solution.py:57
  23.7 5.8 %collective-permute-start.7 = (bf16[384,128]{1,0:T(8,128)(2,1)S(1)}, bf16[384,128]{1,0:T(8,128)(2,1)S(1)}, u32[]{:S(2)}, u32[]{:S(2)}) collective-permute-start(bf16[384,128]{1,0:T(8,128)(2,1)S(1)} %bitcast.15), channel_id=1, source_target_pairs={{0,16},{1,17},{2,18},{3,19},{4,20},{5,21},{6,22},{7,23},{8,24},{9,... | collective-permute-start | bytes 294920 | tf_op jit(solution)/shard_map/ppermute | solution.py:57

commit v6 on v5

--- a/solution.py
+++ b/solution.py
@@ -375,8 +375,10 @@
         **cost,
     )(index, target, old)
 
+    valid = trap_index[0, 0] >= 0
     if crossing:
-        t_across = swap_pairs(transfer[:, :, :crossing], n_cols)
+        piece, now_cross, valid = lax.optimization_barrier((transfer[:, :, :crossing], now_cross, valid))
+        t_across = swap_pairs(piece, n_cols)
     other, now = lax.optimization_barrier((other, now))
     own_out, own_trap = call(
         own_kernel,
@@ -439,7 +441,7 @@
     if crossing:
         shapes = jax.eval_shape(sums, trap, keep, send, now)
         trap, block, *slots = lax.cond(
-            trap_index[0, 0] >= 0, sums, lambda *args: tuple(jnp.zeros(x.shape, x.dtype) for x in shapes), trap, keep, send, now
+            valid, sums, lambda *args: tuple(jnp.zeros(x.shape, x.dtype) for x in shapes), trap, keep, send, now
         )
     else:
         trap, block, *slots = sums(trap, keep, send, now)

time: 31.1 us -> 30.7 us (0.987)
  starting transfers between devices: 11.6 us -> 10.9 us
  waiting for transfers between devices: 8.12 us -> 8.67 us
    ppermute x9, starting transfers between devices: 11.6 us -> 10.9 us  [swap_pairs(): return lax.ppermute(x, AXES, [(i, i ^ mask) for i in range(n)])]
    ppermute x9, waiting for transfers between devices: 8.12 us -> 8.67 us  [swap_pairs(): return lax.ppermute(x, AXES, [(i, i ^ mask) for i in range(n)])]
where the time goes in v6:
time: 30.7 us; the launch traced here: 30.5 us
  starting transfers between devices  10.9 us (36%)
  waiting for transfers between devices  8.67 us (28%)
  Pallas kernels  5.88 us (19%)
  local copies, waits for them, and re-layouts  2.38 us (8%)
  between operations  1.37 us (4%)
  other arithmetic  1.21 us (4%)
    ppermute x9, starting transfers between devices, swap_pairs(): return lax.ppermute(x, AXES, [(i, i ^ mask) for i in range(n)])  10.9 us
    ppermute x9, waiting for transfers between devices, swap_pairs(): return lax.ppermute(x, AXES, [(i, i ^ mask) for i in range(n)])  8.67 us
    pallas_call x2, Pallas kernels, plan_slots(): call(functools.partial(slot_kernel, which), 'slots', [((rows, padded(n)),...  1.76 us
    pallas_call x1, Pallas kernels, body(): call(functools.partial(final_kernel, per_row, crossing), 'final', [((2, p...  1.3 us
    slice x1, local copies, waits for them, and re-layouts, body(): transfer[:, :, :crossing]  1.23 us
    convert_element_type x1, other arithmetic, body(): code = code.astype(BF)  1.11 us
    pallas_call x1, Pallas kernels, body(): call(functools.partial(mine_kernel, per_row), 'mine', [((2 * per_row, mod...  0.65 us
    pallas_call x1, Pallas kernels, body(): call(functools.partial(values_kernel, per_row, crossing), 'values', [((tr...  0.64 us
  transfers between devices with their start and end apart: 9, of which 7 were waited for; matrix products, arithmetic and copies ran while one was open for 8% of the time, Pallas kernels for 15%

profile of v6, /device:TPU:0, one launch (start us, length us, event | category | flops | bytes accessed | tf_op | source)
XLA Modules:
  0.0 30.5 jit_solution(13719889988612016583)
XLA Ops:
  0.6 0.0 copy-start.2
  0.6 0.0 copy-start.4
  0.7 0.0 copy-start.3
  0.7 0.0 copy-start
  0.7 1.1 %multiply_convert_fusion = bf16[64,1024]{1,0:T(8,128)(2,1)S(1)} fusion(f32[1024,64]{0,1:T(8,128)} %param.8), kind=kLoop, calls=%fused_computation.11 | loop fusion | flops 393216 | bytes 393216 | tf_op jit(solution)/shard_map/convert_element_type | solution.py:360
  1.8 3.0 %collective-permute-start.6 = (bf16[64,1024]{1,0:T(8,128)(2,1)S(1)}, bf16[64,1024]{1,0:T(8,128)(2,1)S(1)}, u32[]{:S(2)}, u32[]{:S(2)}) collective-permute-start(bf16[64,1024]{1,0:T(8,128)(2,1)S(1)} %multiply_convert_fusion), channel_id=1, source_target_pairs={{0,16},{1,17},{2,18},{3,19},{4,20},{5,21},{6,22},{7,23},{8,24},{9,... | collective-permute-start | bytes 393224 | tf_op jit(solution)/shard_map/ppermute | solution.py:57
  4.8 0.0 copy-done.2
  4.8 0.0 copy-done.4
  4.8 0.0 copy-done.3
  4.8 0.2 plan.1
  5.0 0.5 %slice.53 = s32[1,1]{0,1:T(1,128)} slice(s32[128,64]{0,1:T(8,128)S(1)} %copy-done.2), slice={[0:1], [0:1]} | slice | bytes 8 | tf_op jit(solution)/shard_map/slice | solution.py:378
  5.5 0.0 copy-start.1
  5.5 1.2 %slice.52 = bf16[2,256,768]{2,1,0:T(8,128)(2,1)S(1)} slice(bf16[2,256,1024]{2,1,0:T(8,128)(2,1)} %t_ref.7), slice={[0:2], [0:256], [0:768]} | slice | bytes 1572864 | tf_op jit(solution)/shard_map/slice | solution.py:380
  7.4 0.1 collective-permute-start.8
  7.5 0.0 copy-done
  7.5 0.0 copy-done.1
  7.5 0.5 %own.1 = (f32[256,128]{1,0:T(8,128)S(1)}, f32[64,128]{1,0:T(8,128)S(1)}) custom-call(f32[64,1024]{1,0:T(8,128)S(1)} %bitcast.11, s32[64,128]{1,0:T(8,128)S(1)} %bitcast.13, bf16[2,256,1024]{2,1,0:T(8,128)(2,1)S(1)} %copy-done), custom_call_target="tpu_custom_call" | custom-call | flops 1 | bytes 1 | tf_op jit(solution)/shard_map/own/pallas_call | solution.py:383
  8.1 0.3 collective-permute-done.6.code_ref
  8.3 0.6 %other.1 = (f32[128,128]{1,0:T(8,128)S(1)}, f32[256,128]{1,0:T(8,128)S(1)}, bf16[256,128]{1,0:T(8,128)(2,1)S(1)}) custom-call(bf16[64,1024]{1,0:T(8,128)(2,1)S(1)} %collective-permute-done.6.code_ref, s32[64,128]{1,0:T(8,128)S(1)} %bitcast.14, bf16[2,256,1024]{2,1,0:T(8,128)(2,1)S(1)} %copy-done, f32[256,128]{1,0:T(8,128)S(1)} %get-tuple-element.55.own_ref, ...), custom_call_target="tpu_custom_call" | custom-call | flops 30000001024 | bytes 1 | tf_op jit(solution)/shard_map/other/pallas_call | solution.py:392
  8.9 13.9 %conditional.1 = (f32[128,128]{1,0:T(8,128)S(1)}, f32[32,128]{1,0:T(8,128)S(1)}, s32[256,128]{1,0:T(8,128)S(1)}, s32[256,128]{1,0:T(8,128)S(1)}) conditional(s32[]{:T(128)} %convert_element_type.49, () %tuple.22, (f32[128,128]{1,0:T(8,128)S(1)}, s32[64,128]{1,0:T(8,128)S(1)}, bf16[256,128]{1,0:T(8,128)(2,1)S(1)}, f32[256,128]{1,0:T(8,128)S(1)}) %tuple.24), branch_computations={%region_0.1_spmd, %region_1.2_spmd} | conditional | flops 679937 | bytes 2711825 | solution.py:443
  9.0 0.1 collective-permute-start.1
  9.0 0.5 %collective-permute-start = (f32[128,128]{1,0:T(8,128)S(1)}, f32[128,128]{1,0:T(8,128)S(1)}, u32[]{:S(2)}, u32[]{:S(2)}) collective-permute-start(f32[128,128]{1,0:T(8,128)S(1)} %get-tuple-element.8), channel_id=1, source_target_pairs={{0,1},{1,0},{2,3},{3,2},{4,5},{5,4},{6,7},{7,6},{8,9},{9,8},{10,11... | collective-permute-start | bytes 196616 | tf_op jit(solution)/shard_map/cond/branch_1_fun/ppermute | solution.py:57
  9.5 0.7 %collective-permute-done.1 = bf16[256,128]{1,0:T(8,128)(2,1)S(1)} collective-permute-done((bf16[256,128]{1,0:T(8,128)(2,1)S(1)}, bf16[256,128]{1,0:T(8,128)(2,1)S(1)}, u32[]{:S(2)}, u32[]{:S(2)}) %collective-permute-start.1) | collective-permute-done | bytes 65568 | tf_op jit(solution)/shard_map/cond/branch_1_fun/ppermute | solution.py:57
  10.3 0.1 collective-permute-done
  10.5 1.8 %collective-permute-start.2 = (bf16[192,128]{1,0:T(8,128)(2,1)S(1)}, bf16[192,128]{1,0:T(8,128)(2,1)S(1)}, u32[]{:S(2)}, u32[]{:S(2)}) collective-permute-start(bf16[192,128]{1,0:T(8,128)(2,1)S(1)} %get-tuple-element.88), channel_id=1, source_target_pairs={{0,5},{1,4},{2,7},{3,6},{4,1},{5,0},{6,3},{7,2},{8,13},{9,12},{10,... | collective-permute-start | bytes 147464 | tf_op jit(solution)/shard_map/cond/branch_1_fun/ppermute | solution.py:57
  12.3 1.4 %collective-permute-start.4 = (bf16[192,128]{1,0:T(8,128)(2,1)S(1)}, bf16[192,128]{1,0:T(8,128)(2,1)S(1)}, u32[]{:S(2)}, u32[]{:S(2)}) collective-permute-start(bf16[192,128]{1,0:T(8,128)(2,1)S(1)} %get-tuple-element.89), channel_id=1, source_target_pairs={{0,6},{1,7},{2,4},{3,5},{4,2},{5,3},{6,0},{7,1},{8,14},{9,15},{10,... | collective-permute-start | bytes 147464 | tf_op jit(solution)/shard_map/cond/branch_1_fun/ppermute | solution.py:57
  13.7 0.0 collective-permute-start.3
  13.7 0.9 %slots.2 = (s32[256,128]{1,0:T(8,128)S(1)}, s32[256,128]{1,0:T(8,128)S(1)}) custom-call(s32[64,128]{1,0:T(8,128)S(1)} %get-tuple-element.13.now_ref), custom_call_target="tpu_custom_call" | custom-call | flops 1 | bytes 1 | tf_op jit(solution)/shard_map/cond/branch_1_fun/slots/pallas_call | solution.py:405
  14.6 0.0 collective-permute-done.2
  14.6 2.8 %collective-permute-done.4 = bf16[192,128]{1,0:T(8,128)(2,1)S(1)} collective-permute-done((bf16[192,128]{1,0:T(8,128)(2,1)S(1)}, bf16[192,128]{1,0:T(8,128)(2,1)S(1)}, u32[]{:S(2)}, u32[]{:S(2)}) %collective-permute-start.4) | collective-permute-done | bytes 49184 | tf_op jit(solution)/shard_map/cond/branch_1_fun/ppermute | solution.py:57
  17.4 0.8 %collective-permute-done.3 = bf16[192,128]{1,0:T(8,128)(2,1)S(1)} collective-permute-done((bf16[192,128]{1,0:T(8,128)(2,1)S(1)}, bf16[192,128]{1,0:T(8,128)(2,1)S(1)}, u32[]{:S(2)}, u32[]{:S(2)}) %collective-permute-start.3) | collective-permute-done | bytes 49184 | tf_op jit(solution)/shard_map/cond/branch_1_fun/ppermute | solution.py:57
  18.3 2.4 %collective-permute-start.5 = (bf16[160,128]{1,0:T(8,128)(2,1)S(1)}, bf16[160,128]{1,0:T(8,128)(2,1)S(1)}, u32[]{:S(2)}, u32[]{:S(2)}) collective-permute-start(bf16[160,128]{1,0:T(8,128)(2,1)S(1)} %pad_maximum_fusion.3), channel_id=1, source_target_pairs={{0,9},{1,8},{2,11},{3,10},{4,13},{5,12},{6,15},{7,14},{8,1},{9,0},... | collective-permute-start | bytes 122888 | tf_op jit(solution)/shard_map/cond/branch_1_fun/ppermute | solution.py:57
  20.7 2.1 %collective-permute-done.5 = bf16[160,128]{1,0:T(8,128)(2,1)S(1)} collective-permute-done((bf16[160,128]{1,0:T(8,128)(2,1)S(1)}, bf16[160,128]{1,0:T(8,128)(2,1)S(1)}, u32[]{:S(2)}, u32[]{:S(2)}) %collective-permute-start.5) | collective-permute-done | bytes 40992 | tf_op jit(solution)/shard_map/cond/branch_1_fun/ppermute | solution.py:57
  22.8 0.6 %values.1 = (f32[64,128]{1,0:T(8,128)S(1)}, bf16[1,384,128]{2,1,0:T(8,128)(2,1)S(1)}) custom-call(f32[128,128]{1,0:T(8,128)S(1)} %get-tuple-element.63.trap_ref, bf16[2,256,1024]{2,1,0:T(8,128)(2,1)S(1)} %copy-done, s32[64,128]{1,0:T(8,128)S(1)} %get-tuple-element.64.refs_0_.idx_ref, f32[64,128]{1,0:T(8,128)S(1)} %get-tuple-element.65.refs_1_, ...), custom_call_target="tpu_custom_call" | custom-call | flops 1 | bytes 1 | tf_op jit(solution)/shard_map/values/pallas_call | solution.py:450
  23.5 1.6 %collective-permute-start.7 = (bf16[384,128]{1,0:T(8,128)(2,1)S(1)}, bf16[384,128]{1,0:T(8,128)(2,1)S(1)}, u32[]{:S(2)}, u32[]{:S(2)}) collective-permute-start(bf16[384,128]{1,0:T(8,128)(2,1)S(1)} %bitcast.15), channel_id=1, source_target_pairs={{0,16},{1,17},{2,18},{3,19},{4,20},{5,21},{6,22},{7,23},{8,24},{9,... | collective-permute-start | bytes 294920 | tf_op jit(solution)/shard_map/ppermute | solution.py:57
  25.1 0.2 far.1
  25.3 0.7 %mine.1.mine_ref = f32[128,1024]{1,0:T(8,128)S(1)} custom-call(f32[64,128]{1,0:T(8,128)S(1)} %get-tuple-element.71.value_ref, s32[64,128]{1,0:T(8,128)S(1)} %get-tuple-element.64.refs_0_.idx_ref, s32[256,128]{1,0:T(8,128)S(1)} %get-tuple-element.72.slot_ref, bf16[2,256,1024]{2,1,0:T(8,128)(2,1)S(1)} %copy-done), custom_call_target="tpu_custom_call" | custom-call | flops 1 | bytes 1 | tf_op jit(solution)/shard_map/mine/pallas_call | solution.py:461
  25.9 0.9 %slots.3.refs_0_ = s32[256,128]{1,0:T(8,128)S(1)} custom-call(s32[64,128]{1,0:T(8,128)S(1)} %get-tuple-element.76.now_ref), custom_call_target="tpu_custom_call" | custom-call | flops 1 | bytes 1 | tf_op jit(solution)/shard_map/slots/pallas_call | solution.py:405
  26.8 0.6 %copy.8 = bf16[16,2,128]{2,1,0:T(2,128)(2,1)} copy(bf16[16,2,128]{2,0,1:T(8,128)(2,1)S(1)} %bitcast.19) | data formatting | bytes 16384
  27.4 1.8 %collective-permute-done.7 = bf16[384,128]{1,0:T(8,128)(2,1)S(1)} collective-permute-done((bf16[384,128]{1,0:T(8,128)(2,1)S(1)}, bf16[384,128]{1,0:T(8,128)(2,1)S(1)}, u32[]{:S(2)}, u32[]{:S(2)}) %collective-permute-start.7) | collective-permute-done | bytes 98336 | tf_op jit(solution)/shard_map/ppermute | solution.py:57
  29.2 0.0 collective-permute-done.8.refs_1_
  29.2 1.3 %final.1 = (f32[2,64,1024]{2,1,0:T(8,128)}, f32[64,128]{1,0:T(8,128)}) custom-call(f32[64,128]{1,0:T(8,128)S(1)} %get-tuple-element.62.old_ref, f32[128,1024]{1,0:T(8,128)S(1)} %mine.1.mine_ref, bf16[1,384,128]{2,1,0:T(8,128)(2,1)S(1)} %get-tuple-element.75.sent_ref, bf16[1,384,128]{2,1,0:T(8,128)(2,1)S(1)} %bitcast.16, s32[256,128]{1,0:T(8,128)S(1)} %slots.3.refs_0_, ...), custom_call_target="tpu_custom_call" | custom-call | flops 1 | bytes 1 | tf_op jit(solution)/shard_map/final/pallas_call | solution.py:474
  (10 shorter events, 0.1 us)
Async XLA Ops:
  0.6 4.2 %copy-start.2 = (s32[128,64]{0,1:T(8,128)S(1)}, s32[128,64]{0,1:T(8,128)}, u32[]{:S(2)}) copy-start(s32[128,64]{0,1:T(8,128)} %param.9) | copy-start | bytes 98308
  0.6 4.2 %copy-start.4 = (f32[128,64]{0,1:T(8,128)S(1)}, f32[128,64]{0,1:T(8,128)}, u32[]{:S(2)}) copy-start(f32[128,64]{0,1:T(8,128)} %param.11) | copy-start | bytes 98308
  0.7 4.2 %copy-start.3 = (s32[128,64]{0,1:T(8,128)S(1)}, s32[128,64]{0,1:T(8,128)}, u32[]{:S(2)}) copy-start(s32[128,64]{0,1:T(8,128)} %param.10) | copy-start | bytes 98308
  0.7 6.9 %copy-start = (bf16[2,256,1024]{2,1,0:T(8,128)(2,1)S(1)}, bf16[2,256,1024]{2,1,0:T(8,128)(2,1)}, u32[]{:S(2)}) copy-start(bf16[2,256,1024]{2,1,0:T(8,128)(2,1)} %t_ref.7) | copy-start | bytes 3145732
  1.8 6.5 %collective-permute-start.6 = (bf16[64,1024]{1,0:T(8,128)(2,1)S(1)}, bf16[64,1024]{1,0:T(8,128)(2,1)S(1)}, u32[]{:S(2)}, u32[]{:S(2)}) collective-permute-start(bf16[64,1024]{1,0:T(8,128)(2,1)S(1)} %multiply_convert_fusion), channel_id=1, source_target_pairs={{0,16},{1,17},{2,18},{3,19},{4,20},{5,21},{6,22},{7,23},{8,24},{9,... | collective-permute-start | bytes 393224 | tf_op jit(solution)/shard_map/ppermute | solution.py:57
  5.5 2.0 %copy-start.1 = (f32[1024,64]{0,1:T(8,128)S(1)}, f32[1024,64]{0,1:T(8,128)}, u32[]{:S(2)}) copy-start(f32[1024,64]{0,1:T(8,128)} %param.8) | copy-start | bytes 786436
  7.4 21.8 %collective-permute-start.8 = (bf16[2,256,768]{2,1,0:T(8,128)(2,1)S(1)}, bf16[2,256,768]{2,1,0:T(8,128)(2,1)S(1)}, u32[]{:S(2)}, u32[]{:S(2)}) collective-permute-start(bf16[2,256,768]{2,1,0:T(8,128)(2,1)S(1)} %slice.52), channel_id=1, source_target_pairs={{0,16},{1,17},{2,18},{3,19},{4,20},{5,21},{6,22},{7,23},{8,24},{9,... | collective-permute-start | bytes 2359304 | tf_op jit(solution)/shard_map/ppermute | solution.py:57
  9.0 1.3 %collective-permute-start.1 = (bf16[256,128]{1,0:T(8,128)(2,1)S(1)}, bf16[256,128]{1,0:T(8,128)(2,1)S(1)}, u32[]{:S(2)}, u32[]{:S(2)}) collective-permute-start(bf16[256,128]{1,0:T(8,128)(2,1)S(1)} %get-tuple-element.12), channel_id=1, source_target_pairs={{0,1},{1,0},{2,3},{3,2},{4,5},{5,4},{6,7},{7,6},{8,9},{9,8},{10,11... | collective-permute-start | bytes 196616 | tf_op jit(solution)/shard_map/cond/branch_1_fun/ppermute | solution.py:57
  9.0 1.4 %collective-permute-start = (f32[128,128]{1,0:T(8,128)S(1)}, f32[128,128]{1,0:T(8,128)S(1)}, u32[]{:S(2)}, u32[]{:S(2)}) collective-permute-start(f32[128,128]{1,0:T(8,128)S(1)} %get-tuple-element.8), channel_id=1, source_target_pairs={{0,1},{1,0},{2,3},{3,2},{4,5},{5,4},{6,7},{7,6},{8,9},{9,8},{10,11... | collective-permute-start | bytes 196616 | tf_op jit(solution)/shard_map/cond/branch_1_fun/ppermute | solution.py:57
  10.5 4.1 %collective-permute-start.2 = (bf16[192,128]{1,0:T(8,128)(2,1)S(1)}, bf16[192,128]{1,0:T(8,128)(2,1)S(1)}, u32[]{:S(2)}, u32[]{:S(2)}) collective-permute-start(bf16[192,128]{1,0:T(8,128)(2,1)S(1)} %get-tuple-element.88), channel_id=1, source_target_pairs={{0,5},{1,4},{2,7},{3,6},{4,1},{5,0},{6,3},{7,2},{8,13},{9,12},{10,... | collective-permute-start | bytes 147464 | tf_op jit(solution)/shard_map/cond/branch_1_fun/ppermute | solution.py:57
  12.3 5.1 %collective-permute-start.4 = (bf16[192,128]{1,0:T(8,128)(2,1)S(1)}, bf16[192,128]{1,0:T(8,128)(2,1)S(1)}, u32[]{:S(2)}, u32[]{:S(2)}) collective-permute-start(bf16[192,128]{1,0:T(8,128)(2,1)S(1)} %get-tuple-element.89), channel_id=1, source_target_pairs={{0,6},{1,7},{2,4},{3,5},{4,2},{5,3},{6,0},{7,1},{8,14},{9,15},{10,... | collective-permute-start | bytes 147464 | tf_op jit(solution)/shard_map/cond/branch_1_fun/ppermute | solution.py:57
  13.7 4.5 %collective-permute-start.3 = (bf16[192,128]{1,0:T(8,128)(2,1)S(1)}, bf16[192,128]{1,0:T(8,128)(2,1)S(1)}, u32[]{:S(2)}, u32[]{:S(2)}) collective-permute-start(bf16[192,128]{1,0:T(8,128)(2,1)S(1)} %get-tuple-element.90), channel_id=1, source_target_pairs={{0,3},{1,2},{2,1},{3,0},{4,7},{5,6},{6,5},{7,4},{8,11},{9,10},{10,... | collective-permute-start | bytes 147464 | tf_op jit(solution)/shard_map/cond/branch_1_fun/ppermute | solution.py:57
  18.3 4.6 %collective-permute-start.5 = (bf16[160,128]{1,0:T(8,128)(2,1)S(1)}, bf16[160,128]{1,0:T(8,128)(2,1)S(1)}, u32[]{:S(2)}, u32[]{:S(2)}) collective-permute-start(bf16[160,128]{1,0:T(8,128)(2,1)S(1)} %pad_maximum_fusion.3), channel_id=1, source_target_pairs={{0,9},{1,8},{2,11},{3,10},{4,13},{5,12},{6,15},{7,14},{8,1},{9,0},... | collective-permute-start | bytes 122888 | tf_op jit(solution)/shard_map/cond/branch_1_fun/ppermute | solution.py:57
  23.5 5.7 %collective-permute-start.7 = (bf16[384,128]{1,0:T(8,128)(2,1)S(1)}, bf16[384,128]{1,0:T(8,128)(2,1)S(1)}, u32[]{:S(2)}, u32[]{:S(2)}) collective-permute-start(bf16[384,128]{1,0:T(8,128)(2,1)S(1)} %bitcast.15), channel_id=1, source_target_pairs={{0,16},{1,17},{2,18},{3,19},{4,20},{5,21},{6,22},{7,23},{8,24},{9,... | collective-permute-start | bytes 294920 | tf_op jit(solution)/shard_map/ppermute | solution.py:57

commit v7 on v6

--- a/solution.py
+++ b/solution.py
@@ -428,10 +428,14 @@
                 for i, b in enumerate(group):
                     if (way >> (len(group) - 1 - i)) & 1:
                         mask ^= masks[b]
-                load = jnp.concatenate([short, whole[way * part:(way + 1) * part].astype(BF)], axis=0)
-                got = swap_pairs(load, mask)
-                traps_of.append(got[:short.shape[0]])
-                fields.append(got[short.shape[0]:])
+                away = whole[way * part:(way + 1) * part].astype(BF)
+                if mask & 1:
+                    got = swap_pairs(jnp.concatenate([short, away], axis=0), mask)
+                    traps_of.append(got[:short.shape[0]])
+                    fields.append(got[short.shape[0]:])
+                else:
+                    traps_of.append(swap_pairs(short, mask | 1))
+                    fields.append(swap_pairs(away, mask))
             trap = tree_sum([x.astype(F32) for x in traps_of])
             block = tree_sum([x.astype(F32) for x in fields])
             if group[0] == 1:

time: 30.7 us -> 30.1 us (0.980)
  waiting for transfers between devices: 8.67 us -> 5.31 us
  starting transfers between devices: 10.9 us -> 13.6 us
    ppermute x9 -> x10, waiting for transfers between devices: 8.67 us -> 5.31 us  [swap_pairs(): return lax.ppermute(x, AXES, [(i, i ^ mask) for i in range(n)])]
    ppermute x9 -> x10, starting transfers between devices: 10.9 us -> 13.6 us  [swap_pairs(): return lax.ppermute(x, AXES, [(i, i ^ mask) for i in range(n)])]
  transfers between devices with their start and end apart: 9 -> 10, of which waited for: 7 -> 6; matrix products, arithmetic and copies ran while one was open for 8% -> 8% of each run, Pallas kernels for 15% -> 15%
where the time goes in v7:
time: 30.1 us; the launch traced here: 29.9 us
  starting transfers between devices  13.6 us (45%)
  Pallas kernels  5.88 us (20%)
  waiting for transfers between devices  5.31 us (18%)
  local copies, waits for them, and re-layouts  2.38 us (8%)
  between operations  1.37 us (5%)
  other arithmetic  1.2 us (4%)
    ppermute x10, starting transfers between devices, swap_pairs(): return lax.ppermute(x, AXES, [(i, i ^ mask) for i in range(n)])  13.6 us
    ppermute x10, waiting for transfers between devices, swap_pairs(): return lax.ppermute(x, AXES, [(i, i ^ mask) for i in range(n)])  5.31 us
    pallas_call x2, Pallas kernels, plan_slots(): call(functools.partial(slot_kernel, which), 'slots', [((rows, padded(n)),...  1.76 us
    pallas_call x1, Pallas kernels, body(): call(functools.partial(final_kernel, per_row, crossing), 'final', [((2, p...  1.3 us
    slice x1, local copies, waits for them, and re-layouts, body(): transfer[:, :, :crossing]  1.23 us
    convert_element_type x1, other arithmetic, body(): code = code.astype(BF)  1.11 us
    pallas_call x1, Pallas kernels, body(): call(functools.partial(mine_kernel, per_row), 'mine', [((2 * per_row, mod...  0.65 us
    pallas_call x1, Pallas kernels, body(): call(functools.partial(values_kernel, per_row, crossing), 'values', [((tr...  0.64 us
  transfers between devices with their start and end apart: 10, of which 6 were waited for; matrix products, arithmetic and copies ran while one was open for 8% of the time, Pallas kernels for 15%

profile of v7, /device:TPU:0, one launch (start us, length us, event | category | flops | bytes accessed | tf_op | source)
XLA Modules:
  0.0 29.9 jit_solution(15328473277390230745)
XLA Ops:
  0.6 0.0 copy-start.2
  0.6 0.0 copy-start.4
  0.7 0.0 copy-start.3
  0.7 0.0 copy-start
  0.7 1.1 %multiply_convert_fusion = bf16[64,1024]{1,0:T(8,128)(2,1)S(1)} fusion(f32[1024,64]{0,1:T(8,128)} %param.8), kind=kLoop, calls=%fused_computation.10 | loop fusion | flops 393216 | bytes 393216 | tf_op jit(solution)/shard_map/convert_element_type | solution.py:360
  1.8 3.0 %collective-permute-start.7 = (bf16[64,1024]{1,0:T(8,128)(2,1)S(1)}, bf16[64,1024]{1,0:T(8,128)(2,1)S(1)}, u32[]{:S(2)}, u32[]{:S(2)}) collective-permute-start(bf16[64,1024]{1,0:T(8,128)(2,1)S(1)} %multiply_convert_fusion), channel_id=1, source_target_pairs={{0,16},{1,17},{2,18},{3,19},{4,20},{5,21},{6,22},{7,23},{8,24},{9,... | collective-permute-start | bytes 393224 | tf_op jit(solution)/shard_map/ppermute | solution.py:57
  4.8 0.0 copy-done.2
  4.8 0.0 copy-done.4
  4.8 0.0 copy-done.3
  4.8 0.2 plan.1
  5.0 0.5 %slice.47 = s32[1,1]{0,1:T(1,128)} slice(s32[128,64]{0,1:T(8,128)S(1)} %copy-done.2), slice={[0:1], [0:1]} | slice | bytes 8 | tf_op jit(solution)/shard_map/slice | solution.py:378
  5.5 0.0 copy-start.1
  5.5 1.2 %slice.46 = bf16[2,256,768]{2,1,0:T(8,128)(2,1)S(1)} slice(bf16[2,256,1024]{2,1,0:T(8,128)(2,1)} %t_ref.7), slice={[0:2], [0:256], [0:768]} | slice | bytes 1572864 | tf_op jit(solution)/shard_map/slice | solution.py:380
  7.4 0.1 collective-permute-start.9
  7.5 0.0 copy-done
  7.5 0.0 copy-done.1
  7.5 0.5 %own.1 = (f32[256,128]{1,0:T(8,128)S(1)}, f32[64,128]{1,0:T(8,128)S(1)}) custom-call(f32[64,1024]{1,0:T(8,128)S(1)} %bitcast.11, s32[64,128]{1,0:T(8,128)S(1)} %bitcast.13, bf16[2,256,1024]{2,1,0:T(8,128)(2,1)S(1)} %copy-done), custom_call_target="tpu_custom_call" | custom-call | flops 1 | bytes 1 | tf_op jit(solution)/shard_map/own/pallas_call | solution.py:383
  8.1 0.3 collective-permute-done.7.code_ref
  8.3 0.6 %other.1 = (f32[128,128]{1,0:T(8,128)S(1)}, f32[256,128]{1,0:T(8,128)S(1)}, bf16[256,128]{1,0:T(8,128)(2,1)S(1)}) custom-call(bf16[64,1024]{1,0:T(8,128)(2,1)S(1)} %collective-permute-done.7.code_ref, s32[64,128]{1,0:T(8,128)S(1)} %bitcast.14, bf16[2,256,1024]{2,1,0:T(8,128)(2,1)S(1)} %copy-done, f32[256,128]{1,0:T(8,128)S(1)} %get-tuple-element.55.own_ref, ...), custom_call_target="tpu_custom_call" | custom-call | flops 30000001024 | bytes 1 | tf_op jit(solution)/shard_map/other/pallas_call | solution.py:392
  8.9 14.0 %conditional.1 = (f32[128,128]{1,0:T(8,128)S(1)}, f32[32,128]{1,0:T(8,128)S(1)}, s32[256,128]{1,0:T(8,128)S(1)}, s32[256,128]{1,0:T(8,128)S(1)}) conditional(s32[]{:T(128)} %convert_element_type.49, () %tuple.22, (f32[128,128]{1,0:T(8,128)S(1)}, s32[64,128]{1,0:T(8,128)S(1)}, bf16[256,128]{1,0:T(8,128)(2,1)S(1)}, f32[256,128]{1,0:T(8,128)S(1)}) %tuple.24), branch_computations={%region_0.1_spmd, %region_1.2_spmd} | conditional | flops 606209 | bytes 2646329 | solution.py:447
  9.0 0.1 collective-permute-start.1
  9.0 0.5 %collective-permute-start = (f32[128,128]{1,0:T(8,128)S(1)}, f32[128,128]{1,0:T(8,128)S(1)}, u32[]{:S(2)}, u32[]{:S(2)}) collective-permute-start(f32[128,128]{1,0:T(8,128)S(1)} %get-tuple-element.8), channel_id=1, source_target_pairs={{0,1},{1,0},{2,3},{3,2},{4,5},{5,4},{6,7},{7,6},{8,9},{9,8},{10,11... | collective-permute-start | bytes 196616 | tf_op jit(solution)/shard_map/cond/branch_1_fun/ppermute | solution.py:57
  9.5 0.7 %collective-permute-done.1 = bf16[256,128]{1,0:T(8,128)(2,1)S(1)} collective-permute-done((bf16[256,128]{1,0:T(8,128)(2,1)S(1)}, bf16[256,128]{1,0:T(8,128)(2,1)S(1)}, u32[]{:S(2)}, u32[]{:S(2)}) %collective-permute-start.1) | collective-permute-done | bytes 65568 | tf_op jit(solution)/shard_map/cond/branch_1_fun/ppermute | solution.py:57
  10.3 0.1 collective-permute-done
  10.5 1.8 %collective-permute-start.2 = (bf16[192,128]{1,0:T(8,128)(2,1)S(1)}, bf16[192,128]{1,0:T(8,128)(2,1)S(1)}, u32[]{:S(2)}, u32[]{:S(2)}) collective-permute-start(bf16[192,128]{1,0:T(8,128)(2,1)S(1)} %get-tuple-element.88), channel_id=1, source_target_pairs={{0,5},{1,4},{2,7},{3,6},{4,1},{5,0},{6,3},{7,2},{8,13},{9,12},{10,... | collective-permute-start | bytes 147464 | tf_op jit(solution)/shard_map/cond/branch_1_fun/ppermute | solution.py:57
  12.3 1.3 %collective-permute-start.3 = (bf16[192,128]{1,0:T(8,128)(2,1)S(1)}, bf16[192,128]{1,0:T(8,128)(2,1)S(1)}, u32[]{:S(2)}, u32[]{:S(2)}) collective-permute-start(bf16[192,128]{1,0:T(8,128)(2,1)S(1)} %get-tuple-element.89), channel_id=1, source_target_pairs={{0,3},{1,2},{2,1},{3,0},{4,7},{5,6},{6,5},{7,4},{8,11},{9,10},{10,... | collective-permute-start | bytes 147464 | tf_op jit(solution)/shard_map/cond/branch_1_fun/ppermute | solution.py:57
  13.5 0.3 collective-permute-start.5
  13.8 2.3 %collective-permute-start.4 = (bf16[128,128]{1,0:T(8,128)(2,1)S(1)}, bf16[128,128]{1,0:T(8,128)(2,1)S(1)}, u32[]{:S(2)}, u32[]{:S(2)}) collective-permute-start(bf16[128,128]{1,0:T(8,128)(2,1)S(1)} %add.20), channel_id=1, source_target_pairs={{0,7},{1,6},{2,5},{3,4},{4,3},{5,2},{6,1},{7,0},{8,15},{9,14},{10,... | collective-permute-start | bytes 98312 | tf_op jit(solution)/shard_map/cond/branch_1_fun/ppermute | solution.py:57
  16.2 0.9 %slots.2 = (s32[256,128]{1,0:T(8,128)S(1)}, s32[256,128]{1,0:T(8,128)S(1)}) custom-call(s32[64,128]{1,0:T(8,128)S(1)} %get-tuple-element.13.now_ref), custom_call_target="tpu_custom_call" | custom-call | flops 1 | bytes 1 | tf_op jit(solution)/shard_map/cond/branch_1_fun/slots/pallas_call | solution.py:405
  17.0 1.2 %collective-permute-done.5 = bf16[64,128]{1,0:T(8,128)(2,1)S(1)} collective-permute-done((bf16[64,128]{1,0:T(8,128)(2,1)S(1)}, bf16[64,128]{1,0:T(8,128)(2,1)S(1)}, u32[]{:S(2)}, u32[]{:S(2)}) %collective-permute-start.5) | collective-permute-done | bytes 16416 | tf_op jit(solution)/shard_map/cond/branch_1_fun/ppermute | solution.py:57
  18.2 0.0 collective-permute-done.2
  18.3 0.0 collective-permute-done.3
  18.3 0.0 collective-permute-done.4
  18.3 2.5 %collective-permute-start.6 = (bf16[160,128]{1,0:T(8,128)(2,1)S(1)}, bf16[160,128]{1,0:T(8,128)(2,1)S(1)}, u32[]{:S(2)}, u32[]{:S(2)}) collective-permute-start(bf16[160,128]{1,0:T(8,128)(2,1)S(1)} %pad_maximum_fusion.2), channel_id=1, source_target_pairs={{0,9},{1,8},{2,11},{3,10},{4,13},{5,12},{6,15},{7,14},{8,1},{9,0},... | collective-permute-start | bytes 122888 | tf_op jit(solution)/shard_map/cond/branch_1_fun/ppermute | solution.py:57
  20.9 2.1 %collective-permute-done.6 = bf16[160,128]{1,0:T(8,128)(2,1)S(1)} collective-permute-done((bf16[160,128]{1,0:T(8,128)(2,1)S(1)}, bf16[160,128]{1,0:T(8,128)(2,1)S(1)}, u32[]{:S(2)}, u32[]{:S(2)}) %collective-permute-start.6) | collective-permute-done | bytes 40992 | tf_op jit(solution)/shard_map/cond/branch_1_fun/ppermute | solution.py:57
  22.9 0.6 %values.1 = (f32[64,128]{1,0:T(8,128)S(1)}, bf16[1,384,128]{2,1,0:T(8,128)(2,1)S(1)}) custom-call(f32[128,128]{1,0:T(8,128)S(1)} %get-tuple-element.63.trap_ref, bf16[2,256,1024]{2,1,0:T(8,128)(2,1)S(1)} %copy-done, s32[64,128]{1,0:T(8,128)S(1)} %get-tuple-element.64.refs_0_.idx_ref, f32[64,128]{1,0:T(8,128)S(1)} %get-tuple-element.65.refs_1_, ...), custom_call_target="tpu_custom_call" | custom-call | flops 1 | bytes 1 | tf_op jit(solution)/shard_map/values/pallas_call | solution.py:454
  23.6 1.8 %collective-permute-start.8 = (bf16[384,128]{1,0:T(8,128)(2,1)S(1)}, bf16[384,128]{1,0:T(8,128)(2,1)S(1)}, u32[]{:S(2)}, u32[]{:S(2)}) collective-permute-start(bf16[384,128]{1,0:T(8,128)(2,1)S(1)} %bitcast.15), channel_id=1, source_target_pairs={{0,16},{1,17},{2,18},{3,19},{4,20},{5,21},{6,22},{7,23},{8,24},{9,... | collective-permute-start | bytes 294920 | tf_op jit(solution)/shard_map/ppermute | solution.py:57
  25.3 0.2 far.1
  25.5 0.7 %mine.1.mine_ref = f32[128,1024]{1,0:T(8,128)S(1)} custom-call(f32[64,128]{1,0:T(8,128)S(1)} %get-tuple-element.71.value_ref, s32[64,128]{1,0:T(8,128)S(1)} %get-tuple-element.64.refs_0_.idx_ref, s32[256,128]{1,0:T(8,128)S(1)} %get-tuple-element.72.slot_ref, bf16[2,256,1024]{2,1,0:T(8,128)(2,1)S(1)} %copy-done), custom_call_target="tpu_custom_call" | custom-call | flops 1 | bytes 1 | tf_op jit(solution)/shard_map/mine/pallas_call | solution.py:465
  26.2 0.9 %slots.3.refs_0_ = s32[256,128]{1,0:T(8,128)S(1)} custom-call(s32[64,128]{1,0:T(8,128)S(1)} %get-tuple-element.76.now_ref), custom_call_target="tpu_custom_call" | custom-call | flops 1 | bytes 1 | tf_op jit(solution)/shard_map/slots/pallas_call | solution.py:405
  27.1 0.6 %copy.8 = bf16[16,2,128]{2,1,0:T(2,128)(2,1)} copy(bf16[16,2,128]{2,0,1:T(8,128)(2,1)S(1)} %bitcast.19) | data formatting | bytes 16384
  27.7 0.9 %collective-permute-done.8 = bf16[384,128]{1,0:T(8,128)(2,1)S(1)} collective-permute-done((bf16[384,128]{1,0:T(8,128)(2,1)S(1)}, bf16[384,128]{1,0:T(8,128)(2,1)S(1)}, u32[]{:S(2)}, u32[]{:S(2)}) %collective-permute-start.8) | collective-permute-done | bytes 98336 | tf_op jit(solution)/shard_map/ppermute | solution.py:57
  28.6 0.0 collective-permute-done.9.refs_1_
  28.6 1.3 %final.1 = (f32[2,64,1024]{2,1,0:T(8,128)}, f32[64,128]{1,0:T(8,128)}) custom-call(f32[64,128]{1,0:T(8,128)S(1)} %get-tuple-element.62.old_ref, f32[128,1024]{1,0:T(8,128)S(1)} %mine.1.mine_ref, bf16[1,384,128]{2,1,0:T(8,128)(2,1)S(1)} %get-tuple-element.75.sent_ref, bf16[1,384,128]{2,1,0:T(8,128)(2,1)S(1)} %bitcast.16, s32[256,128]{1,0:T(8,128)S(1)} %slots.3.refs_0_, ...), custom_call_target="tpu_custom_call" | custom-call | flops 1 | bytes 1 | tf_op jit(solution)/shard_map/final/pallas_call | solution.py:478
  (10 shorter events, 0.1 us)
Async XLA Ops:
  0.6 4.2 %copy-start.2 = (s32[128,64]{0,1:T(8,128)S(1)}, s32[128,64]{0,1:T(8,128)}, u32[]{:S(2)}) copy-start(s32[128,64]{0,1:T(8,128)} %param.9) | copy-start | bytes 98308
  0.6 4.2 %copy-start.4 = (f32[128,64]{0,1:T(8,128)S(1)}, f32[128,64]{0,1:T(8,128)}, u32[]{:S(2)}) copy-start(f32[128,64]{0,1:T(8,128)} %param.11) | copy-start | bytes 98308
  0.7 4.2 %copy-start.3 = (s32[128,64]{0,1:T(8,128)S(1)}, s32[128,64]{0,1:T(8,128)}, u32[]{:S(2)}) copy-start(s32[128,64]{0,1:T(8,128)} %param.10) | copy-start | bytes 98308
  0.7 6.9 %copy-start = (bf16[2,256,1024]{2,1,0:T(8,128)(2,1)S(1)}, bf16[2,256,1024]{2,1,0:T(8,128)(2,1)}, u32[]{:S(2)}) copy-start(bf16[2,256,1024]{2,1,0:T(8,128)(2,1)} %t_ref.7) | copy-start | bytes 3145732
  1.8 6.5 %collective-permute-start.7 = (bf16[64,1024]{1,0:T(8,128)(2,1)S(1)}, bf16[64,1024]{1,0:T(8,128)(2,1)S(1)}, u32[]{:S(2)}, u32[]{:S(2)}) collective-permute-start(bf16[64,1024]{1,0:T(8,128)(2,1)S(1)} %multiply_convert_fusion), channel_id=1, source_target_pairs={{0,16},{1,17},{2,18},{3,19},{4,20},{5,21},{6,22},{7,23},{8,24},{9,... | collective-permute-start | bytes 393224 | tf_op jit(solution)/shard_map/ppermute | solution.py:57
  5.5 2.0 %copy-start.1 = (f32[1024,64]{0,1:T(8,128)S(1)}, f32[1024,64]{0,1:T(8,128)}, u32[]{:S(2)}) copy-start(f32[1024,64]{0,1:T(8,128)} %param.8) | copy-start | bytes 786436
  7.4 21.2 %collective-permute-start.9 = (bf16[2,256,768]{2,1,0:T(8,128)(2,1)S(1)}, bf16[2,256,768]{2,1,0:T(8,128)(2,1)S(1)}, u32[]{:S(2)}, u32[]{:S(2)}) collective-permute-start(bf16[2,256,768]{2,1,0:T(8,128)(2,1)S(1)} %slice.46), channel_id=1, source_target_pairs={{0,16},{1,17},{2,18},{3,19},{4,20},{5,21},{6,22},{7,23},{8,24},{9,... | collective-permute-start | bytes 2359304 | tf_op jit(solution)/shard_map/ppermute | solution.py:57
  9.0 1.3 %collective-permute-start.1 = (bf16[256,128]{1,0:T(8,128)(2,1)S(1)}, bf16[256,128]{1,0:T(8,128)(2,1)S(1)}, u32[]{:S(2)}, u32[]{:S(2)}) collective-permute-start(bf16[256,128]{1,0:T(8,128)(2,1)S(1)} %get-tuple-element.12), channel_id=1, source_target_pairs={{0,1},{1,0},{2,3},{3,2},{4,5},{5,4},{6,7},{7,6},{8,9},{9,8},{10,11... | collective-permute-start | bytes 196616 | tf_op jit(solution)/shard_map/cond/branch_1_fun/ppermute | solution.py:57
  9.0 1.4 %collective-permute-start = (f32[128,128]{1,0:T(8,128)S(1)}, f32[128,128]{1,0:T(8,128)S(1)}, u32[]{:S(2)}, u32[]{:S(2)}) collective-permute-start(f32[128,128]{1,0:T(8,128)S(1)} %get-tuple-element.8), channel_id=1, source_target_pairs={{0,1},{1,0},{2,3},{3,2},{4,5},{5,4},{6,7},{7,6},{8,9},{9,8},{10,11... | collective-permute-start | bytes 196616 | tf_op jit(solution)/shard_map/cond/branch_1_fun/ppermute | solution.py:57
  10.5 7.8 %collective-permute-start.2 = (bf16[192,128]{1,0:T(8,128)(2,1)S(1)}, bf16[192,128]{1,0:T(8,128)(2,1)S(1)}, u32[]{:S(2)}, u32[]{:S(2)}) collective-permute-start(bf16[192,128]{1,0:T(8,128)(2,1)S(1)} %get-tuple-element.88), channel_id=1, source_target_pairs={{0,5},{1,4},{2,7},{3,6},{4,1},{5,0},{6,3},{7,2},{8,13},{9,12},{10,... | collective-permute-start | bytes 147464 | tf_op jit(solution)/shard_map/cond/branch_1_fun/ppermute | solution.py:57
  12.3 6.0 %collective-permute-start.3 = (bf16[192,128]{1,0:T(8,128)(2,1)S(1)}, bf16[192,128]{1,0:T(8,128)(2,1)S(1)}, u32[]{:S(2)}, u32[]{:S(2)}) collective-permute-start(bf16[192,128]{1,0:T(8,128)(2,1)S(1)} %get-tuple-element.89), channel_id=1, source_target_pairs={{0,3},{1,2},{2,1},{3,0},{4,7},{5,6},{6,5},{7,4},{8,11},{9,10},{10,... | collective-permute-start | bytes 147464 | tf_op jit(solution)/shard_map/cond/branch_1_fun/ppermute | solution.py:57
  13.5 4.7 %collective-permute-start.5 = (bf16[64,128]{1,0:T(8,128)(2,1)S(1)}, bf16[64,128]{1,0:T(8,128)(2,1)S(1)}, u32[]{:S(2)}, u32[]{:S(2)}) collective-permute-start(bf16[64,128]{1,0:T(8,128)(2,1)S(1)} %get-tuple-element.85), channel_id=1, source_target_pairs={{0,6},{1,7},{2,4},{3,5},{4,2},{5,3},{6,0},{7,1},{8,14},{9,15},{10,... | collective-permute-start | bytes 49160 | tf_op jit(solution)/shard_map/cond/branch_1_fun/ppermute | solution.py:57
  13.8 4.5 %collective-permute-start.4 = (bf16[128,128]{1,0:T(8,128)(2,1)S(1)}, bf16[128,128]{1,0:T(8,128)(2,1)S(1)}, u32[]{:S(2)}, u32[]{:S(2)}) collective-permute-start(bf16[128,128]{1,0:T(8,128)(2,1)S(1)} %add.20), channel_id=1, source_target_pairs={{0,7},{1,6},{2,5},{3,4},{4,3},{5,2},{6,1},{7,0},{8,15},{9,14},{10,... | collective-permute-start | bytes 98312 | tf_op jit(solution)/shard_map/cond/branch_1_fun/ppermute | solution.py:57
  18.3 4.6 %collective-permute-start.6 = (bf16[160,128]{1,0:T(8,128)(2,1)S(1)}, bf16[160,128]{1,0:T(8,128)(2,1)S(1)}, u32[]{:S(2)}, u32[]{:S(2)}) collective-permute-start(bf16[160,128]{1,0:T(8,128)(2,1)S(1)} %pad_maximum_fusion.2), channel_id=1, source_target_pairs={{0,9},{1,8},{2,11},{3,10},{4,13},{5,12},{6,15},{7,14},{8,1},{9,0},... | collective-permute-start | bytes 122888 | tf_op jit(solution)/shard_map/cond/branch_1_fun/ppermute | solution.py:57
  23.6 5.0 %collective-permute-start.8 = (bf16[384,128]{1,0:T(8,128)(2,1)S(1)}, bf16[384,128]{1,0:T(8,128)(2,1)S(1)}, u32[]{:S(2)}, u32[]{:S(2)}) collective-permute-start(bf16[384,128]{1,0:T(8,128)(2,1)S(1)} %bitcast.15), channel_id=1, source_target_pairs={{0,16},{1,17},{2,18},{3,19},{4,20},{5,21},{6,22},{7,23},{8,24},{9,... | collective-permute-start | bytes 294920 | tf_op jit(solution)/shard_map/ppermute | solution.py:57
